TPU v7x, 32 devices: a whole 2x2x4 slice. The times are simulated.
32 devices in a mesh: grp: 8 (over z, x), rep: 4 (over y, core).
Axes of the slice: x: 2, y: 2, z: 4, core: 2. Of those that a mesh axis runs over, the one named last changes fastest.
Arguments:
- strain: bfloat16 [1280, 384], P(None, 'grp'), may hold values from -27 to 27
- fir_taps: float32 [64], replicated, may hold values from -0.75 to 0.75
- half_widths: int32 [1280], P('grp'), may hold values from 32 to 160
- pairs: int32 [32, 8], replicated, may hold values from -1 to 31, as said below
Outputs:
- correlations: bfloat16 [32, 8, 40, 40, 256], P(('grp', 'rep'))
Inputs may be any that keep to these rules, and one draw needn't show every extreme that they name: `pairs`: row e lists tile numbers; -1 marks an unused entry and used entries come first; no two used entries of a row lie in the same group of 4 consecutive tiles, none equals e; every row has a used entry and some row uses all 8.
All inputs are finite; a program needn't handle non-finite values.
Results may differ from a plain program's by a relative error of at most 0.0052.
Values may be sent and summed in bfloat16 or wider, within the bound.
No kernel may reach another device: no remote copies, remote signals or barrier semaphores. Data moves between devices by JAX's collectives and lax.ppermute only.
A program may use at most 128 MiB of HBM per device.

v0:
```python
import math

import jax
import jax.numpy as jnp
from jax import lax
from jax.sharding import PartitionSpec as P

TILE = 40
LAGS = 256


def band_filter(samples, fir_taps):
    channels, length = samples.shape
    blocks = length // 128
    count = fir_taps.shape[0]
    rows_at = jnp.arange(128, dtype=jnp.int32)[:, None]
    cols_at = jnp.arange(128, dtype=jnp.int32)[None, :]
    tap_ids = jnp.arange(count, dtype=jnp.int32)
    near_gap = cols_at - rows_at
    far_gap = near_gap + 128
    taps_near = jnp.sum(
        jnp.where(near_gap[:, :, None] == tap_ids, fir_taps, jnp.float32(0.0)), axis=2
    )
    taps_far = jnp.sum(
        jnp.where(far_gap[:, :, None] == tap_ids, fir_taps, jnp.float32(0.0)), axis=2
    )
    blocked = samples.reshape(channels, blocks, 128)
    previous = jnp.concatenate(
        [jnp.zeros((channels, 1, 128), jnp.float32), blocked[:, :-1]], axis=1
    )
    result = jnp.einsum("cbs,st->cbt", blocked, taps_near, precision=lax.Precision.HIGHEST)
    result = result + jnp.einsum("cbs,st->cbt", previous, taps_far, precision=lax.Precision.HIGHEST)
    return result.reshape(channels, length)


def normalize(filtered, widths):
    channels, length = filtered.shape
    running = jnp.cumsum(jnp.abs(filtered), axis=1)
    prefix = jnp.concatenate([jnp.zeros((channels, 1), jnp.float32), running], axis=1)
    steps = jnp.arange(length, dtype=jnp.int32)[None, :]
    upper_end = jnp.minimum(steps + widths[:, None], length - 1) + 1
    lower_end = jnp.maximum(steps - widths[:, None], 0)
    window_sum = jnp.take_along_axis(prefix, upper_end, axis=1) - jnp.take_along_axis(
        prefix, lower_end, axis=1
    )
    level = window_sum / (2.0 * widths[:, None].astype(jnp.float32) + 1.0)
    return (filtered / (level + 1e-05)).astype(jnp.bfloat16)


def condition(samples, fir_taps, widths):
    return normalize(band_filter(samples.astype(jnp.float32), fir_taps), widths)


def lag_matrix(own, first, count, summed):
    tile_width, length = own.shape
    padded = jnp.concatenate(
        [
            jnp.zeros((tile_width, LAGS), own.dtype),
            own[:, :summed],
            jnp.zeros((tile_width, length - summed), own.dtype),
        ],
        axis=1,
    )
    shifted_rows = []
    for offset in range(count):
        begin = LAGS - (first + offset)
        shifted_rows.append(padded[:, begin : begin + length])
    return jnp.stack(shifted_rows, axis=1)


def correlate(own, chosen):
    listed, tile_width, length = chosen.shape
    summed = length - LAGS
    normalizer = 1.0 / math.sqrt(summed)
    lag_width = LAGS // 8
    flat = chosen.reshape(listed * tile_width, length)
    pieces = []
    for block_index in range(8):
        shifted = lag_matrix(own, block_index * lag_width, lag_width, summed)
        product = lax.dot_general(
            flat,
            shifted.reshape(tile_width * lag_width, length),
            (((1,), (1,)), ((), ())),
            preferred_element_type=jnp.float32,
        )
        pieces.append((product * normalizer).reshape(listed, tile_width, tile_width, lag_width))
    return jnp.concatenate(pieces, axis=3).astype(jnp.bfloat16)


def on_device(strain, fir_taps, half_widths, pairs):
    rep_count = lax.axis_size("rep")
    rep_index = lax.axis_index("rep")
    grp_index = lax.axis_index("grp")
    row_raw = lax.all_to_all(strain, "grp", split_axis=0, concat_axis=1, tiled=True)
    tile_width = TILE
    length = row_raw.shape[1]
    own_raw = lax.dynamic_slice_in_dim(row_raw, rep_index * tile_width, tile_width, 0)
    own_widths = lax.dynamic_slice_in_dim(half_widths, rep_index * tile_width, tile_width, 0)
    own = condition(own_raw, fir_taps, own_widths)
    row_tiles = lax.all_gather(own[None], "rep", axis=0, tiled=True)
    listed = pairs.shape[1]
    chosen_ids = lax.dynamic_index_in_dim(
        pairs, grp_index * rep_count + rep_index, 0, keepdims=False
    )
    empty = jnp.zeros((listed, tile_width, length), jnp.bfloat16)
    piece = lax.all_gather(row_tiles, "grp", axis=0, tiled=True)
    inside = (chosen_ids >= 0) & (chosen_ids < piece.shape[0])
    taken = jnp.take(piece, jnp.clip(chosen_ids, 0, piece.shape[0] - 1), axis=0)
    chosen = jnp.where(inside[:, None, None], taken, empty)
    return correlate(own, chosen)[None]


def solution(mesh):
    placed = (P(None, "grp"), P(), P("grp"), P())
    return jax.shard_map(
        on_device,
        mesh=mesh,
        in_specs=placed,
        out_specs=P(("grp", "rep"), None, None, None, None),
        check_vma=False,
    )
```

profile of v0, /device:TPU:0, one launch (start us, length us, event | category | flops | bytes accessed | tf_op | source)
XLA Modules:
  0.0 396.6 jit_solution(14959579781692741844)
XLA Ops:
  0.0 1.1 all_to_all.14
  1.9 7.3 %all-to-all-start = ((bf16[8,160,48]{1,2,0:T(8,128)(2,1)}), bf16[8,160,48]{1,2,0:T(8,128)(2,1)S(1)}, u32[]{:S(2)}, u32[]{:S(2)}) async-start(bf16[8,160,48]{1,2,0:T(8,128)(2,1)} %copy.58), calls=%async_computation | async-start | bytes 393216 | tf_op jit(solution)/shard_map/all_to_all | solution.py:94
  9.1 0.9 clamp_reduce_fusion
  10.0 0.9 and_reduce_fusion
  10.9 0.8 multiply_add_fusion
  11.8 3.5 select_reduce_fusion
  15.4 1.7 all-to-all-done
  17.7 0.9 reduce-window.6
  19.0 121.4 %gather_fusion.2 = f32[15360]{0:T(1024)S(1)} fusion(f32[40,385]{1,0:T(8,128)S(1)} %concatenate.50, s32[15360]{0:T(1024)S(1)} %reshape.668), kind=kCustom, calls=%fused_computation.1.clone | custom fusion | bytes 245760 | tf_op jit(solution)/shard_map/jit(take_along_axis)/gather | solution.py:43
  140.4 121.4 %gather_fusion.1 = f32[15360]{0:T(1024)S(1)} fusion(f32[40,385]{1,0:T(8,128)S(1)} %concatenate.50, s32[15360]{0:T(1024)S(1)} %reshape.663), kind=kCustom, calls=%fused_computation.clone | custom fusion | bytes 245760 | tf_op jit(solution)/shard_map/jit(take_along_axis)/gather | solution.py:43
  262.1 5.4 %all-gather = bf16[160,384]{1,0:T(8,128)(2,1)S(1)} all-gather(bf16[40,384]{1,0:T(8,128)(2,1)S(1)} %get-tuple-element.9), channel_id=2, replica_groups=mesh['grp'=8,'rep'=4] {'rep'}, dimensions={0}, use_global_device_ids=true | all-gather | bytes 153600 | tf_op jit(solution)/shard_map/all_gather | solution.py:100
  268.3 32.7 %all_gather.7 = bf16[32,40,384]{2,1,0:T(8,128)(2,1)S(1)} all-gather(bf16[4,40,384]{2,1,0:T(8,128)(2,1)S(1)} %bitcast.1107), channel_id=1, replica_groups=mesh['grp'=8,'rep'=4] {'grp'}, dimensions={0}, use_global_device_ids=true | all-gather | bytes 1105920 | tf_op jit(solution)/shard_map/all_gather | solution.py:106
  305.1 0.9 copy-done.5
  306.1 1.0 copy-done.7
  310.2 1.6 fusion
  311.8 4.8 %reshape.674 = bf16[1,8,40,40,32]{4,3,2,1,0:T(8,128)(2,1)} reshape(bf16[320,1280]{1,0:T(8,128)(2,1)} %fusion) | data formatting | bytes 1638400 | tf_op jit(solution)/shard_map/concatenate | solution.py:87
  316.6 3.4 reshape.675
  320.0 3.4 reshape.676
  323.4 3.4 reshape.677
  326.8 0.7 constant_dynamic-update-slice_fusion.254
  328.3 0.7 constant_dynamic-update-slice_fusion.252
  329.0 0.7 constant_dynamic-update-slice_fusion.251
  329.8 0.8 constant_dynamic-update-slice_fusion.250
  330.5 0.7 constant_dynamic-update-slice_fusion.249
  331.3 0.7 constant_dynamic-update-slice_fusion.248
  332.0 0.7 constant_dynamic-update-slice_fusion.247
  332.7 0.8 constant_dynamic-update-slice_fusion.246
  334.2 0.7 constant_dynamic-update-slice_fusion.244
  335.0 0.7 constant_dynamic-update-slice_fusion.243
  339.4 0.7 constant_dynamic-update-slice_fusion.237
  340.1 0.8 constant_dynamic-update-slice_fusion.236
  340.9 0.8 constant_dynamic-update-slice_fusion.235
  341.6 0.8 constant_dynamic-update-slice_fusion.234
  342.4 0.7 constant_dynamic-update-slice_fusion.233
  343.1 0.8 constant_dynamic-update-slice_fusion.232
  343.9 0.7 constant_dynamic-update-slice_fusion.231
  344.6 0.8 constant_dynamic-update-slice_fusion.230
  345.4 0.7 constant_dynamic-update-slice_fusion.229
  346.9 0.7 constant_dynamic-update-slice_fusion.227
  348.3 0.7 constant_dynamic-update-slice_fusion.225
  349.1 0.7 constant_dynamic-update-slice_fusion.224
  350.0 1.5 fusion.7
  351.6 1.5 fusion.6
  354.7 3.5 reshape.678
  358.1 3.4 reshape.679
  361.5 5.0 %reshape.680 = bf16[1,8,40,40,32]{4,3,2,1,0:T(8,128)(2,1)} reshape(bf16[320,1280]{1,0:T(8,128)(2,1)} %fusion.6) | data formatting | bytes 1638400 | tf_op jit(solution)/shard_map/concatenate | solution.py:87
  366.5 4.8 %reshape.681 = bf16[1,8,40,40,32]{4,3,2,1,0:T(8,128)(2,1)} reshape(bf16[320,1280]{1,0:T(8,128)(2,1)} %fusion.7) | data formatting | bytes 1638400 | tf_op jit(solution)/shard_map/concatenate | solution.py:87
  371.3 25.2 %concatenate.61 = bf16[1,8,40,40,256]{4,3,2,1,0:T(8,128)(2,1)} concatenate(bf16[1,8,40,40,32]{4,3,2,1,0:T(8,128)(2,1)S(1)} %copy-done, bf16[1,8,40,40,32]{4,3,2,1,0:T(8,128)(2,1)} %reshape.675, bf16[1,8,40,40,32]{4,3,2,1,0:T(8,128)(2,1)} %reshape.676, bf16[1,8,40,40,32]{4,3,2,1,0:T(8,128)(2,1)} %reshape.677, bf16[1,8,40,40,32]{4,3,2,1,0:T(8,128)(2,1)} %reshape.678, ...), dimensions={4} | concatenate | bytes 13107200 | tf_op jit(solution)/shard_map/concatenate | solution.py:87
  (96 shorter events, 18.3 us)
Async XLA Ops:
  1.9 15.2 %all-to-all-start = ((bf16[8,160,48]{1,2,0:T(8,128)(2,1)}), bf16[8,160,48]{1,2,0:T(8,128)(2,1)S(1)}, u32[]{:S(2)}, u32[]{:S(2)}) async-start(bf16[8,160,48]{1,2,0:T(8,128)(2,1)} %copy.58), calls=%async_computation | async-start | bytes 393216 | tf_op jit(solution)/shard_map/all_to_all | solution.py:94
  140.4 121.5 %copy-start.9 = (pred[384]{0:T(512)(128)(4,1)S(1)}, pred[384]{0:T(512)(128)(4,1)}, u32[]{:S(2)}) copy-start(pred[384]{0:T(512)(128)(4,1)} %constant.46.clone.1) | copy-start | bytes 1156
  305.1 0.9 copy-start.5
  306.1 1.0 copy-start.7
  308.0 1.4 copy-start.8
  308.0 2.1 copy-start.6
  320.0 6.8 %copy-start.1 = (bf16[40,32,384]{2,0,1:T(8,128)(2,1)S(1)}, bf16[40,32,384]{2,0,1:T(8,128)(2,1)}, u32[]{:S(2)}) copy-start(bf16[40,32,384]{2,0,1:T(8,128)(2,1)} %get-tuple-element.136) | copy-start | bytes 2949124
  349.8 1.7 copy-start.2
  349.8 3.3 copy-start.3
  351.5 2.4 copy-start.4
  361.5 9.8 %copy-start = (bf16[1,8,40,40,32]{4,3,2,1,0:T(8,128)(2,1)S(1)}, bf16[1,8,40,40,32]{4,3,2,1,0:T(8,128)(2,1)}, u32[]{:S(2)}) copy-start(bf16[1,8,40,40,32]{4,3,2,1,0:T(8,128)(2,1)} %reshape.674) | copy-start | bytes 2457604
where the time goes:
time: 398 us; the launch traced here: 397 us
  local copies, waits for them, and re-layouts  333 us (84%)
  blocking collectives  38.1 us (10%)
  matrix products  8.18 us (2%)
  other arithmetic  7.46 us (2%)
  starting transfers between devices  7.25 us (2%)
    gather x3, local copies, waits for them, and re-layouts, normalize(): jnp.take_along_axis(prefix, lower_end, axis=1)  121 us
    gather x3, local copies, waits for them, and re-layouts, normalize(): jnp.take_along_axis(prefix, upper_end, axis=1)  121 us
    concatenate x9, local copies, waits for them, and re-layouts, correlate(): return jnp.concatenate(pieces, axis=3).astype(jnp.bfloat16)  56.9 us
    all_gather x1, blocking collectives, on_device(): piece = lax.all_gather(row_tiles, 'grp', axis=0, tiled=True)  32.7 us
    unnamed x83, local copies, waits for them, and re-layouts  29.1 us
  transfers between devices with their start and end apart: 1, of which 1 were waited for; matrix products, arithmetic and copies ran while one was open for 2% of the time, Pallas kernels for 0%

commit v1 on v0

v1 whole, which is shorter than its diff:
```python
import functools
import math

import jax
import jax.numpy as jnp
from jax import lax
from jax.experimental import pallas as pl
from jax.experimental.pallas import tpu as pltpu
from jax.sharding import PartitionSpec as P

TILE = 40
LAGS = 256
LANES = 128
PER_BLOCK = LANES // TILE
CHUNK = 2


def pack_kernel(rep_count, pairs_ref, strain_ref, widths_ref, out_ref, blocks_ref, table_ref):
    groups, rows, packed = out_ref.shape
    listed = pairs_ref.shape[0]
    channels = strain_ref.shape[1]
    members = widths_ref.shape[1]
    my_rep = lax.axis_index("rep")
    my_grp = lax.axis_index("grp")

    count = channels // LANES
    for block in range(count):
        blocks_ref[block] = strain_ref[:, block * LANES : (block + 1) * LANES].astype(jnp.float32)
    blocks_ref[count] = jnp.zeros((rows, LANES), jnp.float32)

    wide = jnp.concatenate(
        [widths_ref[...].astype(jnp.float32), jnp.zeros((1, 2 * LANES - members), jnp.float32)],
        axis=1,
    )
    wide = jnp.broadcast_to(wide, (8, 2 * LANES))
    sub = lax.broadcasted_iota(jnp.int32, (8, LANES), 0)
    spare = LANES - 8
    for member in range(rep_count):
        for block in range(packed // LANES):
            runs = []
            for line in range(2):
                run = (line * (packed // LANES) + block) * 8
                shift = (spare - member * TILE - run) % (2 * LANES)
                runs.append(pltpu.roll(wide, shift, 1)[:, :LANES])
            even = lax.rem(sub, 2) == 0
            table_ref[member, :, block * LANES : (block + 1) * LANES] = jnp.where(even, runs[0], runs[1])

    lane = lax.broadcasted_iota(jnp.int32, (rows, LANES), 1)
    row = lax.broadcasted_iota(jnp.int32, (rows, LANES), 0)

    def fill(group, carry):
        tile = group * rep_count + my_rep
        chosen = [tile]
        member = jnp.int32(0)
        for slot in range(listed):
            other = pairs_ref[slot, tile]
            chosen.append(jnp.maximum(other, 0))
            inside = (other >= 0) & (lax.div(other, rep_count) == my_grp)
            member = jnp.where(inside, lax.rem(other, rep_count), member)
        for block in range(packed // LANES):
            total = jnp.zeros((rows, LANES), jnp.float32)
            for place in range(PER_BLOCK):
                index = block * PER_BLOCK + place
                if index > listed:
                    continue
                start = chosen[index] * TILE
                source = lax.div(start, LANES)
                offset = lax.rem(start, LANES)
                both = jnp.where(lane >= offset, blocks_ref[source], blocks_ref[source + 1])
                shift = lax.rem(place * TILE + LANES - offset, LANES)
                moved = pltpu.roll(both, shift, 1)
                here = (lane >= place * TILE) & (lane < (place + 1) * TILE)
                total = jnp.where(here, moved, total)
            at = pl.ds(block * LANES, LANES)
            theirs = table_ref[member, :, at]
            mine = table_ref[my_rep, :, at]
            short = min(rows, 8)
            top_row = row[:short]
            extra = jnp.where(top_row < 2, theirs[:short], mine[:short])
            marked = (lane[:short] >= spare) & (top_row < 4)
            top = jnp.where(marked, extra, total[:short])
            if rows > 8:
                total = jnp.concatenate([top, total[8:]], axis=0)
            else:
                total = top
            out_ref[group, :, at] = total.astype(jnp.bfloat16)
        return carry

    lax.fori_loop(0, groups, fill, 0)


def pack(strain, half_widths, pairs, groups, rep_count):
    channels, rows = strain.shape
    listed = pairs.shape[1]
    packed = -(-(listed + 1) // PER_BLOCK) * LANES
    vmem = pl.BlockSpec(memory_space=pltpu.VMEM)
    return pl.pallas_call(
        functools.partial(pack_kernel, rep_count),
        out_shape=jax.ShapeDtypeStruct((groups, rows, packed), jnp.bfloat16),
        in_specs=[pl.BlockSpec(memory_space=pltpu.SMEM), vmem, vmem],
        out_specs=vmem,
        scratch_shapes=[
            pltpu.VMEM((channels // LANES + 1, rows, LANES), jnp.float32),
            pltpu.VMEM((rep_count, 8, packed), jnp.float32),
        ],
        compiler_params=pltpu.CompilerParams(vmem_limit_bytes=48 * 2**20),
        name="pack",
    )(pairs.T, strain.T, half_widths[None, :])


def split(values):
    high = values.astype(jnp.bfloat16)
    low = (values - high.astype(jnp.float32)).astype(jnp.bfloat16)
    return high, low


def dot(left, right):
    return jnp.dot(left, right, preferred_element_type=jnp.float32)


def condition(rep_count, pairs_ref, raw_ref, taps_ref, tops_ref, white_ref):
    length, packed = raw_ref.shape
    listed = pairs_ref.shape[0]
    groups = lax.axis_size("grp")
    rows = length // groups
    my_rep = lax.axis_index("rep")
    my_grp = lax.axis_index("grp")
    tile = my_grp * rep_count + my_rep

    raw = raw_ref[...]
    raw32 = raw.astype(jnp.float32)
    short = min(rows, 8)
    for group in range(groups):
        tops_ref[group, :short] = raw32[group * rows : group * rows + short]
    samples = jnp.transpose(raw32).astype(jnp.bfloat16)

    count = taps_ref.shape[1]
    taps = jnp.concatenate([taps_ref[...], jnp.zeros((1, 2 * LANES - count), jnp.float32)], axis=1)
    band = pltpu.roll(jnp.broadcast_to(taps, (LANES, 2 * LANES)), 0, 1, stride=1, stride_axis=0)
    parts = []
    empty = jnp.zeros((LANES, LANES), jnp.bfloat16)
    for piece in split(band):
        near, far = piece[:, :LANES], piece[:, LANES:]
        first = jnp.concatenate([piece, jnp.concatenate([empty, near], axis=1)], axis=0)
        second = jnp.concatenate([far, near], axis=0)
        parts.append((dot(samples[:, : 2 * LANES], first), dot(samples[:, LANES:], second)))
    filtered = jnp.concatenate([parts[0][0] + parts[1][0], parts[0][1] + parts[1][1]], axis=1)

    size = jnp.abs(filtered)
    before = lax.broadcasted_iota(jnp.int32, (2 * LANES, 2 * LANES), 0) <= lax.broadcasted_iota(
        jnp.int32, (2 * LANES, 2 * LANES), 1
    )
    upper = jnp.where(before, 1.0, 0.0).astype(jnp.bfloat16)
    ones = jnp.ones((2 * LANES, LANES), jnp.bfloat16)
    sums = []
    for piece in split(size):
        head, tail = piece[:, : 2 * LANES], piece[:, 2 * LANES :]
        sums.append((dot(head, upper), dot(head, ones), dot(tail, upper[:LANES, :LANES])))
    high, low = sums
    head = high[0] + low[0]
    tail = (high[1] + low[1]) + (high[2] + low[2])
    prefix = [head[:, :LANES], head[:, LANES:], tail]

    lane8 = lax.broadcasted_iota(jnp.int32, (8, LANES), 1)
    sub8 = lax.broadcasted_iota(jnp.int32, (8, LANES), 0)
    lane = lax.broadcasted_iota(jnp.int32, (TILE, LANES), 1)
    blocks = packed // LANES
    for slot in range(listed + 1):
        base = slot // PER_BLOCK * LANES + slot % PER_BLOCK * TILE
        at = slice(base, base + TILE)
        if slot == 0:
            source, line = my_grp, 2
            used = None
        else:
            other = pairs_ref[slot - 1, tile]
            source, line = lax.div(jnp.maximum(other, 0), rep_count), 0
            used = other >= 0
        widths = []
        for run in range(TILE // 8):
            lanes = pl.ds(run % blocks * LANES, LANES)
            at_line = pl.ds(line + run // blocks, 1)
            shown = jnp.broadcast_to(tops_ref[source, at_line, lanes], (8, LANES))
            picked = jnp.where(lane8 == sub8 + (LANES - 8), shown, 0.0)
            widths.append(jnp.sum(picked, axis=1, keepdims=True))
        width = jnp.broadcast_to(jnp.concatenate(widths, axis=0), (TILE, LANES))
        whole = width.astype(jnp.int32)
        above = lane + whole
        below = lane - whole - 1
        above_at = above & (LANES - 1)
        below_at = below & (LANES - 1)
        above_by = above >> 7
        below_by = below >> 7
        up = [jnp.take_along_axis(prefix[b][at], above_at, axis=1) for b in range(3)]
        down = [jnp.take_along_axis(prefix[b][at], below_at, axis=1) for b in range(2)]
        full = jnp.broadcast_to(prefix[2][at][:, LANES - 1 :], (TILE, LANES))
        ends = up + [full, full]
        starts = [jnp.zeros((TILE, LANES), jnp.float32)] * 2 + down
        down_last = jnp.take_along_axis(prefix[2][at], below_at, axis=1)
        starts.append(down_last)
        scale = 2.0 * width + 1.0
        for block in range(3):
            top = jnp.where(above_by == 0, ends[block], jnp.where(above_by == 1, ends[block + 1], ends[block + 2]))
            low_end = jnp.where(
                below_by == 0,
                starts[block + 2],
                jnp.where(below_by == -1, starts[block + 1], starts[block]),
            )
            level = (top - low_end) / scale
            value = filtered[at, block * LANES : (block + 1) * LANES] / (level + 1e-05)
            if used is not None:
                value = jnp.where(used, value, 0.0)
            white_ref[slot * TILE : (slot + 1) * TILE, block * LANES : (block + 1) * LANES] = value


def lag_weights(white_ref, weights_ref):
    own = white_ref[:TILE, :LANES].astype(jnp.bfloat16)
    row = lax.broadcasted_iota(jnp.int32, (LANES, LANES), 0)
    col = lax.broadcasted_iota(jnp.int32, (LANES, LANES), 1)
    flip = jnp.where(row + col == LANES - 1, 1.0, 0.0).astype(jnp.bfloat16)
    reverse = dot(own, flip)
    keep = col <= row
    for channel in range(TILE):
        line = jnp.broadcast_to(reverse[channel : channel + 1], (LANES, LANES))
        turned = pltpu.roll(line, 1, 1, stride=1, stride_axis=0)
        first = jnp.where(keep, turned, 0.0).astype(jnp.bfloat16)
        second = jnp.where(keep, 0.0, turned).astype(jnp.bfloat16)
        at = slice(channel % 2 * LANES, (channel % 2 + 1) * LANES)
        weights_ref[channel // 2, :LANES, at] = first
        weights_ref[channel // 2, LANES:, at] = second


def correlate_kernel(
    rep_count, pairs_ref, raw_ref, taps_ref, out_ref, tops_ref, white_ref, weights_ref, low_ref, high_ref
):
    step = pl.program_id(0)

    @pl.when(step == 0)
    def _():
        condition(rep_count, pairs_ref, raw_ref, taps_ref, tops_ref, white_ref)
        lag_weights(white_ref, weights_ref)

    rows = CHUNK * TILE
    start = pl.multiple_of(TILE + step * rows, 8)
    partner = white_ref[pl.ds(start, rows), :].astype(jnp.bfloat16)
    early = partner[:, : 2 * LANES]
    late = partner[:, LANES:]
    normalizer = 1.0 / math.sqrt(LANES)

    def pair_of_channels(index, carry):
        weights = weights_ref[index]
        for part, ref in ((early, low_ref), (late, high_ref)):
            product = dot(part, weights) * normalizer
            for side in range(2):
                ref[pl.ds(2 * index + side, rows, stride=TILE), :] = product[
                    :, side * LANES : (side + 1) * LANES
                ]
        return carry

    lax.fori_loop(0, TILE // 2, pair_of_channels, 0, unroll=4)

    def finish(index, carry):
        at = pl.ds(pl.multiple_of(index * TILE * TILE, TILE * TILE), TILE * TILE)
        for side, ref in enumerate((low_ref, high_ref)):
            block = ref[at, :].astype(jnp.bfloat16).reshape(TILE, TILE, LANES)
            out_ref[0, index, :, :, side * LANES : (side + 1) * LANES] = block
        return carry

    lax.fori_loop(0, CHUNK, finish, 0)


def correlate(raw, fir_taps, pairs, rep_count):
    length, packed = raw.shape
    listed = pairs.shape[1]
    rows = CHUNK * TILE
    vmem = pl.BlockSpec(memory_space=pltpu.VMEM)
    return pl.pallas_call(
        functools.partial(correlate_kernel, rep_count),
        grid=(listed // CHUNK,),
        out_shape=jax.ShapeDtypeStruct((1, listed, TILE, TILE, LAGS), jnp.bfloat16),
        in_specs=[pl.BlockSpec(memory_space=pltpu.SMEM), vmem, vmem],
        out_specs=pl.BlockSpec((1, CHUNK, TILE, TILE, LAGS), lambda step: (0, step, 0, 0, 0)),
        scratch_shapes=[
            pltpu.VMEM((lax.axis_size("grp"), 8, packed), jnp.float32),
            pltpu.VMEM(((listed + 1) * TILE, length), jnp.float32),
            pltpu.VMEM((TILE // 2, 2 * LANES, 2 * LANES), jnp.bfloat16),
            pltpu.VMEM((rows * TILE, LANES), jnp.float32),
            pltpu.VMEM((rows * TILE, LANES), jnp.float32),
        ],
        compiler_params=pltpu.CompilerParams(vmem_limit_bytes=48 * 2**20),
        name="correlate",
    )(pairs.T, raw, fir_taps[None, :])


def on_device(strain, fir_taps, half_widths, pairs):
    groups = lax.axis_size("grp")
    rep_count = lax.axis_size("rep")
    message = pack(strain, half_widths, pairs, groups, rep_count)
    received = lax.all_to_all(message, "grp", split_axis=0, concat_axis=0, tiled=True)
    raw = received.reshape(-1, received.shape[2])
    return correlate(raw, fir_taps, pairs, rep_count)


def solution(mesh):
    placed = (P(None, "grp"), P(), P("grp"), P())
    return jax.shard_map(
        on_device,
        mesh=mesh,
        in_specs=placed,
        out_specs=P(("grp", "rep"), None, None, None, None),
        check_vma=False,
    )
```

time: 398 us -> 33.8 us (0.08)
  local copies, waits for them, and re-layouts: 333 us -> 2.92 us
  blocking collectives: 38.1 us -> 17.4 us
  Pallas kernels: 0 us -> 13.3 us
  matrix products: 8.18 us -> 0 us
  other arithmetic: 7.46 us -> 0 us
  starting transfers between devices: 7.25 us -> 0 us
    gather x7 -> x0, local copies, waits for them, and re-layouts: 243 us -> none  [the longest x3 121 us: normalize(): jnp.take_along_axis(prefix, lower_end, axis=1)]
    concatenate x10 -> x0, local copies, waits for them, and re-layouts: 57 us -> none  [the longest x9 56.9 us: correlate(): return jnp.concatenate(pieces, axis=3).astype(jnp.bfloat16)]
    all_gather x2 -> x0, blocking collectives: 38.1 us -> none  [the longest x1 32.7 us: on_device(): piece = lax.all_gather(row_tiles, 'grp', axis=0, tiled=True)]
    unnamed x83 -> x8, local copies, waits for them, and re-layouts: 29.1 us -> 2.92 us
    all_to_all x0 -> x1, blocking collectives: none -> 17.4 us  [on_device(): lax.all_to_all(message, 'grp', split_axis=0, concat_axis=0, tiled=True)]
    pallas_call x0 -> x2, Pallas kernels: none -> 13.3 us  [the longest x1 11.5 us: correlate(): pl.pallas_call(functools.partial(correlate_kernel, rep_count), grid=(list...]
    dot_general x10 -> x0, matrix products: 8.18 us -> none  [the longest x8 7.65 us: correlate(): lax.dot_general(flat, shifted.reshape(tile_width * lag_width, length), ((...]
    all_to_all x1 -> x0, starting transfers between devices: 7.25 us -> none  [on_device(): lax.all_to_all(strain, 'grp', split_axis=0, concat_axis=1, tiled=True)]
  transfers between devices with their start and end apart: 1 -> 0, of which waited for: 1 -> 0; matrix products, arithmetic and copies ran while one was open for 2% -> 0% of each run, Pallas kernels for 0% -> 0%
where the time goes in v1:
time: 33.8 us; the launch traced here: 33.6 us
  blocking collectives  17.4 us (51%)
  Pallas kernels  13.3 us (39%)
  local copies, waits for them, and re-layouts  2.92 us (9%)
    all_to_all x1, blocking collectives, on_device(): lax.all_to_all(message, 'grp', split_axis=0, concat_axis=0, tiled=True)  17.4 us
    pallas_call x1, Pallas kernels, correlate(): pl.pallas_call(functools.partial(correlate_kernel, rep_count), grid=(list...  11.5 us
    unnamed x8, local copies, waits for them, and re-layouts  2.92 us
    pallas_call x1, Pallas kernels, pack(): pl.pallas_call(functools.partial(pack_kernel, rep_count), out_shape=jax.S...  1.75 us

profile of v1, /device:TPU:0, one launch (start us, length us, event | category | flops | bytes accessed | tf_op | source)
XLA Modules:
  0.0 33.6 jit_solution(13889737399180551504)
XLA Ops:
  0.0 0.0 copy-start
  0.0 0.9 %copy-done = bf16[1280,48]{0,1:T(8,128)(2,1)S(1)} copy-done((bf16[1280,48]{0,1:T(8,128)(2,1)S(1)}, bf16[1280,48]{0,1:T(8,128)(2,1)}, u32[]{:S(2)}) %copy-start) | copy-done | bytes 122904
  0.9 0.0 copy-start.1
  0.9 0.7 %copy-done.1 = s32[32,8]{0,1:T(8,128)S(1)} copy-done((s32[32,8]{0,1:T(8,128)S(1)}, s32[32,8]{0,1:T(8,128)}, u32[]{:S(2)}) %copy-start.1) | copy-done | bytes 1048
  1.6 0.0 copy-start.2
  1.6 0.7 %copy-done.2 = s32[160]{0:T(256)S(1)} copy-done((s32[160]{0:T(256)S(1)}, s32[160]{0:T(256)}, u32[]{:S(2)}) %copy-start.2) | copy-done | bytes 664
  2.3 1.8 %pack.1 = bf16[8,48,384]{2,1,0:T(8,128)(2,1)S(1)} custom-call(s32[8,32]{1,0:T(8,128)S(1)} %bitcast.7, bf16[48,1280]{1,0:T(8,128)(2,1)S(1)} %bitcast.6, s32[1,160]{1,0:T(1,128)S(1)} %bitcast.9), custom_call_target="tpu_custom_call" | custom-call | tf_op jit(solution)/shard_map/pack/pallas_call | solution.py:97
  4.0 17.4 %all_to_all.5 = bf16[8,48,384]{2,1,0:T(8,128)(2,1)S(1)} all-to-all(bf16[8,48,384]{2,1,0:T(8,128)(2,1)S(1)} %pack.1), channel_id=1, replica_groups=mesh['grp'=8,'rep'=4] {'grp'}, dimensions={0} | all-to-all | bytes 589824 | tf_op jit(solution)/shard_map/all_to_all | solution.py:298
  21.4 0.0 copy-start.3
  21.4 0.7 %copy-done.3 = f32[64]{0:T(128)S(1)} copy-done((f32[64]{0:T(128)S(1)}, f32[64]{0:T(128)}, u32[]{:S(2)}) %copy-start.3) | copy-done | bytes 280
  22.1 11.5 %correlate.1 = bf16[1,8,40,40,256]{4,3,2,1,0:T(8,128)(2,1)} custom-call(s32[8,32]{1,0:T(8,128)S(1)} %bitcast.8, bf16[384,384]{1,0:T(8,128)(2,1)S(1)} %bitcast.5, f32[1,64]{1,0:T(1,128)S(1)} %bitcast.10), custom_call_target="tpu_custom_call" | custom-call | tf_op jit(solution)/shard_map/correlate/pallas_call | solution.py:276
Async XLA Ops:
  0.0 0.9 %copy-start = (bf16[1280,48]{0,1:T(8,128)(2,1)S(1)}, bf16[1280,48]{0,1:T(8,128)(2,1)}, u32[]{:S(2)}) copy-start(bf16[1280,48]{0,1:T(8,128)(2,1)} %param.4) | copy-start | bytes 368644
  0.9 0.7 %copy-start.1 = (s32[32,8]{0,1:T(8,128)S(1)}, s32[32,8]{0,1:T(8,128)}, u32[]{:S(2)}) copy-start(s32[32,8]{0,1:T(8,128)} %param.7) | copy-start | bytes 3076
  1.6 0.7 %copy-start.2 = (s32[160]{0:T(256)S(1)}, s32[160]{0:T(256)}, u32[]{:S(2)}) copy-start(s32[160]{0:T(256)} %param.6) | copy-start | bytes 1924
  21.4 0.7 %copy-start.3 = (f32[64]{0:T(128)S(1)}, f32[64]{0:T(128)}, u32[]{:S(2)}) copy-start(f32[64]{0:T(128)} %param.5) | copy-start | bytes 772

commit v2 on v1

v2 whole, which is shorter than its diff:
```python
import functools
import math

import jax
import jax.numpy as jnp
from jax import lax
from jax.experimental import pallas as pl
from jax.experimental.pallas import tpu as pltpu
from jax.sharding import PartitionSpec as P

TILE = 40
LAGS = 256
LANES = 128
STRIDE = 9
PER_BLOCK = LANES // TILE


def fetch(pairs, semaphores):
    copies = [
        pltpu.make_async_copy(source, target, semaphores.at[index])
        for index, (source, target) in enumerate(pairs)
    ]
    for copy in copies:
        copy.start()
    for copy in copies:
        copy.wait()


def partner_of(group, step, groups):
    if groups & (groups - 1) == 0:
        return group ^ step
    return (step + groups - group) % groups


def rounds(groups):
    even = list(range(groups - 1, 0, -1))
    far = groups // 2
    odd = [step for step in even if step < far] + [step for step in even if step >= far]
    return list(zip(even, odd)) + [(0, 0)]


def step_of(steps, member):
    even, odd = steps
    return even if even == odd else jnp.where(lax.rem(member, 2) == 0, even, odd)


def pack_kernel(rep_count, pairs_hbm, strain_hbm, widths_hbm, taps_hbm, *refs):
    outs_hbm = refs[:-9]
    taps_ref, stage_ref, sent = refs[-9:-6]
    out_refs = [stage_ref.at[index] for index in range(len(outs_hbm))]
    pairs_ref, strain_ref, widths_ref, semaphores, blocks_ref, table_ref = refs[-6:]
    groups = len(out_refs)
    rows, packed = out_refs[0].shape
    listed = pairs_ref.shape[0]
    channels = strain_ref.shape[1]
    members = widths_ref.shape[1]
    fetch(
        [
            (strain_hbm, strain_ref),
            (pairs_hbm, pairs_ref),
            (widths_hbm, widths_ref),
            (taps_hbm, taps_ref),
        ],
        semaphores,
    )
    my_rep = lax.axis_index("rep")
    my_grp = lax.axis_index("grp")

    count = channels // LANES
    filled = strain_ref.shape[0]
    for block in range(count):
        values = strain_ref[:, block * LANES : (block + 1) * LANES].astype(jnp.float32)
        if rows > filled:
            values = jnp.concatenate([values, jnp.zeros((rows - filled, LANES), jnp.float32)], axis=0)
        blocks_ref[block] = values
    blocks_ref[count] = jnp.zeros((rows, LANES), jnp.float32)

    wide = jnp.concatenate(
        [widths_ref[...].astype(jnp.float32), jnp.zeros((1, 2 * LANES - members), jnp.float32)],
        axis=1,
    )
    wide = jnp.broadcast_to(wide, (TILE, 2 * LANES))
    tall = lax.broadcasted_iota(jnp.int32, (TILE, 2 * LANES), 0)
    across = lax.broadcasted_iota(jnp.int32, (TILE, 2 * LANES), 1)
    for member in range(rep_count):
        column = jnp.sum(jnp.where(across == tall + member * TILE, wide, 0.0), axis=1, keepdims=True)
        table_ref[member, :TILE] = jnp.broadcast_to(column, (TILE, LANES))
        table_ref[member, TILE:] = jnp.zeros((rows - TILE, LANES), jnp.float32)

    lane = lax.broadcasted_iota(jnp.int32, (rows, LANES), 1)
    spare = LANES - 8
    for steps, out_ref in zip(rounds(groups), out_refs):
        group = partner_of(my_grp, step_of(steps, my_rep), groups)
        tile = group * rep_count + my_rep
        chosen = [tile]
        member, place_of = jnp.int32(0), jnp.int32(-1)
        for slot in range(listed):
            other = pairs_ref[slot, tile]
            chosen.append(jnp.maximum(other, 0))
            inside = (other >= 0) & (lax.div(other, rep_count) == my_grp)
            member = jnp.where(inside, lax.rem(other, rep_count), member)
            place_of = jnp.where(inside, slot + 1, place_of)
        own_at = jnp.where(group == my_grp, spare, -1)
        theirs = table_ref[member]
        mine = table_ref[my_rep]
        for block in range(packed // LANES):
            total = jnp.zeros((rows, LANES), jnp.float32)
            for place in range(PER_BLOCK):
                index = block * PER_BLOCK + place
                if index > listed:
                    continue
                start = chosen[index] * TILE
                source = lax.div(start, LANES)
                offset = lax.rem(start, LANES)
                both = jnp.where(lane >= offset, blocks_ref[source], blocks_ref[source + 1])
                shift = lax.rem(place * TILE + LANES - offset, LANES)
                moved = pltpu.roll(both, shift, 1)
                here = (lane >= place * TILE) & (lane < (place + 1) * TILE)
                total = jnp.where(here, moved, total)
            first = block * PER_BLOCK
            here = (place_of >= first) & (place_of < first + PER_BLOCK)
            marked = jnp.where(here, spare + place_of - first, -1)
            total = jnp.where(lane == marked, theirs, total)
            if block == 0:
                total = jnp.where(lane == own_at, mine, total)
            out_ref[:, block * LANES : (block + 1) * LANES] = total.astype(jnp.bfloat16)
    copies = [
        pltpu.make_async_copy(stage_ref.at[index], out_hbm, sent.at[index])
        for index, out_hbm in enumerate(outs_hbm)
    ]
    for copy in copies:
        copy.start()
    for copy in copies:
        copy.wait()


def pack(strain, fir_taps, half_widths, pairs, groups, rep_count):
    channels, filled = strain.shape
    rows = max(filled, -(-TILE // 16) * 16)
    tiles, listed = pairs.shape
    members = half_widths.shape[0]
    packed = -(-(listed + 1) // PER_BLOCK) * LANES
    hbm = pl.BlockSpec(memory_space=pltpu.HBM)
    vmem = pl.BlockSpec(memory_space=pltpu.VMEM)
    return pl.pallas_call(
        functools.partial(pack_kernel, rep_count),
        out_shape=[pltpu.HBM((rows, packed), jnp.bfloat16)] * groups
        + [jax.ShapeDtypeStruct((1, fir_taps.shape[0]), jnp.float32)],
        in_specs=[hbm] * 4,
        out_specs=[hbm] * groups + [vmem],
        scratch_shapes=[
            pltpu.VMEM((groups, rows, packed), jnp.bfloat16),
            pltpu.SemaphoreType.DMA((groups,)),
            pltpu.SMEM((listed, tiles), jnp.int32),
            pltpu.VMEM((filled, channels), jnp.bfloat16),
            pltpu.VMEM((1, members), jnp.int32),
            pltpu.SemaphoreType.DMA((4,)),
            pltpu.VMEM((channels // LANES + 1, rows, LANES), jnp.float32),
            pltpu.VMEM((rep_count, rows, LANES), jnp.float32),
        ],
        compiler_params=pltpu.CompilerParams(vmem_limit_bytes=48 * 2**20),
        name="pack",
    )(*[
        pltpu.with_memory_space_constraint(array, pltpu.HBM)
        for array in (pairs.T, strain.T, half_widths[None, :], fir_taps[None, :])
    ])


def split(values):
    high = values.astype(jnp.bfloat16)
    low = (values - high.astype(jnp.float32)).astype(jnp.bfloat16)
    return high, low


def dot(left, right):
    return jnp.dot(left, right, preferred_element_type=jnp.float32)


def condition(period, raw_ref, taps_ref, white_ref):
    groups, rows, packed = raw_ref.shape
    listed = white_ref.shape[0] // TILE - 1
    blocks = packed // LANES
    raw = raw_ref[:, :period, :].astype(jnp.float32).reshape(groups * period, packed)
    samples = jnp.transpose(raw).astype(jnp.bfloat16)
    columns = []
    for block in range(blocks):
        piece = raw_ref[:, :TILE, block * LANES : (block + 1) * LANES].astype(jnp.float32)
        columns.append(jnp.sum(piece, axis=0))

    count = taps_ref.shape[1]
    taps = jnp.concatenate([taps_ref[...], jnp.zeros((1, 2 * LANES - count), jnp.float32)], axis=1)
    bands = pltpu.roll(jnp.broadcast_to(taps, (LANES, 2 * LANES)), 0, 1, stride=1, stride_axis=0)
    parts = []
    empty = jnp.zeros((LANES, LANES), jnp.bfloat16)
    for piece in split(bands):
        near, far = piece[:, :LANES], piece[:, LANES:]
        first = jnp.concatenate([piece, jnp.concatenate([empty, near], axis=1)], axis=0)
        second = jnp.concatenate([far, near], axis=0)
        parts.append((dot(samples[:, : 2 * LANES], first), dot(samples[:, LANES:], second)))
    filtered = jnp.concatenate([parts[0][0] + parts[1][0], parts[0][1] + parts[1][1]], axis=1)

    size = jnp.abs(filtered)
    before = lax.broadcasted_iota(jnp.int32, (2 * LANES, 2 * LANES), 0) <= lax.broadcasted_iota(
        jnp.int32, (2 * LANES, 2 * LANES), 1
    )
    upper = jnp.where(before, 1.0, 0.0).astype(jnp.bfloat16)
    ones = jnp.ones((2 * LANES, LANES), jnp.bfloat16)
    sums = []
    for piece in split(size):
        head, tail = piece[:, : 2 * LANES], piece[:, 2 * LANES :]
        sums.append((dot(head, upper), dot(head, ones), dot(tail, upper[:LANES, :LANES])))
    high, low = sums
    head = high[0] + low[0]
    tail = (high[1] + low[1]) + (high[2] + low[2])
    prefix = [head[:, :LANES], head[:, LANES:], tail]

    lane = lax.broadcasted_iota(jnp.int32, (TILE, LANES), 1)
    for slot in range(listed + 1):
        base = slot // PER_BLOCK * LANES + slot % PER_BLOCK * TILE
        at = slice(base, base + TILE)
        from_lane = LANES - 8 + slot % PER_BLOCK
        column = columns[slot // PER_BLOCK][:, from_lane : from_lane + 1]
        width = jnp.broadcast_to(column, (TILE, LANES))
        whole = width.astype(jnp.int32)
        above = lane + whole
        below = lane - whole - 1
        above_at = above & (LANES - 1)
        below_at = below & (LANES - 1)
        above_by = above >> 7
        below_by = below >> 7
        up = [jnp.take_along_axis(prefix[b][at], above_at, axis=1) for b in range(3)]
        down = [jnp.take_along_axis(prefix[b][at], below_at, axis=1) for b in range(2)]
        full = jnp.broadcast_to(prefix[2][at][:, LANES - 1 :], (TILE, LANES))
        ends = up + [full, full]
        starts = [jnp.zeros((TILE, LANES), jnp.float32)] * 2 + down
        down_last = jnp.take_along_axis(prefix[2][at], below_at, axis=1)
        starts.append(down_last)
        scale = 1.0 / (2.0 * width + 1.0)
        high_0, high_1 = above_by == 0, above_by == 1
        low_0, low_1 = below_by == 0, below_by == -1
        for block in range(3 if slot else 1):
            top = jnp.where(high_0, ends[block], jnp.where(high_1, ends[block + 1], ends[block + 2]))
            low_end = jnp.where(
                low_0, starts[block + 2], jnp.where(low_1, starts[block + 1], starts[block])
            )
            level = (top - low_end) * scale
            value = filtered[at, block * LANES : (block + 1) * LANES] / (level + 1e-05)
            if slot:
                value = jnp.where(width > 0.0, value, 0.0)
            white_ref[slot * TILE : (slot + 1) * TILE, block * LANES : (block + 1) * LANES] = value


def condition_kernel(period, taps_ref, *refs):
    received = refs[:-4]
    partner_ref, reverse_ref, raw_ref, white_ref = refs[-4:]
    groups = len(received)
    my_grp = lax.axis_index("grp")
    my_rep = lax.axis_index("rep")
    for steps, ref in zip(rounds(groups), received):
        raw_ref[partner_of(my_grp, step_of(steps, my_rep), groups)] = ref[...]
    condition(period, raw_ref, taps_ref, white_ref)

    partner = white_ref[TILE:, :].astype(jnp.bfloat16)
    rows = partner.shape[0]
    partner_ref[:rows] = partner[:, : 2 * LANES]
    partner_ref[rows:] = partner[:, LANES:]
    own = white_ref[:TILE, :LANES].astype(jnp.bfloat16)
    row = lax.broadcasted_iota(jnp.int32, (LANES, LANES), 0)
    col = lax.broadcasted_iota(jnp.int32, (LANES, LANES), 1)
    flip = jnp.where(row + col == LANES - 1, 1.0, 0.0).astype(jnp.bfloat16)
    reverse_ref[...] = dot(own, flip)


def conditioned(received, taps, period, listed):
    groups = len(received)
    rows, packed = received[0].shape
    vmem = pl.BlockSpec(memory_space=pltpu.VMEM)
    return pl.pallas_call(
        functools.partial(condition_kernel, period),
        out_shape=[
            jax.ShapeDtypeStruct((2 * listed * TILE, 2 * LANES), jnp.bfloat16),
            jax.ShapeDtypeStruct((TILE, LANES), jnp.float32),
        ],
        in_specs=[vmem] * (groups + 1),
        out_specs=[vmem, vmem],
        scratch_shapes=[
            pltpu.VMEM((groups, rows, packed), jnp.bfloat16),
            pltpu.VMEM(((listed + 1) * TILE, groups * period), jnp.float32),
        ],
        compiler_params=pltpu.CompilerParams(vmem_limit_bytes=32 * 2**20),
        name="condition",
    )(taps, *received)


def correlate_kernel(
    partner_ref, reverse_ref, out_hbm, low_even, high_even, low_odd, high_odd, packed_ref, semaphores
):
    listed = out_hbm.shape[1]
    rows = listed * TILE
    normalizer = 1.0 / math.sqrt(LANES)
    keep = lax.broadcasted_iota(jnp.int32, (LANES, LANES), 1) <= lax.broadcasted_iota(
        jnp.int32, (LANES, LANES), 0
    )
    even, odd = (low_even, high_even), (low_odd, high_odd)
    count = TILE // 8
    parts = 4
    share = listed // parts

    def band(channel):
        line = jnp.broadcast_to(reverse_ref[pl.ds(channel, 1), :], (LANES, LANES))
        turned = pltpu.roll(line, 1, 1, stride=1, stride_axis=0)
        first = jnp.where(keep, turned, 0.0).astype(jnp.bfloat16)
        second = jnp.where(keep, 0.0, turned).astype(jnp.bfloat16)
        return jnp.concatenate([first, second], axis=0)

    def outgoing(group, part):
        tiles = pl.ds(part * share, share)
        return pltpu.make_async_copy(
            packed_ref.at[group, tiles],
            out_hbm.at[0, tiles, :, pl.ds(group * 8, 8), :],
            semaphores.at[group, part],
        )

    def multiply(group, part, held):
        channel = group * 8 + 2 * part
        weights = jnp.concatenate([band(channel), band(channel + 1)], axis=1)
        product = dot(partner_ref[...], weights) * normalizer
        for half, ref in enumerate(held):
            for side in range(2):
                ref[pl.ds(2 * part + side, rows, stride=STRIDE), :] = product[
                    half * rows : (half + 1) * rows, side * LANES : (side + 1) * LANES
                ]

    def convert(group, part, held):
        for tile in range(part * share, (part + 1) * share):
            for line in range(TILE):
                at = pl.ds((tile * TILE + line) * STRIDE, 8)
                both = jnp.concatenate([ref[at, :] for ref in held], axis=1)
                packed_ref[group, tile, line] = both.astype(jnp.bfloat16)

    def together(group, held, before):
        for part in range(parts):
            multiply(group, part, held)
            convert(group - 1, part, before)
        for part in range(parts):
            outgoing(group - 1, part).start()

    for part in range(parts):
        multiply(0, part, even)

    def two_groups(index, carry):
        together(2 * index + 1, odd, even)
        together(2 * index + 2, even, odd)
        return carry

    lax.fori_loop(0, count // 2, two_groups, 0)
    for part in range(parts):
        convert(count - 1, part, even)
        outgoing(count - 1, part).start()
    for group in range(count):
        for part in range(parts):
            outgoing(group, part).wait()


def correlate(partner, reverse):
    rows = partner.shape[0] // 2
    listed = rows // TILE
    vmem = pl.BlockSpec(memory_space=pltpu.VMEM)
    return pl.pallas_call(
        correlate_kernel,
        out_shape=jax.ShapeDtypeStruct((1, listed, TILE, TILE, LAGS), jnp.bfloat16),
        in_specs=[vmem, vmem],
        out_specs=pl.BlockSpec(memory_space=pltpu.HBM),
        scratch_shapes=[pltpu.VMEM((rows * STRIDE, LANES), jnp.float32)] * 4
        + [
            pltpu.VMEM((TILE // 8, listed, TILE, 8, LAGS), jnp.bfloat16),
            pltpu.SemaphoreType.DMA((TILE // 8, 4)),
        ],
        compiler_params=pltpu.CompilerParams(vmem_limit_bytes=40 * 2**20),
        name="correlate",
    )(partner, reverse)


def on_device(strain, fir_taps, half_widths, pairs):
    groups = lax.axis_size("grp")
    rep_count = lax.axis_size("rep")
    *messages, taps = pack(strain, fir_taps, half_widths, pairs, groups, rep_count)
    received = []
    for steps, message in zip(rounds(groups), messages):
        if steps == (0, 0):
            received.append(message)
            continue
        route = [
            (
                group * rep_count + member,
                partner_of(group, steps[member % 2], groups) * rep_count + member,
            )
            for group in range(groups)
            for member in range(rep_count)
        ]
        received.append(lax.ppermute(message, ("grp", "rep"), route))
    partner, reverse = conditioned(received, taps, strain.shape[1], pairs.shape[1])
    return correlate(partner, reverse)


def solution(mesh):
    placed = (P(None, "grp"), P(), P("grp"), P())
    return jax.shard_map(
        on_device,
        mesh=mesh,
        in_specs=placed,
        out_specs=P(("grp", "rep"), None, None, None, None),
        check_vma=False,
    )
```

time: 33.8 us -> 25.8 us (0.76)
  blocking collectives: 17.4 us -> 0 us
  starting transfers between devices: 0 us -> 12.5 us
  Pallas kernels: 13.3 us -> 8.54 us
  waiting for transfers between devices: 0 us -> 3.74 us
  local copies, waits for them, and re-layouts: 2.92 us -> 0.77 us
    all_to_all x1 -> x0, blocking collectives: 17.4 us -> none  [on_device(): lax.all_to_all(message, 'grp', split_axis=0, concat_axis=0, tiled=True)]
    ppermute x0 -> x7, starting transfers between devices: none -> 12.5 us  [on_device(): received.append(lax.ppermute(message, ('grp', 'rep'), route))]
    pallas_call x2 -> x3, Pallas kernels: 13.3 us -> 8.54 us  [the longest x1 4.46 us: correlate(): pl.pallas_call(correlate_kernel, out_shape=jax.ShapeDtypeStruct((1, liste...]
    ppermute x0 -> x7, waiting for transfers between devices: none -> 3.74 us  [on_device(): received.append(lax.ppermute(message, ('grp', 'rep'), route))]
    unnamed x8 -> x2, local copies, waits for them, and re-layouts: 2.92 us -> 0.77 us
  transfers between devices with their start and end apart: 0 -> 7, of which waited for: 0 -> 5; matrix products, arithmetic and copies ran while one was open for 0% -> 0% of each run, Pallas kernels for 0% -> 0%
where the time goes in v2:
time: 25.8 us; the launch traced here: 25.6 us
  starting transfers between devices  12.5 us (48%)
  Pallas kernels  8.54 us (33%)
  waiting for transfers between devices  3.74 us (14%)
  local copies, waits for them, and re-layouts  0.77 us (3%)
    ppermute x7, starting transfers between devices, on_device(): received.append(lax.ppermute(message, ('grp', 'rep'), route))  12.5 us
    pallas_call x1, Pallas kernels, correlate(): pl.pallas_call(correlate_kernel, out_shape=jax.ShapeDtypeStruct((1, liste...  4.46 us
    ppermute x7, waiting for transfers between devices, on_device(): received.append(lax.ppermute(message, ('grp', 'rep'), route))  3.74 us
    pallas_call x1, Pallas kernels, pack(): pl.pallas_call(functools.partial(pack_kernel, rep_count), out_shape=[pltp...  2.48 us
    pallas_call x1, Pallas kernels, conditioned(): pl.pallas_call(functools.partial(condition_kernel, period), out_shape=[ja...  1.6 us
    unnamed x2, local copies, waits for them, and re-layouts  0.77 us
  transfers between devices with their start and end apart: 7, of which 5 were waited for; matrix products, arithmetic and copies ran while one was open for 0% of the time, Pallas kernels for 0%

profile of v2, /device:TPU:0, one launch (start us, length us, event | category | flops | bytes accessed | tf_op | source)
XLA Modules:
  0.0 25.6 jit_solution(9141681826271903368)
XLA Ops:
  0.0 2.5 %pack.1 = (bf16[48,384]{1,0:T(8,128)(2,1)}, bf16[48,384]{1,0:T(8,128)(2,1)}, bf16[48,384]{1,0:T(8,128)(2,1)}, bf16[48,384]{1,0:T(8,128)(2,1)}, bf16[48,384]{1,0:...) custom-call(s32[8,32]{1,0:T(8,128)} %bitcast.5, ...), custom_call_target="tpu_custom_call" | custom-call | tf_op jit(solution)/shard_map/pack/pallas_call | solution.py:145
  2.5 6.0 %collective-permute-start = (bf16[48,384]{1,0:T(8,128)(2,1)}, bf16[48,384]{1,0:T(8,128)(2,1)S(1)}, u32[]{:S(2)}, u32[]{:S(2)}) collective-permute-start(bf16[48,384]{1,0:T(8,128)(2,1)} %get-tuple-element.17), channel_id=1, source_target_pairs={{0,28},{1,13},{2,30},{3,15},{4,24},{5,9},{6,26},{7,11},{8,20},{9,5... | collective-permute-start | bytes 110600 | tf_op jit(solution)/shard_map/ppermute | solution.py:401
  8.5 0.2 collective-permute-start.1
  8.8 0.8 %collective-permute-start.2 = (bf16[48,384]{1,0:T(8,128)(2,1)}, bf16[48,384]{1,0:T(8,128)(2,1)S(1)}, u32[]{:S(2)}, u32[]{:S(2)}) collective-permute-start(bf16[48,384]{1,0:T(8,128)(2,1)} %get-tuple-element.19), channel_id=1, source_target_pairs={{0,20},{1,5},{2,22},{3,7},{4,16},{5,1},{6,18},{7,3},{8,28},{9,13},... | collective-permute-start | bytes 110600 | tf_op jit(solution)/shard_map/ppermute | solution.py:401
  9.5 2.0 %collective-permute-start.3 = (bf16[48,384]{1,0:T(8,128)(2,1)}, bf16[48,384]{1,0:T(8,128)(2,1)S(1)}, u32[]{:S(2)}, u32[]{:S(2)}) collective-permute-start(bf16[48,384]{1,0:T(8,128)(2,1)} %get-tuple-element.20), channel_id=1, source_target_pairs={{0,16},{1,29},{2,18},{3,31},{4,20},{5,25},{6,22},{7,27},{8,24},{9,... | collective-permute-start | bytes 110600 | tf_op jit(solution)/shard_map/ppermute | solution.py:401
  11.5 2.3 %collective-permute-start.4 = (bf16[48,384]{1,0:T(8,128)(2,1)}, bf16[48,384]{1,0:T(8,128)(2,1)S(1)}, u32[]{:S(2)}, u32[]{:S(2)}) collective-permute-start(bf16[48,384]{1,0:T(8,128)(2,1)} %get-tuple-element.21), channel_id=1, source_target_pairs={{0,12},{1,25},{2,14},{3,27},{4,8},{5,29},{6,10},{7,31},{8,4},{9,17... | collective-permute-start | bytes 110600 | tf_op jit(solution)/shard_map/ppermute | solution.py:401
  13.8 0.0 collective-permute-done.refs_0_
  13.8 0.8 %collective-permute-start.5 = (bf16[48,384]{1,0:T(8,128)(2,1)}, bf16[48,384]{1,0:T(8,128)(2,1)S(1)}, u32[]{:S(2)}, u32[]{:S(2)}) collective-permute-start(bf16[48,384]{1,0:T(8,128)(2,1)} %get-tuple-element.22), channel_id=1, source_target_pairs={{0,8},{1,21},{2,10},{3,23},{4,12},{5,17},{6,14},{7,19},{8,0},{9,29... | collective-permute-start | bytes 110600 | tf_op jit(solution)/shard_map/ppermute | solution.py:401
  14.6 0.0 collective-permute-done.1.refs_1_
  14.6 0.4 %collective-permute-start.6 = (bf16[48,384]{1,0:T(8,128)(2,1)}, bf16[48,384]{1,0:T(8,128)(2,1)S(1)}, u32[]{:S(2)}, u32[]{:S(2)}) collective-permute-start(bf16[48,384]{1,0:T(8,128)(2,1)} %get-tuple-element.23), channel_id=1, source_target_pairs={{0,4},{1,17},{2,6},{3,19},{4,0},{5,21},{6,2},{7,23},{8,12},{9,25},... | collective-permute-start | bytes 110600 | tf_op jit(solution)/shard_map/ppermute | solution.py:401
  15.0 0.2 collective-permute-done.2.refs_2_
  15.3 1.2 %collective-permute-done.3.refs_3_ = bf16[48,384]{1,0:T(8,128)(2,1)S(1)} collective-permute-done((bf16[48,384]{1,0:T(8,128)(2,1)}, bf16[48,384]{1,0:T(8,128)(2,1)S(1)}, u32[]{:S(2)}, u32[]{:S(2)}) %collective-permute-start.3) | collective-permute-done | bytes 36896 | tf_op jit(solution)/shard_map/ppermute | solution.py:401
  16.5 1.2 %collective-permute-done.4.refs_4_ = bf16[48,384]{1,0:T(8,128)(2,1)S(1)} collective-permute-done((bf16[48,384]{1,0:T(8,128)(2,1)}, bf16[48,384]{1,0:T(8,128)(2,1)S(1)}, u32[]{:S(2)}, u32[]{:S(2)}) %collective-permute-start.4) | collective-permute-done | bytes 36896 | tf_op jit(solution)/shard_map/ppermute | solution.py:401
  17.6 0.4 %collective-permute-done.5.refs_5_ = bf16[48,384]{1,0:T(8,128)(2,1)S(1)} collective-permute-done((bf16[48,384]{1,0:T(8,128)(2,1)}, bf16[48,384]{1,0:T(8,128)(2,1)S(1)}, u32[]{:S(2)}, u32[]{:S(2)}) %collective-permute-start.5) | collective-permute-done | bytes 36896 | tf_op jit(solution)/shard_map/ppermute | solution.py:401
  18.0 0.8 %collective-permute-done.6.refs_6_ = bf16[48,384]{1,0:T(8,128)(2,1)S(1)} collective-permute-done((bf16[48,384]{1,0:T(8,128)(2,1)}, bf16[48,384]{1,0:T(8,128)(2,1)S(1)}, u32[]{:S(2)}, u32[]{:S(2)}) %collective-permute-start.6) | collective-permute-done | bytes 36896 | tf_op jit(solution)/shard_map/ppermute | solution.py:401
  18.8 0.0 copy-start
  18.8 0.8 %copy-done = bf16[48,384]{1,0:T(8,128)(2,1)S(1)} copy-done((bf16[48,384]{1,0:T(8,128)(2,1)S(1)}, bf16[48,384]{1,0:T(8,128)(2,1)}, u32[]{:S(2)}) %copy-start) | copy-done | bytes 36888
  19.6 1.6 %condition.1 = (bf16[640,256]{1,0:T(8,128)(2,1)S(1)}, f32[40,128]{1,0:T(8,128)S(1)}) custom-call(f32[1,64]{1,0:T(1,128)S(1)} %get-tuple-element.16.taps_ref, bf16[48,384]{1,0:T(8,128)(2,1)S(1)} %collective-permute-done.refs_0_, bf16[48,384]{1,0:T(8,128)(2,1)S(1)} %collective-permute-done.1.refs_1_, bf16[48,384]{1,0:T(8,128)(2,1)S(1)} %collective-permute-done.2.refs_2_, ...), custom_call_target="tpu_custom_call" | custom-call | tf_op jit(solution)/shard_map/condition/pallas_call | solution.py:278
  21.2 4.5 %correlate.1 = bf16[1,8,40,40,256]{4,3,2,1,0:T(8,128)(2,1)} custom-call(bf16[640,256]{1,0:T(8,128)(2,1)S(1)} %get-tuple-element.25.partner_ref, f32[40,128]{1,0:T(8,128)S(1)} %get-tuple-element.26.reverse_ref), custom_call_target="tpu_custom_call" | custom-call | tf_op jit(solution)/shard_map/correlate/pallas_call | solution.py:369
Async XLA Ops:
  2.5 11.3 %collective-permute-start = (bf16[48,384]{1,0:T(8,128)(2,1)}, bf16[48,384]{1,0:T(8,128)(2,1)S(1)}, u32[]{:S(2)}, u32[]{:S(2)}) collective-permute-start(bf16[48,384]{1,0:T(8,128)(2,1)} %get-tuple-element.17), channel_id=1, source_target_pairs={{0,28},{1,13},{2,30},{3,15},{4,24},{5,9},{6,26},{7,11},{8,20},{9,5... | collective-permute-start | bytes 110600 | tf_op jit(solution)/shard_map/ppermute | solution.py:401
  8.5 6.1 %collective-permute-start.1 = (bf16[48,384]{1,0:T(8,128)(2,1)}, bf16[48,384]{1,0:T(8,128)(2,1)S(1)}, u32[]{:S(2)}, u32[]{:S(2)}) collective-permute-start(bf16[48,384]{1,0:T(8,128)(2,1)} %get-tuple-element.18), channel_id=1, source_target_pairs={{0,24},{1,9},{2,26},{3,11},{4,28},{5,13},{6,30},{7,15},{8,16},{9,1... | collective-permute-start | bytes 110600 | tf_op jit(solution)/shard_map/ppermute | solution.py:401
  8.8 6.5 %collective-permute-start.2 = (bf16[48,384]{1,0:T(8,128)(2,1)}, bf16[48,384]{1,0:T(8,128)(2,1)S(1)}, u32[]{:S(2)}, u32[]{:S(2)}) collective-permute-start(bf16[48,384]{1,0:T(8,128)(2,1)} %get-tuple-element.19), channel_id=1, source_target_pairs={{0,20},{1,5},{2,22},{3,7},{4,16},{5,1},{6,18},{7,3},{8,28},{9,13},... | collective-permute-start | bytes 110600 | tf_op jit(solution)/shard_map/ppermute | solution.py:401
  9.5 6.9 %collective-permute-start.3 = (bf16[48,384]{1,0:T(8,128)(2,1)}, bf16[48,384]{1,0:T(8,128)(2,1)S(1)}, u32[]{:S(2)}, u32[]{:S(2)}) collective-permute-start(bf16[48,384]{1,0:T(8,128)(2,1)} %get-tuple-element.20), channel_id=1, source_target_pairs={{0,16},{1,29},{2,18},{3,31},{4,20},{5,25},{6,22},{7,27},{8,24},{9,... | collective-permute-start | bytes 110600 | tf_op jit(solution)/shard_map/ppermute | solution.py:401
  11.5 6.1 %collective-permute-start.4 = (bf16[48,384]{1,0:T(8,128)(2,1)}, bf16[48,384]{1,0:T(8,128)(2,1)S(1)}, u32[]{:S(2)}, u32[]{:S(2)}) collective-permute-start(bf16[48,384]{1,0:T(8,128)(2,1)} %get-tuple-element.21), channel_id=1, source_target_pairs={{0,12},{1,25},{2,14},{3,27},{4,8},{5,29},{6,10},{7,31},{8,4},{9,17... | collective-permute-start | bytes 110600 | tf_op jit(solution)/shard_map/ppermute | solution.py:401
  13.8 4.2 %collective-permute-start.5 = (bf16[48,384]{1,0:T(8,128)(2,1)}, bf16[48,384]{1,0:T(8,128)(2,1)S(1)}, u32[]{:S(2)}, u32[]{:S(2)}) collective-permute-start(bf16[48,384]{1,0:T(8,128)(2,1)} %get-tuple-element.22), channel_id=1, source_target_pairs={{0,8},{1,21},{2,10},{3,23},{4,12},{5,17},{6,14},{7,19},{8,0},{9,29... | collective-permute-start | bytes 110600 | tf_op jit(solution)/shard_map/ppermute | solution.py:401
  14.6 4.2 %collective-permute-start.6 = (bf16[48,384]{1,0:T(8,128)(2,1)}, bf16[48,384]{1,0:T(8,128)(2,1)S(1)}, u32[]{:S(2)}, u32[]{:S(2)}) collective-permute-start(bf16[48,384]{1,0:T(8,128)(2,1)} %get-tuple-element.23), channel_id=1, source_target_pairs={{0,4},{1,17},{2,6},{3,19},{4,0},{5,21},{6,2},{7,23},{8,12},{9,25},... | collective-permute-start | bytes 110600 | tf_op jit(solution)/shard_map/ppermute | solution.py:401
  18.8 0.8 %copy-start = (bf16[48,384]{1,0:T(8,128)(2,1)S(1)}, bf16[48,384]{1,0:T(8,128)(2,1)}, u32[]{:S(2)}) copy-start(bf16[48,384]{1,0:T(8,128)(2,1)} %get-tuple-element.24.refs_7_) | copy-start | bytes 110596

commit v3 on v2

--- a/solution.py
+++ b/solution.py
@@ -26,48 +26,16 @@
         copy.wait()
 
 
-def partner_of(group, step, groups):
-    if groups & (groups - 1) == 0:
-        return group ^ step
-    return (step + groups - group) % groups
-
-
-def rounds(groups):
-    even = list(range(groups - 1, 0, -1))
-    far = groups // 2
-    odd = [step for step in even if step < far] + [step for step in even if step >= far]
-    return list(zip(even, odd)) + [(0, 0)]
-
-
-def step_of(steps, member):
-    even, odd = steps
-    return even if even == odd else jnp.where(lax.rem(member, 2) == 0, even, odd)
-
-
-def pack_kernel(rep_count, pairs_hbm, strain_hbm, widths_hbm, taps_hbm, *refs):
-    outs_hbm = refs[:-9]
-    taps_ref, stage_ref, sent = refs[-9:-6]
-    out_refs = [stage_ref.at[index] for index in range(len(outs_hbm))]
-    pairs_ref, strain_ref, widths_ref, semaphores, blocks_ref, table_ref = refs[-6:]
-    groups = len(out_refs)
-    rows, packed = out_refs[0].shape
+def gather_tiles(groups, rep_count, source, pairs_ref, strain_ref, widths_ref, blocks_ref, table_ref, write):
+    rows = blocks_ref.shape[1]
+    filled, channels = strain_ref.shape
     listed = pairs_ref.shape[0]
-    channels = strain_ref.shape[1]
+    packed = -(-(listed + 1) // PER_BLOCK) * LANES
     members = widths_ref.shape[1]
-    fetch(
-        [
-            (strain_hbm, strain_ref),
-            (pairs_hbm, pairs_ref),
-            (widths_hbm, widths_ref),
-            (taps_hbm, taps_ref),
-        ],
-        semaphores,
-    )
     my_rep = lax.axis_index("rep")
     my_grp = lax.axis_index("grp")
 
     count = channels // LANES
-    filled = strain_ref.shape[0]
     for block in range(count):
         values = strain_ref[:, block * LANES : (block + 1) * LANES].astype(jnp.float32)
         if rows > filled:
@@ -89,18 +57,18 @@
 
     lane = lax.broadcasted_iota(jnp.int32, (rows, LANES), 1)
     spare = LANES - 8
-    for steps, out_ref in zip(rounds(groups), out_refs):
-        group = partner_of(my_grp, step_of(steps, my_rep), groups)
+    for step in rounds(groups):
+        group = lax.rem(my_grp + 2 * step, groups)
         tile = group * rep_count + my_rep
         chosen = [tile]
         member, place_of = jnp.int32(0), jnp.int32(-1)
         for slot in range(listed):
             other = pairs_ref[slot, tile]
             chosen.append(jnp.maximum(other, 0))
-            inside = (other >= 0) & (lax.div(other, rep_count) == my_grp)
+            inside = (other >= 0) & (lax.div(other, rep_count) == source)
             member = jnp.where(inside, lax.rem(other, rep_count), member)
             place_of = jnp.where(inside, slot + 1, place_of)
-        own_at = jnp.where(group == my_grp, spare, -1)
+        own_at = jnp.where(group == source, spare, -1)
         theirs = table_ref[member]
         mine = table_ref[my_rep]
         for block in range(packed // LANES):
@@ -110,9 +78,9 @@
                 if index > listed:
                     continue
                 start = chosen[index] * TILE
-                source = lax.div(start, LANES)
+                at = lax.div(start, LANES)
                 offset = lax.rem(start, LANES)
-                both = jnp.where(lane >= offset, blocks_ref[source], blocks_ref[source + 1])
+                both = jnp.where(lane >= offset, blocks_ref[at], blocks_ref[at + 1])
                 shift = lax.rem(place * TILE + LANES - offset, LANES)
                 moved = pltpu.roll(both, shift, 1)
                 here = (lane >= place * TILE) & (lane < (place + 1) * TILE)
@@ -123,10 +91,17 @@
             total = jnp.where(lane == marked, theirs, total)
             if block == 0:
                 total = jnp.where(lane == own_at, mine, total)
-            out_ref[:, block * LANES : (block + 1) * LANES] = total.astype(jnp.bfloat16)
+            write(step, slice(block * LANES, (block + 1) * LANES), total.astype(jnp.bfloat16))
+
+
+def rounds(groups):
+    return list(range(1, groups // 2)) + [0]
+
+
+def fetch(pairs, semaphores):
     copies = [
-        pltpu.make_async_copy(stage_ref.at[index], out_hbm, sent.at[index])
-        for index, out_hbm in enumerate(outs_hbm)
+        pltpu.make_async_copy(source, target, semaphores.at[index])
+        for index, (source, target) in enumerate(pairs)
     ]
     for copy in copies:
         copy.start()
@@ -134,36 +109,91 @@
         copy.wait()
 
 
-def pack(strain, fir_taps, half_widths, pairs, groups, rep_count):
+def pack_own_kernel(
+    groups, rep_count, pairs_hbm, strain_hbm, widths_hbm, taps_hbm, out_ref, list_ref, taps_ref,
+    pairs_ref, strain_ref, widths_ref, semaphores, blocks_ref, table_ref,
+):
+    fetch(
+        [
+            (strain_hbm, strain_ref),
+            (pairs_hbm, pairs_ref),
+            (widths_hbm, widths_ref),
+            (pairs_hbm, list_ref),
+            (taps_hbm, taps_ref),
+        ],
+        semaphores,
+    )
+
+    def write(step, at, value):
+        out_ref[step, :, at] = value
+
+    gather_tiles(
+        groups, rep_count, lax.axis_index("grp"), pairs_ref, strain_ref, widths_ref, blocks_ref, table_ref, write
+    )
+
+
+def pack_both_kernel(groups, rep_count, list_ref, widths_ref, strain_ref, own_ref, *refs):
+    out_refs = refs[:-4]
+    pairs_ref, semaphores, blocks_ref, table_ref = refs[-4:]
+    fetch([(list_ref, pairs_ref)], semaphores)
+    my_grp = lax.axis_index("grp")
+    side = lax.rem(my_grp, 2)
+    by_step = dict(zip(rounds(groups), out_refs))
+    for step, out_ref in by_step.items():
+        out_ref[side] = own_ref[step]
+
+    def write(step, at, value):
+        by_step[step][1 - side, :, at] = value
+
+    gather_tiles(groups, rep_count, my_grp ^ 1, pairs_ref, strain_ref, widths_ref, blocks_ref, table_ref, write)
+
+
+def pack(strain, other_strain, fir_taps, half_widths, other_widths, pairs, groups, rep_count):
     channels, filled = strain.shape
     rows = max(filled, -(-TILE // 16) * 16)
     tiles, listed = pairs.shape
     members = half_widths.shape[0]
     packed = -(-(listed + 1) // PER_BLOCK) * LANES
+    halves = groups // 2
     hbm = pl.BlockSpec(memory_space=pltpu.HBM)
     vmem = pl.BlockSpec(memory_space=pltpu.VMEM)
-    return pl.pallas_call(
-        functools.partial(pack_kernel, rep_count),
-        out_shape=[pltpu.HBM((rows, packed), jnp.bfloat16)] * groups
-        + [jax.ShapeDtypeStruct((1, fir_taps.shape[0]), jnp.float32)],
+    work = [
+        pltpu.VMEM((channels // LANES + 1, rows, LANES), jnp.float32),
+        pltpu.VMEM((rep_count, rows, LANES), jnp.float32),
+    ]
+    params = pltpu.CompilerParams(vmem_limit_bytes=32 * 2**20)
+    own, chosen, taps = pl.pallas_call(
+        functools.partial(pack_own_kernel, groups, rep_count),
+        out_shape=[
+            jax.ShapeDtypeStruct((halves, rows, packed), jnp.bfloat16),
+            jax.ShapeDtypeStruct((listed, tiles), jnp.int32),
+            jax.ShapeDtypeStruct((1, fir_taps.shape[0]), jnp.float32),
+        ],
         in_specs=[hbm] * 4,
-        out_specs=[hbm] * groups + [vmem],
+        out_specs=[vmem] * 3,
         scratch_shapes=[
-            pltpu.VMEM((groups, rows, packed), jnp.bfloat16),
-            pltpu.SemaphoreType.DMA((groups,)),
             pltpu.SMEM((listed, tiles), jnp.int32),
             pltpu.VMEM((filled, channels), jnp.bfloat16),
             pltpu.VMEM((1, members), jnp.int32),
-            pltpu.SemaphoreType.DMA((4,)),
-            pltpu.VMEM((channels // LANES + 1, rows, LANES), jnp.float32),
-            pltpu.VMEM((rep_count, rows, LANES), jnp.float32),
-        ],
-        compiler_params=pltpu.CompilerParams(vmem_limit_bytes=48 * 2**20),
-        name="pack",
+            pltpu.SemaphoreType.DMA((5,)),
+        ]
+        + work,
+        compiler_params=params,
+        name="pack_own",
     )(*[
         pltpu.with_memory_space_constraint(array, pltpu.HBM)
         for array in (pairs.T, strain.T, half_widths[None, :], fir_taps[None, :])
     ])
+    messages = pl.pallas_call(
+        functools.partial(pack_both_kernel, groups, rep_count),
+        out_shape=[jax.ShapeDtypeStruct((2, rows, packed), jnp.bfloat16)] * halves,
+        in_specs=[vmem] * 4,
+        out_specs=[vmem] * halves,
+        scratch_shapes=[pltpu.SMEM((listed, tiles), jnp.int32), pltpu.SemaphoreType.DMA((1,))] + work,
+        compiler_params=params,
+        name="pack_both",
+    )(chosen, other_widths[None, :], other_strain, own)
+    return messages, taps
 
 
 def split(values):
@@ -177,15 +207,16 @@
 
 
 def condition(period, raw_ref, taps_ref, white_ref):
-    groups, rows, packed = raw_ref.shape
+    halves, _, rows, packed = raw_ref.shape
+    groups = 2 * halves
     listed = white_ref.shape[0] // TILE - 1
     blocks = packed // LANES
-    raw = raw_ref[:, :period, :].astype(jnp.float32).reshape(groups * period, packed)
+    raw = raw_ref[:, :, :period, :].astype(jnp.float32).reshape(groups * period, packed)
     samples = jnp.transpose(raw).astype(jnp.bfloat16)
     columns = []
     for block in range(blocks):
-        piece = raw_ref[:, :TILE, block * LANES : (block + 1) * LANES].astype(jnp.float32)
-        columns.append(jnp.sum(piece, axis=0))
+        piece = raw_ref[:, :, :TILE, block * LANES : (block + 1) * LANES].astype(jnp.float32)
+        columns.append(jnp.sum(piece.reshape(groups, TILE, LANES), axis=0))
 
     count = taps_ref.shape[1]
     taps = jnp.concatenate([taps_ref[...], jnp.zeros((1, 2 * LANES - count), jnp.float32)], axis=1)
@@ -253,11 +284,10 @@
 def condition_kernel(period, taps_ref, *refs):
     received = refs[:-4]
     partner_ref, reverse_ref, raw_ref, white_ref = refs[-4:]
-    groups = len(received)
-    my_grp = lax.axis_index("grp")
-    my_rep = lax.axis_index("rep")
-    for steps, ref in zip(rounds(groups), received):
-        raw_ref[partner_of(my_grp, step_of(steps, my_rep), groups)] = ref[...]
+    halves = len(received)
+    my_half = lax.div(lax.axis_index("grp"), 2)
+    for step, ref in zip(rounds(2 * halves), received):
+        raw_ref[lax.rem(my_half + halves - step, halves)] = ref[...]
     condition(period, raw_ref, taps_ref, white_ref)
 
     partner = white_ref[TILE:, :].astype(jnp.bfloat16)
@@ -272,8 +302,8 @@
 
 
 def conditioned(received, taps, period, listed):
-    groups = len(received)
-    rows, packed = received[0].shape
+    halves = len(received)
+    _, rows, packed = received[0].shape
     vmem = pl.BlockSpec(memory_space=pltpu.VMEM)
     return pl.pallas_call(
         functools.partial(condition_kernel, period),
@@ -281,11 +311,11 @@
             jax.ShapeDtypeStruct((2 * listed * TILE, 2 * LANES), jnp.bfloat16),
             jax.ShapeDtypeStruct((TILE, LANES), jnp.float32),
         ],
-        in_specs=[vmem] * (groups + 1),
+        in_specs=[vmem] * (halves + 1),
         out_specs=[vmem, vmem],
         scratch_shapes=[
-            pltpu.VMEM((groups, rows, packed), jnp.bfloat16),
-            pltpu.VMEM(((listed + 1) * TILE, groups * period), jnp.float32),
+            pltpu.VMEM((halves, 2, rows, packed), jnp.bfloat16),
+            pltpu.VMEM(((listed + 1) * TILE, 2 * halves * period), jnp.float32),
         ],
         compiler_params=pltpu.CompilerParams(vmem_limit_bytes=32 * 2**20),
         name="condition",
@@ -384,21 +414,18 @@
 def on_device(strain, fir_taps, half_widths, pairs):
     groups = lax.axis_size("grp")
     rep_count = lax.axis_size("rep")
-    *messages, taps = pack(strain, fir_taps, half_widths, pairs, groups, rep_count)
+    neighbours = [(group, group ^ 1) for group in range(groups)]
+    other_widths = lax.ppermute(half_widths, "grp", neighbours)
+    other_strain = lax.ppermute(strain.T, "grp", neighbours)
+    messages, taps = pack(
+        strain, other_strain, fir_taps, half_widths, other_widths, pairs, groups, rep_count
+    )
     received = []
-    for steps, message in zip(rounds(groups), messages):
-        if steps == (0, 0):
-            received.append(message)
-            continue
-        route = [
-            (
-                group * rep_count + member,
-                partner_of(group, steps[member % 2], groups) * rep_count + member,
-            )
-            for group in range(groups)
-            for member in range(rep_count)
-        ]
-        received.append(lax.ppermute(message, ("grp", "rep"), route))
+    for step, message in zip(rounds(groups), messages):
+        if step:
+            route = [(group, (group + 2 * step) % groups) for group in range(groups)]
+            message = lax.ppermute(message, "grp", route)
+        received.append(message)
     partner, reverse = conditioned(received, taps, strain.shape[1], pairs.shape[1])
     return correlate(partner, reverse)
 

time: 25.8 us -> 23.1 us (0.90)
  starting transfers between devices: 12.5 us -> 8.6 us
  waiting for transfers between devices: 3.74 us -> 5.87 us
  local copies, waits for them, and re-layouts: 0.77 us -> 0 us
    ppermute x7 -> x5, starting transfers between devices: 12.5 us -> 8.6 us  [the longest x3 5.63 us: on_device(): message = lax.ppermute(message, 'grp', route)]
    ppermute x7 -> x5, waiting for transfers between devices: 3.74 us -> 5.87 us  [the longest x3 3.48 us: on_device(): message = lax.ppermute(message, 'grp', route)]
    unnamed x2 -> x0, local copies, waits for them, and re-layouts: 0.77 us -> none
    pallas_call x1 -> x2, Pallas kernels: 2.48 us -> 2.38 us  [the longest x1 1.36 us: pack(): pl.pallas_call(functools.partial(pack_own_kernel, groups, rep_count), out...]
  transfers between devices with their start and end apart: 7 -> 5, of which waited for: 5 -> 4; matrix products, arithmetic and copies ran while one was open for 0% -> 0% of each run, Pallas kernels for 0% -> 6%
where the time goes in v3:
time: 23.1 us; the launch traced here: 22.9 us
  starting transfers between devices  8.6 us (37%)
  Pallas kernels  8.43 us (36%)
  waiting for transfers between devices  5.87 us (25%)
    ppermute x3, starting transfers between devices, on_device(): message = lax.ppermute(message, 'grp', route)  5.63 us
    pallas_call x1, Pallas kernels, correlate(): pl.pallas_call(correlate_kernel, out_shape=jax.ShapeDtypeStruct((1, liste...  4.47 us
    ppermute x3, waiting for transfers between devices, on_device(): message = lax.ppermute(message, 'grp', route)  3.48 us
    ppermute x1, starting transfers between devices, on_device(): other_strain = lax.ppermute(strain.T, 'grp', neighbours)  2.94 us
    ppermute x1, waiting for transfers between devices, on_device(): other_widths = lax.ppermute(half_widths, 'grp', neighbours)  2.38 us
    pallas_call x1, Pallas kernels, conditioned(): pl.pallas_call(functools.partial(condition_kernel, period), out_shape=[ja...  1.59 us
    pallas_call x1, Pallas kernels, pack(): pl.pallas_call(functools.partial(pack_own_kernel, groups, rep_count), out...  1.36 us
    pallas_call x1, Pallas kernels, pack(): pl.pallas_call(functools.partial(pack_both_kernel, groups, rep_count), ou...  1.02 us
  transfers between devices with their start and end apart: 5, of which 4 were waited for; matrix products, arithmetic and copies ran while one was open for 0% of the time, Pallas kernels for 6%

profile of v3, /device:TPU:0, one launch (start us, length us, event | category | flops | bytes accessed | tf_op | source)
XLA Modules:
  0.0 22.9 jit_solution(7175685700709488543)
XLA Ops:
  0.0 2.9 %collective-permute-start.1 = (bf16[48,1280]{1,0:T(8,128)(2,1)}, bf16[48,1280]{1,0:T(8,128)(2,1)S(1)}, u32[]{:S(2)}, u32[]{:S(2)}) collective-permute-start(bf16[48,1280]{1,0:T(8,128)(2,1)} %bitcast.6), channel_id=1, source_target_pairs={{0,4},{4,0},{8,12},{12,8},{16,20},{20,16},{24,28},{28,24},{1,5},{5... | collective-permute-start | bytes 368648 | tf_op jit(solution)/shard_map/ppermute | solution.py:419
  2.9 0.0 collective-permute-start
  3.0 1.4 %pack_own.1 = (bf16[4,48,384]{2,1,0:T(8,128)(2,1)S(1)}, s32[8,32]{1,0:T(8,128)S(1)}, f32[1,64]{1,0:T(1,128)S(1)}) custom-call(s32[8,32]{1,0:T(8,128)} %bitcast.8, bf16[48,1280]{1,0:T(8,128)(2,1)} %bitcast.7, s32[1,160]{1,0:T(1,128)} %bitcast.9, f32[1,64]{1,0:T(1,128)} %bitcast.10), custom_call_target="tpu_custom_call" | custom-call | tf_op jit(solution)/shard_map/pack_own/pallas_call | solution.py:165
  4.3 2.4 %collective-permute-done = s32[160]{0:T(256)S(1)} collective-permute-done((s32[160]{0:T(256)}, s32[160]{0:T(256)S(1)}, u32[]{:S(2)}, u32[]{:S(2)}) %collective-permute-start) | collective-permute-done | bytes 672 | tf_op jit(solution)/shard_map/ppermute | solution.py:418
  6.7 0.0 collective-permute-done.1.strain_ref
  6.7 1.0 %pack_both.1 = (bf16[2,48,384]{2,1,0:T(8,128)(2,1)S(1)}, bf16[2,48,384]{2,1,0:T(8,128)(2,1)S(1)}, bf16[2,48,384]{2,1,0:T(8,128)(2,1)S(1)}, bf16[2,48,384]{2,1,0:T(8,128)(2,1)S(1)}) custom-call(s32[8,32]{1,0:T(8,128)S(1)} %get-tuple-element.15.list_ref, s32[1,160]{1,0:T(1,128)S(1)} %bitcast.5, bf16[48,1280]{1,0:T(8,128)(2,1)S(1)} %collective-permute-done.1.strain_ref, ...), custom_call_target="tpu_custom_call" | custom-call | tf_op jit(solution)/shard_map/pack_both/pallas_call | solution.py:187
  7.8 1.7 %collective-permute-start.2 = (bf16[2,48,384]{2,1,0:T(8,128)(2,1)S(1)}, bf16[2,48,384]{2,1,0:T(8,128)(2,1)S(1)}, u32[]{:S(2)}, u32[]{:S(2)}) collective-permute-start(bf16[2,48,384]{2,1,0:T(8,128)(2,1)S(1)} %get-tuple-element.17), channel_id=1, source_target_pairs={{0,8},{4,12},{8,16},{12,20},{16,24},{20,28},{24,0},{28,4},{1,9},{5... | collective-permute-start | bytes 221192 | tf_op jit(solution)/shard_map/ppermute | solution.py:427
  9.4 2.6 %collective-permute-start.3 = (bf16[2,48,384]{2,1,0:T(8,128)(2,1)S(1)}, bf16[2,48,384]{2,1,0:T(8,128)(2,1)S(1)}, u32[]{:S(2)}, u32[]{:S(2)}) collective-permute-start(bf16[2,48,384]{2,1,0:T(8,128)(2,1)S(1)} %get-tuple-element.18), channel_id=1, source_target_pairs={{0,16},{4,20},{8,24},{12,28},{16,0},{20,4},{24,8},{28,12},{1,17},{... | collective-permute-start | bytes 221192 | tf_op jit(solution)/shard_map/ppermute | solution.py:427
  12.0 1.3 %collective-permute-start.4 = (bf16[2,48,384]{2,1,0:T(8,128)(2,1)S(1)}, bf16[2,48,384]{2,1,0:T(8,128)(2,1)S(1)}, u32[]{:S(2)}, u32[]{:S(2)}) collective-permute-start(bf16[2,48,384]{2,1,0:T(8,128)(2,1)S(1)} %get-tuple-element.19), channel_id=1, source_target_pairs={{0,24},{4,28},{8,0},{12,4},{16,8},{20,12},{24,16},{28,20},{1,25},{... | collective-permute-start | bytes 221192 | tf_op jit(solution)/shard_map/ppermute | solution.py:427
  13.4 1.4 %collective-permute-done.2.refs_0_ = bf16[2,48,384]{2,1,0:T(8,128)(2,1)S(1)} collective-permute-done((bf16[2,48,384]{2,1,0:T(8,128)(2,1)S(1)}, bf16[2,48,384]{2,1,0:T(8,128)(2,1)S(1)}, u32[]{:S(2)}, u32[]{:S(2)}) %collective-permute-start.2) | collective-permute-done | bytes 73760 | tf_op jit(solution)/shard_map/ppermute | solution.py:427
  14.7 2.0 %collective-permute-done.3.refs_1_ = bf16[2,48,384]{2,1,0:T(8,128)(2,1)S(1)} collective-permute-done((bf16[2,48,384]{2,1,0:T(8,128)(2,1)S(1)}, bf16[2,48,384]{2,1,0:T(8,128)(2,1)S(1)}, u32[]{:S(2)}, u32[]{:S(2)}) %collective-permute-start.3) | collective-permute-done | bytes 73760 | tf_op jit(solution)/shard_map/ppermute | solution.py:427
  16.8 0.1 collective-permute-done.4.refs_2_
  16.9 1.6 %condition.1 = (bf16[640,256]{1,0:T(8,128)(2,1)S(1)}, f32[40,128]{1,0:T(8,128)S(1)}) custom-call(f32[1,64]{1,0:T(1,128)S(1)} %get-tuple-element.14.taps_ref, bf16[2,48,384]{2,1,0:T(8,128)(2,1)S(1)} %collective-permute-done.2.refs_0_, bf16[2,48,384]{2,1,0:T(8,128)(2,1)S(1)} %collective-permute-done.3.refs_1_, ...), custom_call_target="tpu_custom_call" | custom-call | tf_op jit(solution)/shard_map/condition/pallas_call | solution.py:308
  18.5 4.5 %correlate.1 = bf16[1,8,40,40,256]{4,3,2,1,0:T(8,128)(2,1)} custom-call(bf16[640,256]{1,0:T(8,128)(2,1)S(1)} %get-tuple-element.21.partner_ref, f32[40,128]{1,0:T(8,128)S(1)} %get-tuple-element.22.reverse_ref), custom_call_target="tpu_custom_call" | custom-call | tf_op jit(solution)/shard_map/correlate/pallas_call | solution.py:399
Async XLA Ops:
  0.0 6.7 %collective-permute-start.1 = (bf16[48,1280]{1,0:T(8,128)(2,1)}, bf16[48,1280]{1,0:T(8,128)(2,1)S(1)}, u32[]{:S(2)}, u32[]{:S(2)}) collective-permute-start(bf16[48,1280]{1,0:T(8,128)(2,1)} %bitcast.6), channel_id=1, source_target_pairs={{0,4},{4,0},{8,12},{12,8},{16,20},{20,16},{24,28},{28,24},{1,5},{5... | collective-permute-start | bytes 368648 | tf_op jit(solution)/shard_map/ppermute | solution.py:419
  2.9 3.8 %collective-permute-start = (s32[160]{0:T(256)}, s32[160]{0:T(256)S(1)}, u32[]{:S(2)}, u32[]{:S(2)}) collective-permute-start(s32[160]{0:T(256)} %param.6), channel_id=1, source_target_pairs={{0,4},{4,0},{8,12},{12,8},{16,20},{20,16},{24,28},{28,24},{1,5},{5... | collective-permute-start | bytes 1928 | tf_op jit(solution)/shard_map/ppermute | solution.py:418
  7.8 7.0 %collective-permute-start.2 = (bf16[2,48,384]{2,1,0:T(8,128)(2,1)S(1)}, bf16[2,48,384]{2,1,0:T(8,128)(2,1)S(1)}, u32[]{:S(2)}, u32[]{:S(2)}) collective-permute-start(bf16[2,48,384]{2,1,0:T(8,128)(2,1)S(1)} %get-tuple-element.17), channel_id=1, source_target_pairs={{0,8},{4,12},{8,16},{12,20},{16,24},{20,28},{24,0},{28,4},{1,9},{5... | collective-permute-start | bytes 221192 | tf_op jit(solution)/shard_map/ppermute | solution.py:427
  9.4 7.3 %collective-permute-start.3 = (bf16[2,48,384]{2,1,0:T(8,128)(2,1)S(1)}, bf16[2,48,384]{2,1,0:T(8,128)(2,1)S(1)}, u32[]{:S(2)}, u32[]{:S(2)}) collective-permute-start(bf16[2,48,384]{2,1,0:T(8,128)(2,1)S(1)} %get-tuple-element.18), channel_id=1, source_target_pairs={{0,16},{4,20},{8,24},{12,28},{16,0},{20,4},{24,8},{28,12},{1,17},{... | collective-permute-start | bytes 221192 | tf_op jit(solution)/shard_map/ppermute | solution.py:427
  12.0 4.8 %collective-permute-start.4 = (bf16[2,48,384]{2,1,0:T(8,128)(2,1)S(1)}, bf16[2,48,384]{2,1,0:T(8,128)(2,1)S(1)}, u32[]{:S(2)}, u32[]{:S(2)}) collective-permute-start(bf16[2,48,384]{2,1,0:T(8,128)(2,1)S(1)} %get-tuple-element.19), channel_id=1, source_target_pairs={{0,24},{4,28},{8,0},{12,4},{16,8},{20,12},{24,16},{28,20},{1,25},{... | collective-permute-start | bytes 221192 | tf_op jit(solution)/shard_map/ppermute | solution.py:427

commit v4 on v2

--- a/solution.py
+++ b/solution.py
@@ -26,28 +26,37 @@
         copy.wait()
 
 
-def partner_of(group, step, groups):
-    if groups & (groups - 1) == 0:
-        return group ^ step
-    return (step + groups - group) % groups
-
-
-def rounds(groups):
-    even = list(range(groups - 1, 0, -1))
-    far = groups // 2
-    odd = [step for step in even if step < far] + [step for step in even if step >= far]
-    return list(zip(even, odd)) + [(0, 0)]
-
-
-def step_of(steps, member):
-    even, odd = steps
-    return even if even == odd else jnp.where(lax.rem(member, 2) == 0, even, odd)
+ROUTES = (
+    (2, 3, 5, 4, 7, 6, 1, 0),
+    (1, 0, 3, 2, 5, 4, 7, 6),
+    (3, 2, 4, 5, 6, 7, 0, 1),
+    (4, 5, 7, 6, 1, 0, 2, 3),
+    (6, 7, 1, 0, 2, 3, 4, 5),
+    (5, 4, 6, 7, 0, 1, 3, 2),
+    (7, 6, 0, 1, 3, 2, 5, 4),
+)
+
+
+def routes(groups):
+    if groups == len(ROUTES[0]):
+        return list(ROUTES) + [tuple(range(groups))]
+    return [tuple(group ^ step for group in range(groups)) for step in reversed(range(groups))]
+
+
+def inverse(route):
+    return tuple(route.index(group) for group in range(len(route)))
+
+
+def pick(route, group):
+    if len(route) > 8:
+        return group ^ route[0]
+    code = sum(target << (3 * index) for index, target in enumerate(route))
+    return (jnp.int32(code) >> (3 * group)) & 7
 
 
 def pack_kernel(rep_count, pairs_hbm, strain_hbm, widths_hbm, taps_hbm, *refs):
-    outs_hbm = refs[:-9]
-    taps_ref, stage_ref, sent = refs[-9:-6]
-    out_refs = [stage_ref.at[index] for index in range(len(outs_hbm))]
+    out_refs = refs[:-7]
+    taps_ref = refs[-7]
     pairs_ref, strain_ref, widths_ref, semaphores, blocks_ref, table_ref = refs[-6:]
     groups = len(out_refs)
     rows, packed = out_refs[0].shape
@@ -89,16 +98,17 @@
 
     lane = lax.broadcasted_iota(jnp.int32, (rows, LANES), 1)
     spare = LANES - 8
-    for steps, out_ref in zip(rounds(groups), out_refs):
-        group = partner_of(my_grp, step_of(steps, my_rep), groups)
+    for route, out_ref in zip(routes(groups), out_refs):
+        group = pick(route, my_grp)
         tile = group * rep_count + my_rep
         chosen = [tile]
         member, place_of = jnp.int32(0), jnp.int32(-1)
         for slot in range(listed):
             other = pairs_ref[slot, tile]
             chosen.append(jnp.maximum(other, 0))
-            inside = (other >= 0) & (lax.div(other, rep_count) == my_grp)
-            member = jnp.where(inside, lax.rem(other, rep_count), member)
+            among = other - my_grp * rep_count
+            inside = (among >= 0) & (among < rep_count)
+            member = jnp.where(inside, among, member)
             place_of = jnp.where(inside, slot + 1, place_of)
         own_at = jnp.where(group == my_grp, spare, -1)
         theirs = table_ref[member]
@@ -110,10 +120,10 @@
                 if index > listed:
                     continue
                 start = chosen[index] * TILE
-                source = lax.div(start, LANES)
-                offset = lax.rem(start, LANES)
+                source = start >> 7
+                offset = start & (LANES - 1)
                 both = jnp.where(lane >= offset, blocks_ref[source], blocks_ref[source + 1])
-                shift = lax.rem(place * TILE + LANES - offset, LANES)
+                shift = (place * TILE - offset) & (LANES - 1)
                 moved = pltpu.roll(both, shift, 1)
                 here = (lane >= place * TILE) & (lane < (place + 1) * TILE)
                 total = jnp.where(here, moved, total)
@@ -124,14 +134,6 @@
             if block == 0:
                 total = jnp.where(lane == own_at, mine, total)
             out_ref[:, block * LANES : (block + 1) * LANES] = total.astype(jnp.bfloat16)
-    copies = [
-        pltpu.make_async_copy(stage_ref.at[index], out_hbm, sent.at[index])
-        for index, out_hbm in enumerate(outs_hbm)
-    ]
-    for copy in copies:
-        copy.start()
-    for copy in copies:
-        copy.wait()
 
 
 def pack(strain, fir_taps, half_widths, pairs, groups, rep_count):
@@ -144,13 +146,11 @@
     vmem = pl.BlockSpec(memory_space=pltpu.VMEM)
     return pl.pallas_call(
         functools.partial(pack_kernel, rep_count),
-        out_shape=[pltpu.HBM((rows, packed), jnp.bfloat16)] * groups
+        out_shape=[jax.ShapeDtypeStruct((rows, packed), jnp.bfloat16)] * groups
         + [jax.ShapeDtypeStruct((1, fir_taps.shape[0]), jnp.float32)],
         in_specs=[hbm] * 4,
-        out_specs=[hbm] * groups + [vmem],
+        out_specs=[vmem] * (groups + 1),
         scratch_shapes=[
-            pltpu.VMEM((groups, rows, packed), jnp.bfloat16),
-            pltpu.SemaphoreType.DMA((groups,)),
             pltpu.SMEM((listed, tiles), jnp.int32),
             pltpu.VMEM((filled, channels), jnp.bfloat16),
             pltpu.VMEM((1, members), jnp.int32),
@@ -250,57 +250,28 @@
             white_ref[slot * TILE : (slot + 1) * TILE, block * LANES : (block + 1) * LANES] = value
 
 
-def condition_kernel(period, taps_ref, *refs):
-    received = refs[:-4]
-    partner_ref, reverse_ref, raw_ref, white_ref = refs[-4:]
+def correlate_kernel(period, taps_ref, *refs):
+    received = refs[:-11]
+    out_hbm, raw_ref, white_ref, partner_ref, reverse_ref = refs[-11:-6]
+    low_even, high_even, low_odd, high_odd, packed_ref, semaphores = refs[-6:]
     groups = len(received)
     my_grp = lax.axis_index("grp")
-    my_rep = lax.axis_index("rep")
-    for steps, ref in zip(rounds(groups), received):
-        raw_ref[partner_of(my_grp, step_of(steps, my_rep), groups)] = ref[...]
+    for route, ref in zip(routes(groups), received):
+        raw_ref[pick(inverse(route), my_grp)] = ref[...]
     condition(period, raw_ref, taps_ref, white_ref)
 
-    partner = white_ref[TILE:, :].astype(jnp.bfloat16)
-    rows = partner.shape[0]
-    partner_ref[:rows] = partner[:, : 2 * LANES]
-    partner_ref[rows:] = partner[:, LANES:]
     own = white_ref[:TILE, :LANES].astype(jnp.bfloat16)
     row = lax.broadcasted_iota(jnp.int32, (LANES, LANES), 0)
     col = lax.broadcasted_iota(jnp.int32, (LANES, LANES), 1)
     flip = jnp.where(row + col == LANES - 1, 1.0, 0.0).astype(jnp.bfloat16)
     reverse_ref[...] = dot(own, flip)
-
-
-def conditioned(received, taps, period, listed):
-    groups = len(received)
-    rows, packed = received[0].shape
-    vmem = pl.BlockSpec(memory_space=pltpu.VMEM)
-    return pl.pallas_call(
-        functools.partial(condition_kernel, period),
-        out_shape=[
-            jax.ShapeDtypeStruct((2 * listed * TILE, 2 * LANES), jnp.bfloat16),
-            jax.ShapeDtypeStruct((TILE, LANES), jnp.float32),
-        ],
-        in_specs=[vmem] * (groups + 1),
-        out_specs=[vmem, vmem],
-        scratch_shapes=[
-            pltpu.VMEM((groups, rows, packed), jnp.bfloat16),
-            pltpu.VMEM(((listed + 1) * TILE, groups * period), jnp.float32),
-        ],
-        compiler_params=pltpu.CompilerParams(vmem_limit_bytes=32 * 2**20),
-        name="condition",
-    )(taps, *received)
-
-
-def correlate_kernel(
-    partner_ref, reverse_ref, out_hbm, low_even, high_even, low_odd, high_odd, packed_ref, semaphores
-):
-    listed = out_hbm.shape[1]
-    rows = listed * TILE
+    partner = white_ref[TILE:, :].astype(jnp.bfloat16)
+    rows = partner.shape[0]
+    partner_ref[:rows] = partner[:, : 2 * LANES]
+    partner_ref[rows:] = partner[:, LANES:]
+    listed = rows // TILE
     normalizer = 1.0 / math.sqrt(LANES)
-    keep = lax.broadcasted_iota(jnp.int32, (LANES, LANES), 1) <= lax.broadcasted_iota(
-        jnp.int32, (LANES, LANES), 0
-    )
+    keep = col <= row
     even, odd = (low_even, high_even), (low_odd, high_odd)
     count = TILE // 8
     parts = 4
@@ -342,7 +313,6 @@
         for part in range(parts):
             multiply(group, part, held)
             convert(group - 1, part, before)
-        for part in range(parts):
             outgoing(group - 1, part).start()
 
     for part in range(parts):
@@ -362,23 +332,30 @@
             outgoing(group, part).wait()
 
 
-def correlate(partner, reverse):
-    rows = partner.shape[0] // 2
-    listed = rows // TILE
+def correlate(received, taps, period, listed):
+    groups = len(received)
+    rows, packed = received[0].shape
+    lines = listed * TILE
     vmem = pl.BlockSpec(memory_space=pltpu.VMEM)
     return pl.pallas_call(
-        correlate_kernel,
+        functools.partial(correlate_kernel, period),
         out_shape=jax.ShapeDtypeStruct((1, listed, TILE, TILE, LAGS), jnp.bfloat16),
-        in_specs=[vmem, vmem],
+        in_specs=[vmem] * (groups + 1),
         out_specs=pl.BlockSpec(memory_space=pltpu.HBM),
-        scratch_shapes=[pltpu.VMEM((rows * STRIDE, LANES), jnp.float32)] * 4
+        scratch_shapes=[
+            pltpu.VMEM((groups, rows, packed), jnp.bfloat16),
+            pltpu.VMEM(((listed + 1) * TILE, groups * period), jnp.float32),
+            pltpu.VMEM((2 * lines, 2 * LANES), jnp.bfloat16),
+            pltpu.VMEM((TILE, LANES), jnp.float32),
+        ]
+        + [pltpu.VMEM((lines * STRIDE, LANES), jnp.float32)] * 4
         + [
             pltpu.VMEM((TILE // 8, listed, TILE, 8, LAGS), jnp.bfloat16),
             pltpu.SemaphoreType.DMA((TILE // 8, 4)),
         ],
         compiler_params=pltpu.CompilerParams(vmem_limit_bytes=40 * 2**20),
         name="correlate",
-    )(partner, reverse)
+    )(taps, *received)
 
 
 def on_device(strain, fir_taps, half_widths, pairs):
@@ -386,21 +363,11 @@
     rep_count = lax.axis_size("rep")
     *messages, taps = pack(strain, fir_taps, half_widths, pairs, groups, rep_count)
     received = []
-    for steps, message in zip(rounds(groups), messages):
-        if steps == (0, 0):
-            received.append(message)
-            continue
-        route = [
-            (
-                group * rep_count + member,
-                partner_of(group, steps[member % 2], groups) * rep_count + member,
-            )
-            for group in range(groups)
-            for member in range(rep_count)
-        ]
-        received.append(lax.ppermute(message, ("grp", "rep"), route))
-    partner, reverse = conditioned(received, taps, strain.shape[1], pairs.shape[1])
-    return correlate(partner, reverse)
+    for route, message in zip(routes(groups), messages):
+        if route != tuple(range(groups)):
+            message = lax.ppermute(message, "grp", list(enumerate(route)))
+        received.append(message)
+    return correlate(received, taps, strain.shape[1], pairs.shape[1])
 
 
 def solution(mesh):

time: 25.8 us -> 22.8 us (0.88)
  waiting for transfers between devices: 3.74 us -> 1.89 us
  Pallas kernels: 8.54 us -> 7.15 us
  starting transfers between devices: 12.5 us -> 13.6 us
  local copies, waits for them, and re-layouts: 0.77 us -> 0 us
    ppermute x7, waiting for transfers between devices: 3.74 us -> 1.89 us  [on_device(): message = lax.ppermute(message, 'grp', list(enumerate(route)))]
    pallas_call x3 -> x2, Pallas kernels: 8.54 us -> 7.15 us  [the longest x1 5.73 us: correlate(): pl.pallas_call(functools.partial(correlate_kernel, period), out_shape=jax...]
    ppermute x7, starting transfers between devices: 12.5 us -> 13.6 us  [on_device(): message = lax.ppermute(message, 'grp', list(enumerate(route)))]
    unnamed x2 -> x0, local copies, waits for them, and re-layouts: 0.77 us -> none
  transfers between devices with their start and end apart: 7 -> 7, of which waited for: 5 -> 3; matrix products, arithmetic and copies ran while one was open for 0% -> 0% of each run, Pallas kernels for 0% -> 0%
where the time goes in v4:
time: 22.8 us; the launch traced here: 22.6 us
  starting transfers between devices  13.6 us (60%)
  Pallas kernels  7.15 us (31%)
  waiting for transfers between devices  1.89 us (8%)
    ppermute x7, starting transfers between devices, on_device(): message = lax.ppermute(message, 'grp', list(enumerate(route)))  13.6 us
    pallas_call x1, Pallas kernels, correlate(): pl.pallas_call(functools.partial(correlate_kernel, period), out_shape=jax...  5.73 us
    ppermute x7, waiting for transfers between devices, on_device(): message = lax.ppermute(message, 'grp', list(enumerate(route)))  1.89 us
    pallas_call x1, Pallas kernels, pack(): pl.pallas_call(functools.partial(pack_kernel, rep_count), out_shape=[jax....  1.42 us
  transfers between devices with their start and end apart: 7, of which 3 were waited for; matrix products, arithmetic and copies ran while one was open for 0% of the time, Pallas kernels for 0%

profile of v4, /device:TPU:0, one launch (start us, length us, event | category | flops | bytes accessed | tf_op | source)
XLA Modules:
  0.0 22.6 jit_solution(14634952284865602286)
XLA Ops:
  0.0 1.4 %pack.1 = (bf16[48,384]{1,0:T(8,128)(2,1)S(1)}, bf16[48,384]{1,0:T(8,128)(2,1)S(1)}, bf16[48,384]{1,0:T(8,128)(2,1)S(1)}, bf16[48,384]{1,0:T(8,128)(2,1)S(1)}, b...) custom-call(s32[8,32]{1,0:T(8,128)} %bitcast.5, ...), custom_call_target="tpu_custom_call" | custom-call | tf_op jit(solution)/shard_map/pack/pallas_call | solution.py:147
  1.4 3.1 %collective-permute-start = (bf16[48,384]{1,0:T(8,128)(2,1)S(1)}, bf16[48,384]{1,0:T(8,128)(2,1)S(1)}, u32[]{:S(2)}, u32[]{:S(2)}) collective-permute-start(bf16[48,384]{1,0:T(8,128)(2,1)S(1)} %get-tuple-element.15), channel_id=1, source_target_pairs={{0,8},{4,12},{8,20},{12,16},{16,28},{20,24},{24,4},{28,0},{1,9},{5... | collective-permute-start | bytes 110600 | tf_op jit(solution)/shard_map/ppermute | solution.py:368
  4.5 1.5 %collective-permute-start.1 = (bf16[48,384]{1,0:T(8,128)(2,1)S(1)}, bf16[48,384]{1,0:T(8,128)(2,1)S(1)}, u32[]{:S(2)}, u32[]{:S(2)}) collective-permute-start(bf16[48,384]{1,0:T(8,128)(2,1)S(1)} %get-tuple-element.16), channel_id=1, source_target_pairs={{0,4},{4,0},{8,12},{12,8},{16,20},{20,16},{24,28},{28,24},{1,5},{5... | collective-permute-start | bytes 110600 | tf_op jit(solution)/shard_map/ppermute | solution.py:368
  6.0 2.5 %collective-permute-start.2 = (bf16[48,384]{1,0:T(8,128)(2,1)S(1)}, bf16[48,384]{1,0:T(8,128)(2,1)S(1)}, u32[]{:S(2)}, u32[]{:S(2)}) collective-permute-start(bf16[48,384]{1,0:T(8,128)(2,1)S(1)} %get-tuple-element.17), channel_id=1, source_target_pairs={{0,12},{4,8},{8,16},{12,20},{16,24},{20,28},{24,0},{28,4},{1,13},{... | collective-permute-start | bytes 110600 | tf_op jit(solution)/shard_map/ppermute | solution.py:368
  8.5 0.2 collective-permute-start.3
  8.7 2.8 %collective-permute-start.4 = (bf16[48,384]{1,0:T(8,128)(2,1)S(1)}, bf16[48,384]{1,0:T(8,128)(2,1)S(1)}, u32[]{:S(2)}, u32[]{:S(2)}) collective-permute-start(bf16[48,384]{1,0:T(8,128)(2,1)S(1)} %get-tuple-element.19), channel_id=1, source_target_pairs={{0,24},{4,28},{8,4},{12,0},{16,8},{20,12},{24,16},{28,20},{1,25},{... | collective-permute-start | bytes 110600 | tf_op jit(solution)/shard_map/ppermute | solution.py:368
  11.5 0.0 collective-permute-done.refs_0_
  11.5 1.3 %collective-permute-start.5 = (bf16[48,384]{1,0:T(8,128)(2,1)S(1)}, bf16[48,384]{1,0:T(8,128)(2,1)S(1)}, u32[]{:S(2)}, u32[]{:S(2)}) collective-permute-start(bf16[48,384]{1,0:T(8,128)(2,1)S(1)} %get-tuple-element.20), channel_id=1, source_target_pairs={{0,20},{4,16},{8,24},{12,28},{16,0},{20,4},{24,12},{28,8},{1,21},{... | collective-permute-start | bytes 110600 | tf_op jit(solution)/shard_map/ppermute | solution.py:368
  12.8 0.0 collective-permute-done.1.refs_1_
  12.8 2.2 %collective-permute-start.6 = (bf16[48,384]{1,0:T(8,128)(2,1)S(1)}, bf16[48,384]{1,0:T(8,128)(2,1)S(1)}, u32[]{:S(2)}, u32[]{:S(2)}) collective-permute-start(bf16[48,384]{1,0:T(8,128)(2,1)S(1)} %get-tuple-element.21), channel_id=1, source_target_pairs={{0,28},{4,24},{8,0},{12,4},{16,12},{20,8},{24,20},{28,16},{1,29},{... | collective-permute-start | bytes 110600 | tf_op jit(solution)/shard_map/ppermute | solution.py:368
  15.0 0.0 collective-permute-done.2.refs_2_
  15.0 0.2 collective-permute-done.3.refs_3_
  15.2 0.0 collective-permute-done.4.refs_4_
  15.2 1.3 %collective-permute-done.5.refs_5_ = bf16[48,384]{1,0:T(8,128)(2,1)S(1)} collective-permute-done((bf16[48,384]{1,0:T(8,128)(2,1)S(1)}, bf16[48,384]{1,0:T(8,128)(2,1)S(1)}, u32[]{:S(2)}, u32[]{:S(2)}) %collective-permute-start.5) | collective-permute-done | bytes 36896 | tf_op jit(solution)/shard_map/ppermute | solution.py:368
  16.5 0.4 %collective-permute-done.6.refs_6_ = bf16[48,384]{1,0:T(8,128)(2,1)S(1)} collective-permute-done((bf16[48,384]{1,0:T(8,128)(2,1)S(1)}, bf16[48,384]{1,0:T(8,128)(2,1)S(1)}, u32[]{:S(2)}, u32[]{:S(2)}) %collective-permute-start.6) | collective-permute-done | bytes 36896 | tf_op jit(solution)/shard_map/ppermute | solution.py:368
  16.9 5.7 %correlate.1 = bf16[1,8,40,40,256]{4,3,2,1,0:T(8,128)(2,1)} custom-call(f32[1,64]{1,0:T(1,128)S(1)} %get-tuple-element.14.taps_ref, bf16[48,384]{1,0:T(8,128)(2,1)S(1)} %collective-permute-done.refs_0_, bf16[48,384]{1,0:T(8,128)(2,1)S(1)} %collective-permute-done.1.refs_1_, bf16[48,384]{1,0:T(8,128)(2,1)S(1)} %collective-permute-done.2.refs_2_, ...), custom_call_target="tpu_custom_call" | custom-call | tf_op jit(solution)/shard_map/correlate/pallas_call | solution.py:340
Async XLA Ops:
  1.4 10.1 %collective-permute-start = (bf16[48,384]{1,0:T(8,128)(2,1)S(1)}, bf16[48,384]{1,0:T(8,128)(2,1)S(1)}, u32[]{:S(2)}, u32[]{:S(2)}) collective-permute-start(bf16[48,384]{1,0:T(8,128)(2,1)S(1)} %get-tuple-element.15), channel_id=1, source_target_pairs={{0,8},{4,12},{8,20},{12,16},{16,28},{20,24},{24,4},{28,0},{1,9},{5... | collective-permute-start | bytes 110600 | tf_op jit(solution)/shard_map/ppermute | solution.py:368
  4.5 8.2 %collective-permute-start.1 = (bf16[48,384]{1,0:T(8,128)(2,1)S(1)}, bf16[48,384]{1,0:T(8,128)(2,1)S(1)}, u32[]{:S(2)}, u32[]{:S(2)}) collective-permute-start(bf16[48,384]{1,0:T(8,128)(2,1)S(1)} %get-tuple-element.16), channel_id=1, source_target_pairs={{0,4},{4,0},{8,12},{12,8},{16,20},{20,16},{24,28},{28,24},{1,5},{5... | collective-permute-start | bytes 110600 | tf_op jit(solution)/shard_map/ppermute | solution.py:368
  6.0 9.0 %collective-permute-start.2 = (bf16[48,384]{1,0:T(8,128)(2,1)S(1)}, bf16[48,384]{1,0:T(8,128)(2,1)S(1)}, u32[]{:S(2)}, u32[]{:S(2)}) collective-permute-start(bf16[48,384]{1,0:T(8,128)(2,1)S(1)} %get-tuple-element.17), channel_id=1, source_target_pairs={{0,12},{4,8},{8,16},{12,20},{16,24},{20,28},{24,0},{28,4},{1,13},{... | collective-permute-start | bytes 110600 | tf_op jit(solution)/shard_map/ppermute | solution.py:368
  8.5 6.7 %collective-permute-start.3 = (bf16[48,384]{1,0:T(8,128)(2,1)S(1)}, bf16[48,384]{1,0:T(8,128)(2,1)S(1)}, u32[]{:S(2)}, u32[]{:S(2)}) collective-permute-start(bf16[48,384]{1,0:T(8,128)(2,1)S(1)} %get-tuple-element.18), channel_id=1, source_target_pairs={{0,16},{4,20},{8,28},{12,24},{16,4},{20,0},{24,8},{28,12},{1,17},{... | collective-permute-start | bytes 110600 | tf_op jit(solution)/shard_map/ppermute | solution.py:368
  8.7 6.5 %collective-permute-start.4 = (bf16[48,384]{1,0:T(8,128)(2,1)S(1)}, bf16[48,384]{1,0:T(8,128)(2,1)S(1)}, u32[]{:S(2)}, u32[]{:S(2)}) collective-permute-start(bf16[48,384]{1,0:T(8,128)(2,1)S(1)} %get-tuple-element.19), channel_id=1, source_target_pairs={{0,24},{4,28},{8,4},{12,0},{16,8},{20,12},{24,16},{28,20},{1,25},{... | collective-permute-start | bytes 110600 | tf_op jit(solution)/shard_map/ppermute | solution.py:368
  11.5 5.0 %collective-permute-start.5 = (bf16[48,384]{1,0:T(8,128)(2,1)S(1)}, bf16[48,384]{1,0:T(8,128)(2,1)S(1)}, u32[]{:S(2)}, u32[]{:S(2)}) collective-permute-start(bf16[48,384]{1,0:T(8,128)(2,1)S(1)} %get-tuple-element.20), channel_id=1, source_target_pairs={{0,20},{4,16},{8,24},{12,28},{16,0},{20,4},{24,12},{28,8},{1,21},{... | collective-permute-start | bytes 110600 | tf_op jit(solution)/shard_map/ppermute | solution.py:368
  12.8 4.1 %collective-permute-start.6 = (bf16[48,384]{1,0:T(8,128)(2,1)S(1)}, bf16[48,384]{1,0:T(8,128)(2,1)S(1)}, u32[]{:S(2)}, u32[]{:S(2)}) collective-permute-start(bf16[48,384]{1,0:T(8,128)(2,1)S(1)} %get-tuple-element.21), channel_id=1, source_target_pairs={{0,28},{4,24},{8,0},{12,4},{16,12},{20,8},{24,20},{28,16},{1,29},{... | collective-permute-start | bytes 110600 | tf_op jit(solution)/shard_map/ppermute | solution.py:368

commit v5 on v4

--- a/solution.py
+++ b/solution.py
@@ -27,20 +27,22 @@
 
 
 ROUTES = (
-    (2, 3, 5, 4, 7, 6, 1, 0),
-    (1, 0, 3, 2, 5, 4, 7, 6),
-    (3, 2, 4, 5, 6, 7, 0, 1),
-    (4, 5, 7, 6, 1, 0, 2, 3),
-    (6, 7, 1, 0, 2, 3, 4, 5),
-    (5, 4, 6, 7, 0, 1, 3, 2),
-    (7, 6, 0, 1, 3, 2, 5, 4),
+    (6, 5, 4, 7, 1, 2, 3, 0),
+    (3, 2, 1, 0, 5, 4, 7, 6),
+    (1, 6, 7, 2, 0, 3, 5, 4),
+    (7, 4, 5, 6, 2, 1, 0, 3),
+    (2, 7, 6, 1, 3, 0, 4, 5),
+    (4, 0, 3, 5, 7, 6, 1, 2),
+    (5, 3, 0, 4, 6, 7, 2, 1),
 )
 
 
 def routes(groups):
     if groups == len(ROUTES[0]):
-        return list(ROUTES) + [tuple(range(groups))]
-    return [tuple(group ^ step for group in range(groups)) for step in reversed(range(groups))]
+        found = list(ROUTES)
+    else:
+        found = [tuple(group ^ step for group in range(groups)) for step in reversed(range(1, groups))]
+    return found[:1] + found + [tuple(range(groups))]
 
 
 def inverse(route):
@@ -58,7 +60,7 @@
     out_refs = refs[:-7]
     taps_ref = refs[-7]
     pairs_ref, strain_ref, widths_ref, semaphores, blocks_ref, table_ref = refs[-6:]
-    groups = len(out_refs)
+    groups = len(out_refs) - 1
     rows, packed = out_refs[0].shape
     listed = pairs_ref.shape[0]
     channels = strain_ref.shape[1]
@@ -98,9 +100,9 @@
 
     lane = lax.broadcasted_iota(jnp.int32, (rows, LANES), 1)
     spare = LANES - 8
-    for route, out_ref in zip(routes(groups), out_refs):
+    for index, (route, out_ref) in enumerate(zip(routes(groups), out_refs)):
         group = pick(route, my_grp)
-        tile = group * rep_count + my_rep
+        tile = group * rep_count + (my_rep & ~1 if index == 1 else my_rep)
         chosen = [tile]
         member, place_of = jnp.int32(0), jnp.int32(-1)
         for slot in range(listed):
@@ -146,10 +148,10 @@
     vmem = pl.BlockSpec(memory_space=pltpu.VMEM)
     return pl.pallas_call(
         functools.partial(pack_kernel, rep_count),
-        out_shape=[jax.ShapeDtypeStruct((rows, packed), jnp.bfloat16)] * groups
+        out_shape=[jax.ShapeDtypeStruct((rows, packed), jnp.bfloat16)] * (groups + 1)
         + [jax.ShapeDtypeStruct((1, fir_taps.shape[0]), jnp.float32)],
         in_specs=[hbm] * 4,
-        out_specs=[vmem] * (groups + 1),
+        out_specs=[vmem] * (groups + 2),
         scratch_shapes=[
             pltpu.SMEM((listed, tiles), jnp.int32),
             pltpu.VMEM((filled, channels), jnp.bfloat16),
@@ -254,10 +256,16 @@
     received = refs[:-11]
     out_hbm, raw_ref, white_ref, partner_ref, reverse_ref = refs[-11:-6]
     low_even, high_even, low_odd, high_odd, packed_ref, semaphores = refs[-6:]
-    groups = len(received)
+    groups = len(received) - 1
     my_grp = lax.axis_index("grp")
-    for route, ref in zip(routes(groups), received):
-        raw_ref[pick(inverse(route), my_grp)] = ref[...]
+    odd_member = lax.rem(lax.axis_index("rep"), 2) == 1
+    for index, (route, ref) in enumerate(zip(routes(groups), received)):
+        if index == 0:
+            continue
+        value = ref[...]
+        if index == 1:
+            value = jnp.where(odd_member, received[0][...], value)
+        raw_ref[pick(inverse(route), my_grp)] = value
     condition(period, raw_ref, taps_ref, white_ref)
 
     own = white_ref[:TILE, :LANES].astype(jnp.bfloat16)
@@ -333,14 +341,14 @@
 
 
 def correlate(received, taps, period, listed):
-    groups = len(received)
+    groups = len(received) - 1
     rows, packed = received[0].shape
     lines = listed * TILE
     vmem = pl.BlockSpec(memory_space=pltpu.VMEM)
     return pl.pallas_call(
         functools.partial(correlate_kernel, period),
         out_shape=jax.ShapeDtypeStruct((1, listed, TILE, TILE, LAGS), jnp.bfloat16),
-        in_specs=[vmem] * (groups + 1),
+        in_specs=[vmem] * (len(received) + 1),
         out_specs=pl.BlockSpec(memory_space=pltpu.HBM),
         scratch_shapes=[
             pltpu.VMEM((groups, rows, packed), jnp.bfloat16),
@@ -363,9 +371,15 @@
     rep_count = lax.axis_size("rep")
     *messages, taps = pack(strain, fir_taps, half_widths, pairs, groups, rep_count)
     received = []
-    for route, message in zip(routes(groups), messages):
+    for index, (route, message) in enumerate(zip(routes(groups), messages)):
         if route != tuple(range(groups)):
-            message = lax.ppermute(message, "grp", list(enumerate(route)))
+            pairs_of = [
+                (group * rep_count + member, target * rep_count + member - (index == 1))
+                for group, target in enumerate(route)
+                for member in range(rep_count)
+                if index > 1 or member % 2
+            ]
+            message = lax.ppermute(message, ("grp", "rep"), pairs_of)
         received.append(message)
     return correlate(received, taps, strain.shape[1], pairs.shape[1])
 

time: 22.8 us -> 23.8 us (1.044)
  waiting for transfers between devices: 1.89 us -> 2.44 us
  starting transfers between devices: 13.6 us -> 14 us
    ppermute x7 -> x8, waiting for transfers between devices: 1.89 us -> 2.44 us  [on_device(): message = lax.ppermute(message, ('grp', 'rep'), pairs_of)]
    ppermute x7 -> x8, starting transfers between devices: 13.6 us -> 14 us  [on_device(): message = lax.ppermute(message, ('grp', 'rep'), pairs_of)]
  transfers between devices with their start and end apart: 7 -> 8, of which waited for: 3 -> 3; matrix products, arithmetic and copies ran while one was open for 0% -> 0% of each run, Pallas kernels for 0% -> 0%
where the time goes in v5:
time: 23.8 us; the launch traced here: 23.7 us
  starting transfers between devices  14 us (59%)
  Pallas kernels  7.22 us (30%)
  waiting for transfers between devices  2.44 us (10%)
    ppermute x8, starting transfers between devices, on_device(): message = lax.ppermute(message, ('grp', 'rep'), pairs_of)  14 us
    pallas_call x1, Pallas kernels, correlate(): pl.pallas_call(functools.partial(correlate_kernel, period), out_shape=jax...  5.75 us
    ppermute x8, waiting for transfers between devices, on_device(): message = lax.ppermute(message, ('grp', 'rep'), pairs_of)  2.44 us
    pallas_call x1, Pallas kernels, pack(): pl.pallas_call(functools.partial(pack_kernel, rep_count), out_shape=[jax....  1.47 us
  transfers between devices with their start and end apart: 8, of which 3 were waited for; matrix products, arithmetic and copies ran while one was open for 0% of the time, Pallas kernels for 0%

profile of v5, /device:TPU:0, one launch (start us, length us, event | category | flops | bytes accessed | tf_op | source)
XLA Modules:
  0.0 23.7 jit_solution(2781537343677210959)
XLA Ops:
  0.0 1.5 %pack.1 = (bf16[48,384]{1,0:T(8,128)(2,1)S(1)}, bf16[48,384]{1,0:T(8,128)(2,1)S(1)}, bf16[48,384]{1,0:T(8,128)(2,1)S(1)}, bf16[48,384]{1,0:T(8,128)(2,1)S(1)}, b...) custom-call(s32[8,32]{1,0:T(8,128)} %bitcast.5, ...), custom_call_target="tpu_custom_call" | custom-call | tf_op jit(solution)/shard_map/pack/pallas_call | solution.py:149
  1.5 0.7 %collective-permute-start = (bf16[48,384]{1,0:T(8,128)(2,1)S(1)}, bf16[48,384]{1,0:T(8,128)(2,1)S(1)}, u32[]{:S(2)}, u32[]{:S(2)}) collective-permute-start(bf16[48,384]{1,0:T(8,128)(2,1)S(1)} %get-tuple-element.16), channel_id=1, source_target_pairs={{1,25},{3,27},{5,21},{7,23},{9,17},{11,19},{13,29},{15,31},{17,5},... | collective-permute-start | bytes 110600 | tf_op jit(solution)/shard_map/ppermute | solution.py:382
  2.1 1.3 %collective-permute-start.1 = (bf16[48,384]{1,0:T(8,128)(2,1)S(1)}, bf16[48,384]{1,0:T(8,128)(2,1)S(1)}, u32[]{:S(2)}, u32[]{:S(2)}) collective-permute-start(bf16[48,384]{1,0:T(8,128)(2,1)S(1)} %get-tuple-element.17), channel_id=1, source_target_pairs={{1,24},{3,26},{5,20},{7,22},{9,16},{11,18},{13,28},{15,30},{17,4},... | collective-permute-start | bytes 110600 | tf_op jit(solution)/shard_map/ppermute | solution.py:382
  3.4 4.0 %collective-permute-start.2 = (bf16[48,384]{1,0:T(8,128)(2,1)S(1)}, bf16[48,384]{1,0:T(8,128)(2,1)S(1)}, u32[]{:S(2)}, u32[]{:S(2)}) collective-permute-start(bf16[48,384]{1,0:T(8,128)(2,1)S(1)} %get-tuple-element.18), channel_id=1, source_target_pairs={{0,12},{1,13},{2,14},{3,15},{4,8},{5,9},{6,10},{7,11},{8,4},{9,5},... | collective-permute-start | bytes 110600 | tf_op jit(solution)/shard_map/ppermute | solution.py:382
  7.5 0.5 %collective-permute-start.3 = (bf16[48,384]{1,0:T(8,128)(2,1)S(1)}, bf16[48,384]{1,0:T(8,128)(2,1)S(1)}, u32[]{:S(2)}, u32[]{:S(2)}) collective-permute-start(bf16[48,384]{1,0:T(8,128)(2,1)S(1)} %get-tuple-element.19), channel_id=1, source_target_pairs={{0,4},{1,5},{2,6},{3,7},{4,24},{5,25},{6,26},{7,27},{8,28},{9,29},... | collective-permute-start | bytes 110600 | tf_op jit(solution)/shard_map/ppermute | solution.py:382
  8.0 3.4 %collective-permute-start.4 = (bf16[48,384]{1,0:T(8,128)(2,1)S(1)}, bf16[48,384]{1,0:T(8,128)(2,1)S(1)}, u32[]{:S(2)}, u32[]{:S(2)}) collective-permute-start(bf16[48,384]{1,0:T(8,128)(2,1)S(1)} %get-tuple-element.20), channel_id=1, source_target_pairs={{0,28},{1,29},{2,30},{3,31},{4,16},{5,17},{6,18},{7,19},{8,20},{9,... | collective-permute-start | bytes 110600 | tf_op jit(solution)/shard_map/ppermute | solution.py:382
  11.4 0.0 collective-permute-done.refs_0_
  11.4 0.0 collective-permute-start.5
  11.4 0.3 %collective-permute-done.1.refs_1_ = bf16[48,384]{1,0:T(8,128)(2,1)S(1)} collective-permute-done((bf16[48,384]{1,0:T(8,128)(2,1)S(1)}, bf16[48,384]{1,0:T(8,128)(2,1)S(1)}, u32[]{:S(2)}, u32[]{:S(2)}) %collective-permute-start.1) | collective-permute-done | bytes 36896 | tf_op jit(solution)/shard_map/ppermute | solution.py:382
  11.7 1.7 %collective-permute-start.6 = (bf16[48,384]{1,0:T(8,128)(2,1)S(1)}, bf16[48,384]{1,0:T(8,128)(2,1)S(1)}, u32[]{:S(2)}, u32[]{:S(2)}) collective-permute-start(bf16[48,384]{1,0:T(8,128)(2,1)S(1)} %get-tuple-element.22), channel_id=1, source_target_pairs={{0,16},{1,17},{2,18},{3,19},{4,0},{5,1},{6,2},{7,3},{8,12},{9,13},... | collective-permute-start | bytes 110600 | tf_op jit(solution)/shard_map/ppermute | solution.py:382
  13.4 0.0 collective-permute-done.2.refs_2_
  13.4 2.4 %collective-permute-start.7 = (bf16[48,384]{1,0:T(8,128)(2,1)S(1)}, bf16[48,384]{1,0:T(8,128)(2,1)S(1)}, u32[]{:S(2)}, u32[]{:S(2)}) collective-permute-start(bf16[48,384]{1,0:T(8,128)(2,1)S(1)} %get-tuple-element.23), channel_id=1, source_target_pairs={{0,20},{1,21},{2,22},{3,23},{4,12},{5,13},{6,14},{7,15},{8,0},{9,1... | collective-permute-start | bytes 110600 | tf_op jit(solution)/shard_map/ppermute | solution.py:382
  15.8 0.0 collective-permute-done.3.refs_3_
  15.8 0.0 collective-permute-done.4.refs_4_
  15.8 1.4 %collective-permute-done.5.refs_5_ = bf16[48,384]{1,0:T(8,128)(2,1)S(1)} collective-permute-done((bf16[48,384]{1,0:T(8,128)(2,1)S(1)}, bf16[48,384]{1,0:T(8,128)(2,1)S(1)}, u32[]{:S(2)}, u32[]{:S(2)}) %collective-permute-start.5) | collective-permute-done | bytes 36896 | tf_op jit(solution)/shard_map/ppermute | solution.py:382
  17.2 0.0 collective-permute-done.6.refs_6_
  17.2 0.7 %collective-permute-done.7.refs_7_ = bf16[48,384]{1,0:T(8,128)(2,1)S(1)} collective-permute-done((bf16[48,384]{1,0:T(8,128)(2,1)S(1)}, bf16[48,384]{1,0:T(8,128)(2,1)S(1)}, u32[]{:S(2)}, u32[]{:S(2)}) %collective-permute-start.7) | collective-permute-done | bytes 36896 | tf_op jit(solution)/shard_map/ppermute | solution.py:382
  17.9 5.7 %correlate.1 = bf16[1,8,40,40,256]{4,3,2,1,0:T(8,128)(2,1)} custom-call(f32[1,64]{1,0:T(1,128)S(1)} %get-tuple-element.15.taps_ref, bf16[48,384]{1,0:T(8,128)(2,1)S(1)} %collective-permute-done.refs_0_, bf16[48,384]{1,0:T(8,128)(2,1)S(1)} %collective-permute-done.1.refs_1_, bf16[48,384]{1,0:T(8,128)(2,1)S(1)} %collective-permute-done.2.refs_2_, ...), custom_call_target="tpu_custom_call" | custom-call | tf_op jit(solution)/shard_map/correlate/pallas_call | solution.py:348
Async XLA Ops:
  1.5 9.9 %collective-permute-start = (bf16[48,384]{1,0:T(8,128)(2,1)S(1)}, bf16[48,384]{1,0:T(8,128)(2,1)S(1)}, u32[]{:S(2)}, u32[]{:S(2)}) collective-permute-start(bf16[48,384]{1,0:T(8,128)(2,1)S(1)} %get-tuple-element.16), channel_id=1, source_target_pairs={{1,25},{3,27},{5,21},{7,23},{9,17},{11,19},{13,29},{15,31},{17,5},... | collective-permute-start | bytes 110600 | tf_op jit(solution)/shard_map/ppermute | solution.py:382
  2.1 9.6 %collective-permute-start.1 = (bf16[48,384]{1,0:T(8,128)(2,1)S(1)}, bf16[48,384]{1,0:T(8,128)(2,1)S(1)}, u32[]{:S(2)}, u32[]{:S(2)}) collective-permute-start(bf16[48,384]{1,0:T(8,128)(2,1)S(1)} %get-tuple-element.17), channel_id=1, source_target_pairs={{1,24},{3,26},{5,20},{7,22},{9,16},{11,18},{13,28},{15,30},{17,4},... | collective-permute-start | bytes 110600 | tf_op jit(solution)/shard_map/ppermute | solution.py:382
  3.4 10.0 %collective-permute-start.2 = (bf16[48,384]{1,0:T(8,128)(2,1)S(1)}, bf16[48,384]{1,0:T(8,128)(2,1)S(1)}, u32[]{:S(2)}, u32[]{:S(2)}) collective-permute-start(bf16[48,384]{1,0:T(8,128)(2,1)S(1)} %get-tuple-element.18), channel_id=1, source_target_pairs={{0,12},{1,13},{2,14},{3,15},{4,8},{5,9},{6,10},{7,11},{8,4},{9,5},... | collective-permute-start | bytes 110600 | tf_op jit(solution)/shard_map/ppermute | solution.py:382
  7.5 8.3 %collective-permute-start.3 = (bf16[48,384]{1,0:T(8,128)(2,1)S(1)}, bf16[48,384]{1,0:T(8,128)(2,1)S(1)}, u32[]{:S(2)}, u32[]{:S(2)}) collective-permute-start(bf16[48,384]{1,0:T(8,128)(2,1)S(1)} %get-tuple-element.19), channel_id=1, source_target_pairs={{0,4},{1,5},{2,6},{3,7},{4,24},{5,25},{6,26},{7,27},{8,28},{9,29},... | collective-permute-start | bytes 110600 | tf_op jit(solution)/shard_map/ppermute | solution.py:382
  8.0 7.8 %collective-permute-start.4 = (bf16[48,384]{1,0:T(8,128)(2,1)S(1)}, bf16[48,384]{1,0:T(8,128)(2,1)S(1)}, u32[]{:S(2)}, u32[]{:S(2)}) collective-permute-start(bf16[48,384]{1,0:T(8,128)(2,1)S(1)} %get-tuple-element.20), channel_id=1, source_target_pairs={{0,28},{1,29},{2,30},{3,31},{4,16},{5,17},{6,18},{7,19},{8,20},{9,... | collective-permute-start | bytes 110600 | tf_op jit(solution)/shard_map/ppermute | solution.py:382
  11.4 5.8 %collective-permute-start.5 = (bf16[48,384]{1,0:T(8,128)(2,1)S(1)}, bf16[48,384]{1,0:T(8,128)(2,1)S(1)}, u32[]{:S(2)}, u32[]{:S(2)}) collective-permute-start(bf16[48,384]{1,0:T(8,128)(2,1)S(1)} %get-tuple-element.21), channel_id=1, source_target_pairs={{0,8},{1,9},{2,10},{3,11},{4,28},{5,29},{6,30},{7,31},{8,24},{9,25... | collective-permute-start | bytes 110600 | tf_op jit(solution)/shard_map/ppermute | solution.py:382
  11.7 5.5 %collective-permute-start.6 = (bf16[48,384]{1,0:T(8,128)(2,1)S(1)}, bf16[48,384]{1,0:T(8,128)(2,1)S(1)}, u32[]{:S(2)}, u32[]{:S(2)}) collective-permute-start(bf16[48,384]{1,0:T(8,128)(2,1)S(1)} %get-tuple-element.22), channel_id=1, source_target_pairs={{0,16},{1,17},{2,18},{3,19},{4,0},{5,1},{6,2},{7,3},{8,12},{9,13},... | collective-permute-start | bytes 110600 | tf_op jit(solution)/shard_map/ppermute | solution.py:382
  13.4 4.5 %collective-permute-start.7 = (bf16[48,384]{1,0:T(8,128)(2,1)S(1)}, bf16[48,384]{1,0:T(8,128)(2,1)S(1)}, u32[]{:S(2)}, u32[]{:S(2)}) collective-permute-start(bf16[48,384]{1,0:T(8,128)(2,1)S(1)} %get-tuple-element.23), channel_id=1, source_target_pairs={{0,20},{1,21},{2,22},{3,23},{4,12},{5,13},{6,14},{7,15},{8,0},{9,1... | collective-permute-start | bytes 110600 | tf_op jit(solution)/shard_map/ppermute | solution.py:382

commit v6 on v4

--- a/solution.py
+++ b/solution.py
@@ -27,20 +27,34 @@
 
 
 ROUTES = (
-    (2, 3, 5, 4, 7, 6, 1, 0),
-    (1, 0, 3, 2, 5, 4, 7, 6),
-    (3, 2, 4, 5, 6, 7, 0, 1),
-    (4, 5, 7, 6, 1, 0, 2, 3),
-    (6, 7, 1, 0, 2, 3, 4, 5),
-    (5, 4, 6, 7, 0, 1, 3, 2),
-    (7, 6, 0, 1, 3, 2, 5, 4),
+    ((3, 2, 5, 4, 7, 6, 1, 0), (2, 3, 4, 5, 6, 7, 0, 1), 0),
+    ((1, 0, 3, 2, 5, 4, 7, 6), (6, 7, 0, 1, 2, 3, 4, 5), 1),
+    ((7, 6, 1, 0, 3, 2, 5, 4), (4, 5, 6, 7, 0, 1, 2, 3), 0),
+    ((2, 3, 4, 5, 6, 7, 0, 1), (3, 2, 5, 4, 7, 6, 1, 0), 0),
+    ((5, 4, 7, 6, 1, 0, 3, 2), (5, 4, 7, 6, 1, 0, 3, 2), 0),
+    ((4, 5, 6, 7, 0, 1, 2, 3), (7, 6, 1, 0, 3, 2, 5, 4), 0),
+    ((1, 0, 3, 2, 5, 4, 7, 6), (6, 7, 0, 1, 2, 3, 4, 5), 0),
 )
 
 
-def routes(groups):
-    if groups == len(ROUTES[0]):
-        return list(ROUTES) + [tuple(range(groups))]
-    return [tuple(group ^ step for group in range(groups)) for step in reversed(range(groups))]
+def rounds(groups):
+    stay = tuple(range(groups))
+    if groups == len(ROUTES[0][0]):
+        return list(ROUTES) + [(stay, stay, 0)]
+    steps = [tuple(group ^ step for group in range(groups)) for step in reversed(range(groups))]
+    return [(route, route, 0) for route in steps]
+
+
+def goes_to(plan, group, member):
+    even, odd, _ = plan
+    if even == odd:
+        return pick(even, group)
+    return jnp.where(lax.rem(member, 2) == 0, pick(even, group), pick(odd, group))
+
+
+def comes_from(plan, group, member):
+    even, odd, crossed = plan
+    return goes_to((inverse(even), inverse(odd), 0), group, member ^ crossed)
 
 
 def inverse(route):
@@ -98,9 +112,9 @@
 
     lane = lax.broadcasted_iota(jnp.int32, (rows, LANES), 1)
     spare = LANES - 8
-    for route, out_ref in zip(routes(groups), out_refs):
-        group = pick(route, my_grp)
-        tile = group * rep_count + my_rep
+    for plan, out_ref in zip(rounds(groups), out_refs):
+        group = goes_to(plan, my_grp, my_rep)
+        tile = group * rep_count + (my_rep ^ plan[2])
         chosen = [tile]
         member, place_of = jnp.int32(0), jnp.int32(-1)
         for slot in range(listed):
@@ -180,8 +194,21 @@
     groups, rows, packed = raw_ref.shape
     listed = white_ref.shape[0] // TILE - 1
     blocks = packed // LANES
-    raw = raw_ref[:, :period, :].astype(jnp.float32).reshape(groups * period, packed)
-    samples = jnp.transpose(raw).astype(jnp.bfloat16)
+    raw = raw_ref[:, :period, :].reshape(groups * period, packed)
+    same = lax.broadcasted_iota(jnp.int32, (LANES, LANES), 0) == lax.broadcasted_iota(
+        jnp.int32, (LANES, LANES), 1
+    )
+    identity = jnp.where(same, 1.0, 0.0).astype(jnp.bfloat16)
+    turned = [
+        lax.dot_general(
+            identity,
+            raw[:, block * LANES : (block + 1) * LANES],
+            (((1,), (1,)), ((), ())),
+            preferred_element_type=jnp.float32,
+        ).astype(jnp.bfloat16)
+        for block in range(blocks)
+    ]
+    samples = jnp.concatenate(turned, axis=0)
     columns = []
     for block in range(blocks):
         piece = raw_ref[:, :TILE, block * LANES : (block + 1) * LANES].astype(jnp.float32)
@@ -256,8 +283,9 @@
     low_even, high_even, low_odd, high_odd, packed_ref, semaphores = refs[-6:]
     groups = len(received)
     my_grp = lax.axis_index("grp")
-    for route, ref in zip(routes(groups), received):
-        raw_ref[pick(inverse(route), my_grp)] = ref[...]
+    my_rep = lax.axis_index("rep")
+    for plan, ref in zip(rounds(groups), received):
+        raw_ref[comes_from(plan, my_grp, my_rep)] = ref[...]
     condition(period, raw_ref, taps_ref, white_ref)
 
     own = white_ref[:TILE, :LANES].astype(jnp.bfloat16)
@@ -363,9 +391,14 @@
     rep_count = lax.axis_size("rep")
     *messages, taps = pack(strain, fir_taps, half_widths, pairs, groups, rep_count)
     received = []
-    for route, message in zip(routes(groups), messages):
-        if route != tuple(range(groups)):
-            message = lax.ppermute(message, "grp", list(enumerate(route)))
+    for plan, message in zip(rounds(groups), messages):
+        if plan[0] != tuple(range(groups)):
+            way = [
+                (group * rep_count + member, plan[member % 2][group] * rep_count + (member ^ plan[2]))
+                for group in range(groups)
+                for member in range(rep_count)
+            ]
+            message = lax.ppermute(message, ("grp", "rep"), way)
         received.append(message)
     return correlate(received, taps, strain.shape[1], pairs.shape[1])
 

time: 22.8 us -> 22.1 us (0.969)
  starting transfers between devices: 13.6 us -> 10.6 us
  waiting for transfers between devices: 1.89 us -> 4.13 us
    ppermute x7, starting transfers between devices: 13.6 us -> 10.6 us  [on_device(): message = lax.ppermute(message, ('grp', 'rep'), way)]
    ppermute x7, waiting for transfers between devices: 1.89 us -> 4.13 us  [on_device(): message = lax.ppermute(message, ('grp', 'rep'), way)]
  transfers between devices with their start and end apart: 7 -> 7, of which waited for: 3 -> 2; matrix products, arithmetic and copies ran while one was open for 0% -> 0% of each run, Pallas kernels for 0% -> 0%
where the time goes in v6:
time: 22.1 us; the launch traced here: 22 us
  starting transfers between devices  10.6 us (48%)
  Pallas kernels  7.27 us (33%)
  waiting for transfers between devices  4.13 us (19%)
    ppermute x7, starting transfers between devices, on_device(): message = lax.ppermute(message, ('grp', 'rep'), way)  10.6 us
    pallas_call x1, Pallas kernels, correlate(): pl.pallas_call(functools.partial(correlate_kernel, period), out_shape=jax...  5.83 us
    ppermute x7, waiting for transfers between devices, on_device(): message = lax.ppermute(message, ('grp', 'rep'), way)  4.13 us
    pallas_call x1, Pallas kernels, pack(): pl.pallas_call(functools.partial(pack_kernel, rep_count), out_shape=[jax....  1.43 us
  transfers between devices with their start and end apart: 7, of which 2 were waited for; matrix products, arithmetic and copies ran while one was open for 0% of the time, Pallas kernels for 0%

profile of v6, /device:TPU:0, one launch (start us, length us, event | category | flops | bytes accessed | tf_op | source)
XLA Modules:
  0.0 22.0 jit_solution(7628046525377233407)
XLA Ops:
  0.0 1.4 %pack.1 = (bf16[48,384]{1,0:T(8,128)(2,1)S(1)}, bf16[48,384]{1,0:T(8,128)(2,1)S(1)}, bf16[48,384]{1,0:T(8,128)(2,1)S(1)}, bf16[48,384]{1,0:T(8,128)(2,1)S(1)}, b...) custom-call(s32[8,32]{1,0:T(8,128)} %bitcast.5, ...), custom_call_target="tpu_custom_call" | custom-call | tf_op jit(solution)/shard_map/pack/pallas_call | solution.py:161
  1.4 4.0 %collective-permute-start = (bf16[48,384]{1,0:T(8,128)(2,1)S(1)}, bf16[48,384]{1,0:T(8,128)(2,1)S(1)}, u32[]{:S(2)}, u32[]{:S(2)}) collective-permute-start(bf16[48,384]{1,0:T(8,128)(2,1)S(1)} %get-tuple-element.15), channel_id=1, source_target_pairs={{0,12},{1,9},{2,14},{3,11},{4,8},{5,13},{6,10},{7,15},{8,20},{9,17... | collective-permute-start | bytes 110600 | tf_op jit(solution)/shard_map/ppermute | solution.py:401
  5.4 0.0 collective-permute-start.1
  5.4 2.2 %collective-permute-start.2 = (bf16[48,384]{1,0:T(8,128)(2,1)S(1)}, bf16[48,384]{1,0:T(8,128)(2,1)S(1)}, u32[]{:S(2)}, u32[]{:S(2)}) collective-permute-start(bf16[48,384]{1,0:T(8,128)(2,1)S(1)} %get-tuple-element.17), channel_id=1, source_target_pairs={{0,28},{1,17},{2,30},{3,19},{4,24},{5,21},{6,26},{7,23},{8,4},{9,2... | collective-permute-start | bytes 110600 | tf_op jit(solution)/shard_map/ppermute | solution.py:401
  7.6 0.0 collective-permute-start.3
  7.6 3.4 %collective-permute-start.4 = (bf16[48,384]{1,0:T(8,128)(2,1)S(1)}, bf16[48,384]{1,0:T(8,128)(2,1)S(1)}, u32[]{:S(2)}, u32[]{:S(2)}) collective-permute-start(bf16[48,384]{1,0:T(8,128)(2,1)S(1)} %get-tuple-element.19), channel_id=1, source_target_pairs={{0,20},{1,21},{2,22},{3,23},{4,16},{5,17},{6,18},{7,19},{8,28},{9,... | collective-permute-start | bytes 110600 | tf_op jit(solution)/shard_map/ppermute | solution.py:401
  11.0 0.0 collective-permute-done.refs_0_
  11.0 0.6 %collective-permute-start.5 = (bf16[48,384]{1,0:T(8,128)(2,1)S(1)}, bf16[48,384]{1,0:T(8,128)(2,1)S(1)}, u32[]{:S(2)}, u32[]{:S(2)}) collective-permute-start(bf16[48,384]{1,0:T(8,128)(2,1)S(1)} %get-tuple-element.20), channel_id=1, source_target_pairs={{0,16},{1,29},{2,18},{3,31},{4,20},{5,25},{6,22},{7,27},{8,24},{9,... | collective-permute-start | bytes 110600 | tf_op jit(solution)/shard_map/ppermute | solution.py:401
  11.5 0.0 collective-permute-done.1.refs_1_
  11.5 0.5 %collective-permute-start.6 = (bf16[48,384]{1,0:T(8,128)(2,1)S(1)}, bf16[48,384]{1,0:T(8,128)(2,1)S(1)}, u32[]{:S(2)}, u32[]{:S(2)}) collective-permute-start(bf16[48,384]{1,0:T(8,128)(2,1)S(1)} %get-tuple-element.21), channel_id=1, source_target_pairs={{0,4},{1,25},{2,6},{3,27},{4,0},{5,29},{6,2},{7,31},{8,12},{9,1},{... | collective-permute-start | bytes 110600 | tf_op jit(solution)/shard_map/ppermute | solution.py:401
  12.0 0.0 collective-permute-done.2.refs_2_
  12.0 1.5 %collective-permute-done.3.refs_3_ = bf16[48,384]{1,0:T(8,128)(2,1)S(1)} collective-permute-done((bf16[48,384]{1,0:T(8,128)(2,1)S(1)}, bf16[48,384]{1,0:T(8,128)(2,1)S(1)}, u32[]{:S(2)}, u32[]{:S(2)}) %collective-permute-start.3) | collective-permute-done | bytes 36896 | tf_op jit(solution)/shard_map/ppermute | solution.py:401
  13.5 0.0 collective-permute-done.4.refs_4_
  13.5 2.6 %collective-permute-done.5.refs_5_ = bf16[48,384]{1,0:T(8,128)(2,1)S(1)} collective-permute-done((bf16[48,384]{1,0:T(8,128)(2,1)S(1)}, bf16[48,384]{1,0:T(8,128)(2,1)S(1)}, u32[]{:S(2)}, u32[]{:S(2)}) %collective-permute-start.5) | collective-permute-done | bytes 36896 | tf_op jit(solution)/shard_map/ppermute | solution.py:401
  16.1 0.0 collective-permute-done.6.refs_6_
  16.1 5.8 %correlate.1 = bf16[1,8,40,40,256]{4,3,2,1,0:T(8,128)(2,1)} custom-call(f32[1,64]{1,0:T(1,128)S(1)} %get-tuple-element.14.taps_ref, bf16[48,384]{1,0:T(8,128)(2,1)S(1)} %collective-permute-done.refs_0_, bf16[48,384]{1,0:T(8,128)(2,1)S(1)} %collective-permute-done.1.refs_1_, bf16[48,384]{1,0:T(8,128)(2,1)S(1)} %collective-permute-done.2.refs_2_, ...), custom_call_target="tpu_custom_call" | custom-call | tf_op jit(solution)/shard_map/correlate/pallas_call | solution.py:368
Async XLA Ops:
  1.4 9.5 %collective-permute-start = (bf16[48,384]{1,0:T(8,128)(2,1)S(1)}, bf16[48,384]{1,0:T(8,128)(2,1)S(1)}, u32[]{:S(2)}, u32[]{:S(2)}) collective-permute-start(bf16[48,384]{1,0:T(8,128)(2,1)S(1)} %get-tuple-element.15), channel_id=1, source_target_pairs={{0,12},{1,9},{2,14},{3,11},{4,8},{5,13},{6,10},{7,15},{8,20},{9,17... | collective-permute-start | bytes 110600 | tf_op jit(solution)/shard_map/ppermute | solution.py:401
  5.4 6.1 %collective-permute-start.1 = (bf16[48,384]{1,0:T(8,128)(2,1)S(1)}, bf16[48,384]{1,0:T(8,128)(2,1)S(1)}, u32[]{:S(2)}, u32[]{:S(2)}) collective-permute-start(bf16[48,384]{1,0:T(8,128)(2,1)S(1)} %get-tuple-element.16), channel_id=1, source_target_pairs={{0,5},{1,24},{2,7},{3,26},{4,1},{5,28},{6,3},{7,30},{8,13},{9,0},{... | collective-permute-start | bytes 110600 | tf_op jit(solution)/shard_map/ppermute | solution.py:401
  5.4 6.6 %collective-permute-start.2 = (bf16[48,384]{1,0:T(8,128)(2,1)S(1)}, bf16[48,384]{1,0:T(8,128)(2,1)S(1)}, u32[]{:S(2)}, u32[]{:S(2)}) collective-permute-start(bf16[48,384]{1,0:T(8,128)(2,1)S(1)} %get-tuple-element.17), channel_id=1, source_target_pairs={{0,28},{1,17},{2,30},{3,19},{4,24},{5,21},{6,26},{7,23},{8,4},{9,2... | collective-permute-start | bytes 110600 | tf_op jit(solution)/shard_map/ppermute | solution.py:401
  7.6 5.9 %collective-permute-start.3 = (bf16[48,384]{1,0:T(8,128)(2,1)S(1)}, bf16[48,384]{1,0:T(8,128)(2,1)S(1)}, u32[]{:S(2)}, u32[]{:S(2)}) collective-permute-start(bf16[48,384]{1,0:T(8,128)(2,1)S(1)} %get-tuple-element.18), channel_id=1, source_target_pairs={{0,8},{1,13},{2,10},{3,15},{4,12},{5,9},{6,14},{7,11},{8,16},{9,21... | collective-permute-start | bytes 110600 | tf_op jit(solution)/shard_map/ppermute | solution.py:401
  7.6 5.9 %collective-permute-start.4 = (bf16[48,384]{1,0:T(8,128)(2,1)S(1)}, bf16[48,384]{1,0:T(8,128)(2,1)S(1)}, u32[]{:S(2)}, u32[]{:S(2)}) collective-permute-start(bf16[48,384]{1,0:T(8,128)(2,1)S(1)} %get-tuple-element.19), channel_id=1, source_target_pairs={{0,20},{1,21},{2,22},{3,23},{4,16},{5,17},{6,18},{7,19},{8,28},{9,... | collective-permute-start | bytes 110600 | tf_op jit(solution)/shard_map/ppermute | solution.py:401
  11.0 5.2 %collective-permute-start.5 = (bf16[48,384]{1,0:T(8,128)(2,1)S(1)}, bf16[48,384]{1,0:T(8,128)(2,1)S(1)}, u32[]{:S(2)}, u32[]{:S(2)}) collective-permute-start(bf16[48,384]{1,0:T(8,128)(2,1)S(1)} %get-tuple-element.20), channel_id=1, source_target_pairs={{0,16},{1,29},{2,18},{3,31},{4,20},{5,25},{6,22},{7,27},{8,24},{9,... | collective-permute-start | bytes 110600 | tf_op jit(solution)/shard_map/ppermute | solution.py:401
  11.5 4.6 %collective-permute-start.6 = (bf16[48,384]{1,0:T(8,128)(2,1)S(1)}, bf16[48,384]{1,0:T(8,128)(2,1)S(1)}, u32[]{:S(2)}, u32[]{:S(2)}) collective-permute-start(bf16[48,384]{1,0:T(8,128)(2,1)S(1)} %get-tuple-element.21), channel_id=1, source_target_pairs={{0,4},{1,25},{2,6},{3,27},{4,0},{5,29},{6,2},{7,31},{8,12},{9,1},{... | collective-permute-start | bytes 110600 | tf_op jit(solution)/shard_map/ppermute | solution.py:401

commit v7 on v6

--- a/solution.py
+++ b/solution.py
@@ -194,21 +194,8 @@
     groups, rows, packed = raw_ref.shape
     listed = white_ref.shape[0] // TILE - 1
     blocks = packed // LANES
-    raw = raw_ref[:, :period, :].reshape(groups * period, packed)
-    same = lax.broadcasted_iota(jnp.int32, (LANES, LANES), 0) == lax.broadcasted_iota(
-        jnp.int32, (LANES, LANES), 1
-    )
-    identity = jnp.where(same, 1.0, 0.0).astype(jnp.bfloat16)
-    turned = [
-        lax.dot_general(
-            identity,
-            raw[:, block * LANES : (block + 1) * LANES],
-            (((1,), (1,)), ((), ())),
-            preferred_element_type=jnp.float32,
-        ).astype(jnp.bfloat16)
-        for block in range(blocks)
-    ]
-    samples = jnp.concatenate(turned, axis=0)
+    raw = raw_ref[:, :period, :].astype(jnp.float32).reshape(groups * period, packed)
+    samples = jnp.transpose(raw).astype(jnp.bfloat16)
     columns = []
     for block in range(blocks):
         piece = raw_ref[:, :TILE, block * LANES : (block + 1) * LANES].astype(jnp.float32)
@@ -320,13 +307,15 @@
             semaphores.at[group, part],
         )
 
+    wide = 4
+
     def multiply(group, part, held):
-        channel = group * 8 + 2 * part
-        weights = jnp.concatenate([band(channel), band(channel + 1)], axis=1)
+        channel = group * 8 + wide * part
+        weights = jnp.concatenate([band(channel + side) for side in range(wide)], axis=1)
         product = dot(partner_ref[...], weights) * normalizer
         for half, ref in enumerate(held):
-            for side in range(2):
-                ref[pl.ds(2 * part + side, rows, stride=STRIDE), :] = product[
+            for side in range(wide):
+                ref[pl.ds(wide * part + side, rows, stride=STRIDE), :] = product[
                     half * rows : (half + 1) * rows, side * LANES : (side + 1) * LANES
                 ]
 
@@ -339,11 +328,12 @@
 
     def together(group, held, before):
         for part in range(parts):
-            multiply(group, part, held)
+            if part % 2 == 0:
+                multiply(group, part // 2, held)
             convert(group - 1, part, before)
             outgoing(group - 1, part).start()
 
-    for part in range(parts):
+    for part in range(8 // wide):
         multiply(0, part, even)
 
     def two_groups(index, carry):

time: 22.1 us -> 22 us (level)
  no operation moved by 1% of the time
where the time goes in v7:
time: 22 us; the launch traced here: 21.8 us
  starting transfers between devices  10.6 us (48%)
  Pallas kernels  7.15 us (32%)
  waiting for transfers between devices  4.13 us (19%)
    ppermute x7, starting transfers between devices, on_device(): message = lax.ppermute(message, ('grp', 'rep'), way)  10.6 us
    pallas_call x1, Pallas kernels, correlate(): pl.pallas_call(functools.partial(correlate_kernel, period), out_shape=jax...  5.71 us
    ppermute x7, waiting for transfers between devices, on_device(): message = lax.ppermute(message, ('grp', 'rep'), way)  4.13 us
    pallas_call x1, Pallas kernels, pack(): pl.pallas_call(functools.partial(pack_kernel, rep_count), out_shape=[jax....  1.43 us
  transfers between devices with their start and end apart: 7, of which 2 were waited for; matrix products, arithmetic and copies ran while one was open for 0% of the time, Pallas kernels for 0%

profile of v7, /device:TPU:0, one launch (start us, length us, event | category | flops | bytes accessed | tf_op | source)
XLA Modules:
  0.0 21.8 jit_solution(15245064307328043151)
XLA Ops:
  0.0 1.4 %pack.1 = (bf16[48,384]{1,0:T(8,128)(2,1)S(1)}, bf16[48,384]{1,0:T(8,128)(2,1)S(1)}, bf16[48,384]{1,0:T(8,128)(2,1)S(1)}, bf16[48,384]{1,0:T(8,128)(2,1)S(1)}, b...) custom-call(s32[8,32]{1,0:T(8,128)} %bitcast.5, ...), custom_call_target="tpu_custom_call" | custom-call | tf_op jit(solution)/shard_map/pack/pallas_call | solution.py:161
  1.4 4.0 %collective-permute-start = (bf16[48,384]{1,0:T(8,128)(2,1)S(1)}, bf16[48,384]{1,0:T(8,128)(2,1)S(1)}, u32[]{:S(2)}, u32[]{:S(2)}) collective-permute-start(bf16[48,384]{1,0:T(8,128)(2,1)S(1)} %get-tuple-element.15), channel_id=1, source_target_pairs={{0,12},{1,9},{2,14},{3,11},{4,8},{5,13},{6,10},{7,15},{8,20},{9,17... | collective-permute-start | bytes 110600 | tf_op jit(solution)/shard_map/ppermute | solution.py:391
  5.4 0.0 collective-permute-start.1
  5.4 2.2 %collective-permute-start.2 = (bf16[48,384]{1,0:T(8,128)(2,1)S(1)}, bf16[48,384]{1,0:T(8,128)(2,1)S(1)}, u32[]{:S(2)}, u32[]{:S(2)}) collective-permute-start(bf16[48,384]{1,0:T(8,128)(2,1)S(1)} %get-tuple-element.17), channel_id=1, source_target_pairs={{0,28},{1,17},{2,30},{3,19},{4,24},{5,21},{6,26},{7,23},{8,4},{9,2... | collective-permute-start | bytes 110600 | tf_op jit(solution)/shard_map/ppermute | solution.py:391
  7.6 0.0 collective-permute-start.3
  7.6 3.4 %collective-permute-start.4 = (bf16[48,384]{1,0:T(8,128)(2,1)S(1)}, bf16[48,384]{1,0:T(8,128)(2,1)S(1)}, u32[]{:S(2)}, u32[]{:S(2)}) collective-permute-start(bf16[48,384]{1,0:T(8,128)(2,1)S(1)} %get-tuple-element.19), channel_id=1, source_target_pairs={{0,20},{1,21},{2,22},{3,23},{4,16},{5,17},{6,18},{7,19},{8,28},{9,... | collective-permute-start | bytes 110600 | tf_op jit(solution)/shard_map/ppermute | solution.py:391
  11.0 0.0 collective-permute-done.refs_0_
  11.0 0.6 %collective-permute-start.5 = (bf16[48,384]{1,0:T(8,128)(2,1)S(1)}, bf16[48,384]{1,0:T(8,128)(2,1)S(1)}, u32[]{:S(2)}, u32[]{:S(2)}) collective-permute-start(bf16[48,384]{1,0:T(8,128)(2,1)S(1)} %get-tuple-element.20), channel_id=1, source_target_pairs={{0,16},{1,29},{2,18},{3,31},{4,20},{5,25},{6,22},{7,27},{8,24},{9,... | collective-permute-start | bytes 110600 | tf_op jit(solution)/shard_map/ppermute | solution.py:391
  11.5 0.0 collective-permute-done.1.refs_1_
  11.5 0.5 %collective-permute-start.6 = (bf16[48,384]{1,0:T(8,128)(2,1)S(1)}, bf16[48,384]{1,0:T(8,128)(2,1)S(1)}, u32[]{:S(2)}, u32[]{:S(2)}) collective-permute-start(bf16[48,384]{1,0:T(8,128)(2,1)S(1)} %get-tuple-element.21), channel_id=1, source_target_pairs={{0,4},{1,25},{2,6},{3,27},{4,0},{5,29},{6,2},{7,31},{8,12},{9,1},{... | collective-permute-start | bytes 110600 | tf_op jit(solution)/shard_map/ppermute | solution.py:391
  12.0 0.0 collective-permute-done.2.refs_2_
  12.0 1.5 %collective-permute-done.3.refs_3_ = bf16[48,384]{1,0:T(8,128)(2,1)S(1)} collective-permute-done((bf16[48,384]{1,0:T(8,128)(2,1)S(1)}, bf16[48,384]{1,0:T(8,128)(2,1)S(1)}, u32[]{:S(2)}, u32[]{:S(2)}) %collective-permute-start.3) | collective-permute-done | bytes 36896 | tf_op jit(solution)/shard_map/ppermute | solution.py:391
  13.5 0.0 collective-permute-done.4.refs_4_
  13.5 2.6 %collective-permute-done.5.refs_5_ = bf16[48,384]{1,0:T(8,128)(2,1)S(1)} collective-permute-done((bf16[48,384]{1,0:T(8,128)(2,1)S(1)}, bf16[48,384]{1,0:T(8,128)(2,1)S(1)}, u32[]{:S(2)}, u32[]{:S(2)}) %collective-permute-start.5) | collective-permute-done | bytes 36896 | tf_op jit(solution)/shard_map/ppermute | solution.py:391
  16.1 0.0 collective-permute-done.6.refs_6_
  16.1 5.7 %correlate.1 = bf16[1,8,40,40,256]{4,3,2,1,0:T(8,128)(2,1)} custom-call(f32[1,64]{1,0:T(1,128)S(1)} %get-tuple-element.14.taps_ref, bf16[48,384]{1,0:T(8,128)(2,1)S(1)} %collective-permute-done.refs_0_, bf16[48,384]{1,0:T(8,128)(2,1)S(1)} %collective-permute-done.1.refs_1_, bf16[48,384]{1,0:T(8,128)(2,1)S(1)} %collective-permute-done.2.refs_2_, ...), custom_call_target="tpu_custom_call" | custom-call | tf_op jit(solution)/shard_map/correlate/pallas_call | solution.py:358
Async XLA Ops:
  1.4 9.5 %collective-permute-start = (bf16[48,384]{1,0:T(8,128)(2,1)S(1)}, bf16[48,384]{1,0:T(8,128)(2,1)S(1)}, u32[]{:S(2)}, u32[]{:S(2)}) collective-permute-start(bf16[48,384]{1,0:T(8,128)(2,1)S(1)} %get-tuple-element.15), channel_id=1, source_target_pairs={{0,12},{1,9},{2,14},{3,11},{4,8},{5,13},{6,10},{7,15},{8,20},{9,17... | collective-permute-start | bytes 110600 | tf_op jit(solution)/shard_map/ppermute | solution.py:391
  5.4 6.1 %collective-permute-start.1 = (bf16[48,384]{1,0:T(8,128)(2,1)S(1)}, bf16[48,384]{1,0:T(8,128)(2,1)S(1)}, u32[]{:S(2)}, u32[]{:S(2)}) collective-permute-start(bf16[48,384]{1,0:T(8,128)(2,1)S(1)} %get-tuple-element.16), channel_id=1, source_target_pairs={{0,5},{1,24},{2,7},{3,26},{4,1},{5,28},{6,3},{7,30},{8,13},{9,0},{... | collective-permute-start | bytes 110600 | tf_op jit(solution)/shard_map/ppermute | solution.py:391
  5.4 6.6 %collective-permute-start.2 = (bf16[48,384]{1,0:T(8,128)(2,1)S(1)}, bf16[48,384]{1,0:T(8,128)(2,1)S(1)}, u32[]{:S(2)}, u32[]{:S(2)}) collective-permute-start(bf16[48,384]{1,0:T(8,128)(2,1)S(1)} %get-tuple-element.17), channel_id=1, source_target_pairs={{0,28},{1,17},{2,30},{3,19},{4,24},{5,21},{6,26},{7,23},{8,4},{9,2... | collective-permute-start | bytes 110600 | tf_op jit(solution)/shard_map/ppermute | solution.py:391
  7.6 5.9 %collective-permute-start.3 = (bf16[48,384]{1,0:T(8,128)(2,1)S(1)}, bf16[48,384]{1,0:T(8,128)(2,1)S(1)}, u32[]{:S(2)}, u32[]{:S(2)}) collective-permute-start(bf16[48,384]{1,0:T(8,128)(2,1)S(1)} %get-tuple-element.18), channel_id=1, source_target_pairs={{0,8},{1,13},{2,10},{3,15},{4,12},{5,9},{6,14},{7,11},{8,16},{9,21... | collective-permute-start | bytes 110600 | tf_op jit(solution)/shard_map/ppermute | solution.py:391
  7.6 5.9 %collective-permute-start.4 = (bf16[48,384]{1,0:T(8,128)(2,1)S(1)}, bf16[48,384]{1,0:T(8,128)(2,1)S(1)}, u32[]{:S(2)}, u32[]{:S(2)}) collective-permute-start(bf16[48,384]{1,0:T(8,128)(2,1)S(1)} %get-tuple-element.19), channel_id=1, source_target_pairs={{0,20},{1,21},{2,22},{3,23},{4,16},{5,17},{6,18},{7,19},{8,28},{9,... | collective-permute-start | bytes 110600 | tf_op jit(solution)/shard_map/ppermute | solution.py:391
  11.0 5.2 %collective-permute-start.5 = (bf16[48,384]{1,0:T(8,128)(2,1)S(1)}, bf16[48,384]{1,0:T(8,128)(2,1)S(1)}, u32[]{:S(2)}, u32[]{:S(2)}) collective-permute-start(bf16[48,384]{1,0:T(8,128)(2,1)S(1)} %get-tuple-element.20), channel_id=1, source_target_pairs={{0,16},{1,29},{2,18},{3,31},{4,20},{5,25},{6,22},{7,27},{8,24},{9,... | collective-permute-start | bytes 110600 | tf_op jit(solution)/shard_map/ppermute | solution.py:391
  11.5 4.6 %collective-permute-start.6 = (bf16[48,384]{1,0:T(8,128)(2,1)S(1)}, bf16[48,384]{1,0:T(8,128)(2,1)S(1)}, u32[]{:S(2)}, u32[]{:S(2)}) collective-permute-start(bf16[48,384]{1,0:T(8,128)(2,1)S(1)} %get-tuple-element.21), channel_id=1, source_target_pairs={{0,4},{1,25},{2,6},{3,27},{4,0},{5,29},{6,2},{7,31},{8,12},{9,1},{... | collective-permute-start | bytes 110600 | tf_op jit(solution)/shard_map/ppermute | solution.py:391

commit v8 on v7

--- a/solution.py
+++ b/solution.py
@@ -331,7 +331,9 @@
             if part % 2 == 0:
                 multiply(group, part // 2, held)
             convert(group - 1, part, before)
-            outgoing(group - 1, part).start()
+            if part % 2:
+                outgoing(group - 1, part - 1).start(priority=0)
+                outgoing(group - 1, part).start(priority=1)
 
     for part in range(8 // wide):
         multiply(0, part, even)
@@ -344,7 +346,7 @@
     lax.fori_loop(0, count // 2, two_groups, 0)
     for part in range(parts):
         convert(count - 1, part, even)
-        outgoing(count - 1, part).start()
+        outgoing(count - 1, part).start(priority=part % 2)
     for group in range(count):
         for part in range(parts):
             outgoing(group, part).wait()

time: 22 us -> 22 us (level)
  no operation moved by 1% of the time
where the time goes in v8:
time: 22 us; the launch traced here: 21.9 us
  starting transfers between devices  10.6 us (48%)
  Pallas kernels  7.17 us (33%)
  waiting for transfers between devices  4.13 us (19%)
    ppermute x7, starting transfers between devices, on_device(): message = lax.ppermute(message, ('grp', 'rep'), way)  10.6 us
    pallas_call x1, Pallas kernels, correlate(): pl.pallas_call(functools.partial(correlate_kernel, period), out_shape=jax...  5.74 us
    ppermute x7, waiting for transfers between devices, on_device(): message = lax.ppermute(message, ('grp', 'rep'), way)  4.13 us
    pallas_call x1, Pallas kernels, pack(): pl.pallas_call(functools.partial(pack_kernel, rep_count), out_shape=[jax....  1.43 us
  transfers between devices with their start and end apart: 7, of which 2 were waited for; matrix products, arithmetic and copies ran while one was open for 0% of the time, Pallas kernels for 0%

profile of v8, /device:TPU:0, one launch (start us, length us, event | category | flops | bytes accessed | tf_op | source)
XLA Modules:
  0.0 21.9 jit_solution(9249372104446497283)
XLA Ops:
  0.0 1.4 %pack.1 = (bf16[48,384]{1,0:T(8,128)(2,1)S(1)}, bf16[48,384]{1,0:T(8,128)(2,1)S(1)}, bf16[48,384]{1,0:T(8,128)(2,1)S(1)}, bf16[48,384]{1,0:T(8,128)(2,1)S(1)}, b...) custom-call(s32[8,32]{1,0:T(8,128)} %bitcast.5, ...), custom_call_target="tpu_custom_call" | custom-call | tf_op jit(solution)/shard_map/pack/pallas_call | solution.py:161
  1.4 4.0 %collective-permute-start = (bf16[48,384]{1,0:T(8,128)(2,1)S(1)}, bf16[48,384]{1,0:T(8,128)(2,1)S(1)}, u32[]{:S(2)}, u32[]{:S(2)}) collective-permute-start(bf16[48,384]{1,0:T(8,128)(2,1)S(1)} %get-tuple-element.15), channel_id=1, source_target_pairs={{0,12},{1,9},{2,14},{3,11},{4,8},{5,13},{6,10},{7,15},{8,20},{9,17... | collective-permute-start | bytes 110600 | tf_op jit(solution)/shard_map/ppermute | solution.py:393
  5.4 0.0 collective-permute-start.1
  5.4 2.2 %collective-permute-start.2 = (bf16[48,384]{1,0:T(8,128)(2,1)S(1)}, bf16[48,384]{1,0:T(8,128)(2,1)S(1)}, u32[]{:S(2)}, u32[]{:S(2)}) collective-permute-start(bf16[48,384]{1,0:T(8,128)(2,1)S(1)} %get-tuple-element.17), channel_id=1, source_target_pairs={{0,28},{1,17},{2,30},{3,19},{4,24},{5,21},{6,26},{7,23},{8,4},{9,2... | collective-permute-start | bytes 110600 | tf_op jit(solution)/shard_map/ppermute | solution.py:393
  7.6 0.0 collective-permute-start.3
  7.6 3.4 %collective-permute-start.4 = (bf16[48,384]{1,0:T(8,128)(2,1)S(1)}, bf16[48,384]{1,0:T(8,128)(2,1)S(1)}, u32[]{:S(2)}, u32[]{:S(2)}) collective-permute-start(bf16[48,384]{1,0:T(8,128)(2,1)S(1)} %get-tuple-element.19), channel_id=1, source_target_pairs={{0,20},{1,21},{2,22},{3,23},{4,16},{5,17},{6,18},{7,19},{8,28},{9,... | collective-permute-start | bytes 110600 | tf_op jit(solution)/shard_map/ppermute | solution.py:393
  11.0 0.0 collective-permute-done.refs_0_
  11.0 0.6 %collective-permute-start.5 = (bf16[48,384]{1,0:T(8,128)(2,1)S(1)}, bf16[48,384]{1,0:T(8,128)(2,1)S(1)}, u32[]{:S(2)}, u32[]{:S(2)}) collective-permute-start(bf16[48,384]{1,0:T(8,128)(2,1)S(1)} %get-tuple-element.20), channel_id=1, source_target_pairs={{0,16},{1,29},{2,18},{3,31},{4,20},{5,25},{6,22},{7,27},{8,24},{9,... | collective-permute-start | bytes 110600 | tf_op jit(solution)/shard_map/ppermute | solution.py:393
  11.5 0.0 collective-permute-done.1.refs_1_
  11.5 0.5 %collective-permute-start.6 = (bf16[48,384]{1,0:T(8,128)(2,1)S(1)}, bf16[48,384]{1,0:T(8,128)(2,1)S(1)}, u32[]{:S(2)}, u32[]{:S(2)}) collective-permute-start(bf16[48,384]{1,0:T(8,128)(2,1)S(1)} %get-tuple-element.21), channel_id=1, source_target_pairs={{0,4},{1,25},{2,6},{3,27},{4,0},{5,29},{6,2},{7,31},{8,12},{9,1},{... | collective-permute-start | bytes 110600 | tf_op jit(solution)/shard_map/ppermute | solution.py:393
  12.0 0.0 collective-permute-done.2.refs_2_
  12.0 1.5 %collective-permute-done.3.refs_3_ = bf16[48,384]{1,0:T(8,128)(2,1)S(1)} collective-permute-done((bf16[48,384]{1,0:T(8,128)(2,1)S(1)}, bf16[48,384]{1,0:T(8,128)(2,1)S(1)}, u32[]{:S(2)}, u32[]{:S(2)}) %collective-permute-start.3) | collective-permute-done | bytes 36896 | tf_op jit(solution)/shard_map/ppermute | solution.py:393
  13.5 0.0 collective-permute-done.4.refs_4_
  13.5 2.6 %collective-permute-done.5.refs_5_ = bf16[48,384]{1,0:T(8,128)(2,1)S(1)} collective-permute-done((bf16[48,384]{1,0:T(8,128)(2,1)S(1)}, bf16[48,384]{1,0:T(8,128)(2,1)S(1)}, u32[]{:S(2)}, u32[]{:S(2)}) %collective-permute-start.5) | collective-permute-done | bytes 36896 | tf_op jit(solution)/shard_map/ppermute | solution.py:393
  16.1 0.0 collective-permute-done.6.refs_6_
  16.1 5.7 %correlate.1 = bf16[1,8,40,40,256]{4,3,2,1,0:T(8,128)(2,1)} custom-call(f32[1,64]{1,0:T(1,128)S(1)} %get-tuple-element.14.taps_ref, bf16[48,384]{1,0:T(8,128)(2,1)S(1)} %collective-permute-done.refs_0_, bf16[48,384]{1,0:T(8,128)(2,1)S(1)} %collective-permute-done.1.refs_1_, bf16[48,384]{1,0:T(8,128)(2,1)S(1)} %collective-permute-done.2.refs_2_, ...), custom_call_target="tpu_custom_call" | custom-call | tf_op jit(solution)/shard_map/correlate/pallas_call | solution.py:360
Async XLA Ops:
  1.4 9.5 %collective-permute-start = (bf16[48,384]{1,0:T(8,128)(2,1)S(1)}, bf16[48,384]{1,0:T(8,128)(2,1)S(1)}, u32[]{:S(2)}, u32[]{:S(2)}) collective-permute-start(bf16[48,384]{1,0:T(8,128)(2,1)S(1)} %get-tuple-element.15), channel_id=1, source_target_pairs={{0,12},{1,9},{2,14},{3,11},{4,8},{5,13},{6,10},{7,15},{8,20},{9,17... | collective-permute-start | bytes 110600 | tf_op jit(solution)/shard_map/ppermute | solution.py:393
  5.4 6.1 %collective-permute-start.1 = (bf16[48,384]{1,0:T(8,128)(2,1)S(1)}, bf16[48,384]{1,0:T(8,128)(2,1)S(1)}, u32[]{:S(2)}, u32[]{:S(2)}) collective-permute-start(bf16[48,384]{1,0:T(8,128)(2,1)S(1)} %get-tuple-element.16), channel_id=1, source_target_pairs={{0,5},{1,24},{2,7},{3,26},{4,1},{5,28},{6,3},{7,30},{8,13},{9,0},{... | collective-permute-start | bytes 110600 | tf_op jit(solution)/shard_map/ppermute | solution.py:393
  5.4 6.6 %collective-permute-start.2 = (bf16[48,384]{1,0:T(8,128)(2,1)S(1)}, bf16[48,384]{1,0:T(8,128)(2,1)S(1)}, u32[]{:S(2)}, u32[]{:S(2)}) collective-permute-start(bf16[48,384]{1,0:T(8,128)(2,1)S(1)} %get-tuple-element.17), channel_id=1, source_target_pairs={{0,28},{1,17},{2,30},{3,19},{4,24},{5,21},{6,26},{7,23},{8,4},{9,2... | collective-permute-start | bytes 110600 | tf_op jit(solution)/shard_map/ppermute | solution.py:393
  7.6 5.9 %collective-permute-start.3 = (bf16[48,384]{1,0:T(8,128)(2,1)S(1)}, bf16[48,384]{1,0:T(8,128)(2,1)S(1)}, u32[]{:S(2)}, u32[]{:S(2)}) collective-permute-start(bf16[48,384]{1,0:T(8,128)(2,1)S(1)} %get-tuple-element.18), channel_id=1, source_target_pairs={{0,8},{1,13},{2,10},{3,15},{4,12},{5,9},{6,14},{7,11},{8,16},{9,21... | collective-permute-start | bytes 110600 | tf_op jit(solution)/shard_map/ppermute | solution.py:393
  7.6 5.9 %collective-permute-start.4 = (bf16[48,384]{1,0:T(8,128)(2,1)S(1)}, bf16[48,384]{1,0:T(8,128)(2,1)S(1)}, u32[]{:S(2)}, u32[]{:S(2)}) collective-permute-start(bf16[48,384]{1,0:T(8,128)(2,1)S(1)} %get-tuple-element.19), channel_id=1, source_target_pairs={{0,20},{1,21},{2,22},{3,23},{4,16},{5,17},{6,18},{7,19},{8,28},{9,... | collective-permute-start | bytes 110600 | tf_op jit(solution)/shard_map/ppermute | solution.py:393
  11.0 5.2 %collective-permute-start.5 = (bf16[48,384]{1,0:T(8,128)(2,1)S(1)}, bf16[48,384]{1,0:T(8,128)(2,1)S(1)}, u32[]{:S(2)}, u32[]{:S(2)}) collective-permute-start(bf16[48,384]{1,0:T(8,128)(2,1)S(1)} %get-tuple-element.20), channel_id=1, source_target_pairs={{0,16},{1,29},{2,18},{3,31},{4,20},{5,25},{6,22},{7,27},{8,24},{9,... | collective-permute-start | bytes 110600 | tf_op jit(solution)/shard_map/ppermute | solution.py:393
  11.5 4.6 %collective-permute-start.6 = (bf16[48,384]{1,0:T(8,128)(2,1)S(1)}, bf16[48,384]{1,0:T(8,128)(2,1)S(1)}, u32[]{:S(2)}, u32[]{:S(2)}) collective-permute-start(bf16[48,384]{1,0:T(8,128)(2,1)S(1)} %get-tuple-element.21), channel_id=1, source_target_pairs={{0,4},{1,25},{2,6},{3,27},{4,0},{5,29},{6,2},{7,31},{8,12},{9,1},{... | collective-permute-start | bytes 110600 | tf_op jit(solution)/shard_map/ppermute | solution.py:393

commit v9 on v8

--- a/solution.py
+++ b/solution.py
@@ -27,13 +27,13 @@
 
 
 ROUTES = (
-    ((3, 2, 5, 4, 7, 6, 1, 0), (2, 3, 4, 5, 6, 7, 0, 1), 0),
-    ((1, 0, 3, 2, 5, 4, 7, 6), (6, 7, 0, 1, 2, 3, 4, 5), 1),
-    ((7, 6, 1, 0, 3, 2, 5, 4), (4, 5, 6, 7, 0, 1, 2, 3), 0),
     ((2, 3, 4, 5, 6, 7, 0, 1), (3, 2, 5, 4, 7, 6, 1, 0), 0),
-    ((5, 4, 7, 6, 1, 0, 3, 2), (5, 4, 7, 6, 1, 0, 3, 2), 0),
+    ((2, 3, 4, 5, 6, 7, 0, 1), (5, 4, 7, 6, 1, 0, 3, 2), 1),
+    ((1, 0, 3, 2, 5, 4, 7, 6), (7, 6, 1, 0, 3, 2, 5, 4), 1),
     ((4, 5, 6, 7, 0, 1, 2, 3), (7, 6, 1, 0, 3, 2, 5, 4), 0),
-    ((1, 0, 3, 2, 5, 4, 7, 6), (6, 7, 0, 1, 2, 3, 4, 5), 0),
+    ((4, 5, 6, 7, 0, 1, 2, 3), (3, 2, 5, 4, 7, 6, 1, 0), 1),
+    ((1, 0, 3, 2, 5, 4, 7, 6), (5, 4, 7, 6, 1, 0, 3, 2), 0),
+    ((6, 7, 0, 1, 2, 3, 4, 5), (6, 7, 0, 1, 2, 3, 4, 5), 0),
 )
 
 
@@ -331,9 +331,7 @@
             if part % 2 == 0:
                 multiply(group, part // 2, held)
             convert(group - 1, part, before)
-            if part % 2:
-                outgoing(group - 1, part - 1).start(priority=0)
-                outgoing(group - 1, part).start(priority=1)
+            outgoing(group - 1, part).start(priority=part % 2)
 
     for part in range(8 // wide):
         multiply(0, part, even)

time: 22 us -> 21.7 us (0.986)
  waiting for transfers between devices: 4.13 us -> 2.35 us
  starting transfers between devices: 10.6 us -> 12.1 us
    ppermute x7, waiting for transfers between devices: 4.13 us -> 2.35 us  [on_device(): message = lax.ppermute(message, ('grp', 'rep'), way)]
    ppermute x7, starting transfers between devices: 10.6 us -> 12.1 us  [on_device(): message = lax.ppermute(message, ('grp', 'rep'), way)]
  transfers between devices with their start and end apart: 7 -> 7, of which waited for: 2 -> 3; matrix products, arithmetic and copies ran while one was open for 0% -> 0% of each run, Pallas kernels for 0% -> 0%
where the time goes in v9:
time: 21.7 us; the launch traced here: 21.6 us
  starting transfers between devices  12.1 us (56%)
  Pallas kernels  7.14 us (33%)
  waiting for transfers between devices  2.35 us (11%)
    ppermute x7, starting transfers between devices, on_device(): message = lax.ppermute(message, ('grp', 'rep'), way)  12.1 us
    pallas_call x1, Pallas kernels, correlate(): pl.pallas_call(functools.partial(correlate_kernel, period), out_shape=jax...  5.71 us
    ppermute x7, waiting for transfers between devices, on_device(): message = lax.ppermute(message, ('grp', 'rep'), way)  2.35 us
    pallas_call x1, Pallas kernels, pack(): pl.pallas_call(functools.partial(pack_kernel, rep_count), out_shape=[jax....  1.43 us
  transfers between devices with their start and end apart: 7, of which 3 were waited for; matrix products, arithmetic and copies ran while one was open for 0% of the time, Pallas kernels for 0%

profile of v9, /device:TPU:0, one launch (start us, length us, event | category | flops | bytes accessed | tf_op | source)
XLA Modules:
  0.0 21.6 jit_solution(18155263978906809086)
XLA Ops:
  0.0 1.4 %pack.1 = (bf16[48,384]{1,0:T(8,128)(2,1)S(1)}, bf16[48,384]{1,0:T(8,128)(2,1)S(1)}, bf16[48,384]{1,0:T(8,128)(2,1)S(1)}, bf16[48,384]{1,0:T(8,128)(2,1)S(1)}, b...) custom-call(s32[8,32]{1,0:T(8,128)} %bitcast.5, ...), custom_call_target="tpu_custom_call" | custom-call | tf_op jit(solution)/shard_map/pack/pallas_call | solution.py:161
  1.4 3.1 %collective-permute-start = (bf16[48,384]{1,0:T(8,128)(2,1)S(1)}, bf16[48,384]{1,0:T(8,128)(2,1)S(1)}, u32[]{:S(2)}, u32[]{:S(2)}) collective-permute-start(bf16[48,384]{1,0:T(8,128)(2,1)S(1)} %get-tuple-element.15), channel_id=1, source_target_pairs={{0,8},{1,13},{2,10},{3,15},{4,12},{5,9},{6,14},{7,11},{8,16},{9,21... | collective-permute-start | bytes 110600 | tf_op jit(solution)/shard_map/ppermute | solution.py:391
  4.5 1.7 %collective-permute-start.1 = (bf16[48,384]{1,0:T(8,128)(2,1)S(1)}, bf16[48,384]{1,0:T(8,128)(2,1)S(1)}, u32[]{:S(2)}, u32[]{:S(2)}) collective-permute-start(bf16[48,384]{1,0:T(8,128)(2,1)S(1)} %get-tuple-element.16), channel_id=1, source_target_pairs={{0,9},{1,20},{2,11},{3,22},{4,13},{5,16},{6,15},{7,18},{8,17},{9,2... | collective-permute-start | bytes 110600 | tf_op jit(solution)/shard_map/ppermute | solution.py:391
  6.2 2.1 %collective-permute-start.2 = (bf16[48,384]{1,0:T(8,128)(2,1)S(1)}, bf16[48,384]{1,0:T(8,128)(2,1)S(1)}, u32[]{:S(2)}, u32[]{:S(2)}) collective-permute-start(bf16[48,384]{1,0:T(8,128)(2,1)S(1)} %get-tuple-element.17), channel_id=1, source_target_pairs={{0,5},{1,28},{2,7},{3,30},{4,1},{5,24},{6,3},{7,26},{8,13},{9,4},{... | collective-permute-start | bytes 110600 | tf_op jit(solution)/shard_map/ppermute | solution.py:391
  8.3 0.3 %collective-permute-start.3 = (bf16[48,384]{1,0:T(8,128)(2,1)S(1)}, bf16[48,384]{1,0:T(8,128)(2,1)S(1)}, u32[]{:S(2)}, u32[]{:S(2)}) collective-permute-start(bf16[48,384]{1,0:T(8,128)(2,1)S(1)} %get-tuple-element.18), channel_id=1, source_target_pairs={{0,16},{1,29},{2,18},{3,31},{4,20},{5,25},{6,22},{7,27},{8,24},{9,... | collective-permute-start | bytes 110600 | tf_op jit(solution)/shard_map/ppermute | solution.py:391
  8.6 1.4 %collective-permute-start.4 = (bf16[48,384]{1,0:T(8,128)(2,1)S(1)}, bf16[48,384]{1,0:T(8,128)(2,1)S(1)}, u32[]{:S(2)}, u32[]{:S(2)}) collective-permute-start(bf16[48,384]{1,0:T(8,128)(2,1)S(1)} %get-tuple-element.19), channel_id=1, source_target_pairs={{0,17},{1,12},{2,19},{3,14},{4,21},{5,8},{6,23},{7,10},{8,25},{9,2... | collective-permute-start | bytes 110600 | tf_op jit(solution)/shard_map/ppermute | solution.py:391
  10.0 0.0 collective-permute-done.refs_0_
  10.0 0.6 %collective-permute-start.5 = (bf16[48,384]{1,0:T(8,128)(2,1)S(1)}, bf16[48,384]{1,0:T(8,128)(2,1)S(1)}, u32[]{:S(2)}, u32[]{:S(2)}) collective-permute-start(bf16[48,384]{1,0:T(8,128)(2,1)S(1)} %get-tuple-element.20), channel_id=1, source_target_pairs={{0,4},{1,21},{2,6},{3,23},{4,0},{5,17},{6,2},{7,19},{8,12},{9,29},... | collective-permute-start | bytes 110600 | tf_op jit(solution)/shard_map/ppermute | solution.py:391
  10.6 0.2 collective-permute-done.1.refs_1_
  10.8 2.9 %collective-permute-start.6 = (bf16[48,384]{1,0:T(8,128)(2,1)S(1)}, bf16[48,384]{1,0:T(8,128)(2,1)S(1)}, u32[]{:S(2)}, u32[]{:S(2)}) collective-permute-start(bf16[48,384]{1,0:T(8,128)(2,1)S(1)} %get-tuple-element.21), channel_id=1, source_target_pairs={{0,24},{1,25},{2,26},{3,27},{4,28},{5,29},{6,30},{7,31},{8,0},{9,1... | collective-permute-start | bytes 110600 | tf_op jit(solution)/shard_map/ppermute | solution.py:391
  13.7 0.0 collective-permute-done.2.refs_2_
  13.7 0.0 collective-permute-done.3.refs_3_
  13.7 1.2 %collective-permute-done.4.refs_4_ = bf16[48,384]{1,0:T(8,128)(2,1)S(1)} collective-permute-done((bf16[48,384]{1,0:T(8,128)(2,1)S(1)}, bf16[48,384]{1,0:T(8,128)(2,1)S(1)}, u32[]{:S(2)}, u32[]{:S(2)}) %collective-permute-start.4) | collective-permute-done | bytes 36896 | tf_op jit(solution)/shard_map/ppermute | solution.py:391
  14.9 0.0 collective-permute-done.5.refs_5_
  14.9 0.9 %collective-permute-done.6.refs_6_ = bf16[48,384]{1,0:T(8,128)(2,1)S(1)} collective-permute-done((bf16[48,384]{1,0:T(8,128)(2,1)S(1)}, bf16[48,384]{1,0:T(8,128)(2,1)S(1)}, u32[]{:S(2)}, u32[]{:S(2)}) %collective-permute-start.6) | collective-permute-done | bytes 36896 | tf_op jit(solution)/shard_map/ppermute | solution.py:391
  15.9 5.7 %correlate.1 = bf16[1,8,40,40,256]{4,3,2,1,0:T(8,128)(2,1)} custom-call(f32[1,64]{1,0:T(1,128)S(1)} %get-tuple-element.14.taps_ref, bf16[48,384]{1,0:T(8,128)(2,1)S(1)} %collective-permute-done.refs_0_, bf16[48,384]{1,0:T(8,128)(2,1)S(1)} %collective-permute-done.1.refs_1_, bf16[48,384]{1,0:T(8,128)(2,1)S(1)} %collective-permute-done.2.refs_2_, ...), custom_call_target="tpu_custom_call" | custom-call | tf_op jit(solution)/shard_map/correlate/pallas_call | solution.py:358
Async XLA Ops:
  1.4 8.6 %collective-permute-start = (bf16[48,384]{1,0:T(8,128)(2,1)S(1)}, bf16[48,384]{1,0:T(8,128)(2,1)S(1)}, u32[]{:S(2)}, u32[]{:S(2)}) collective-permute-start(bf16[48,384]{1,0:T(8,128)(2,1)S(1)} %get-tuple-element.15), channel_id=1, source_target_pairs={{0,8},{1,13},{2,10},{3,15},{4,12},{5,9},{6,14},{7,11},{8,16},{9,21... | collective-permute-start | bytes 110600 | tf_op jit(solution)/shard_map/ppermute | solution.py:391
  4.5 6.3 %collective-permute-start.1 = (bf16[48,384]{1,0:T(8,128)(2,1)S(1)}, bf16[48,384]{1,0:T(8,128)(2,1)S(1)}, u32[]{:S(2)}, u32[]{:S(2)}) collective-permute-start(bf16[48,384]{1,0:T(8,128)(2,1)S(1)} %get-tuple-element.16), channel_id=1, source_target_pairs={{0,9},{1,20},{2,11},{3,22},{4,13},{5,16},{6,15},{7,18},{8,17},{9,2... | collective-permute-start | bytes 110600 | tf_op jit(solution)/shard_map/ppermute | solution.py:391
  6.2 7.5 %collective-permute-start.2 = (bf16[48,384]{1,0:T(8,128)(2,1)S(1)}, bf16[48,384]{1,0:T(8,128)(2,1)S(1)}, u32[]{:S(2)}, u32[]{:S(2)}) collective-permute-start(bf16[48,384]{1,0:T(8,128)(2,1)S(1)} %get-tuple-element.17), channel_id=1, source_target_pairs={{0,5},{1,28},{2,7},{3,30},{4,1},{5,24},{6,3},{7,26},{8,13},{9,4},{... | collective-permute-start | bytes 110600 | tf_op jit(solution)/shard_map/ppermute | solution.py:391
  8.3 5.4 %collective-permute-start.3 = (bf16[48,384]{1,0:T(8,128)(2,1)S(1)}, bf16[48,384]{1,0:T(8,128)(2,1)S(1)}, u32[]{:S(2)}, u32[]{:S(2)}) collective-permute-start(bf16[48,384]{1,0:T(8,128)(2,1)S(1)} %get-tuple-element.18), channel_id=1, source_target_pairs={{0,16},{1,29},{2,18},{3,31},{4,20},{5,25},{6,22},{7,27},{8,24},{9,... | collective-permute-start | bytes 110600 | tf_op jit(solution)/shard_map/ppermute | solution.py:391
  8.6 6.3 %collective-permute-start.4 = (bf16[48,384]{1,0:T(8,128)(2,1)S(1)}, bf16[48,384]{1,0:T(8,128)(2,1)S(1)}, u32[]{:S(2)}, u32[]{:S(2)}) collective-permute-start(bf16[48,384]{1,0:T(8,128)(2,1)S(1)} %get-tuple-element.19), channel_id=1, source_target_pairs={{0,17},{1,12},{2,19},{3,14},{4,21},{5,8},{6,23},{7,10},{8,25},{9,2... | collective-permute-start | bytes 110600 | tf_op jit(solution)/shard_map/ppermute | solution.py:391
  10.0 4.9 %collective-permute-start.5 = (bf16[48,384]{1,0:T(8,128)(2,1)S(1)}, bf16[48,384]{1,0:T(8,128)(2,1)S(1)}, u32[]{:S(2)}, u32[]{:S(2)}) collective-permute-start(bf16[48,384]{1,0:T(8,128)(2,1)S(1)} %get-tuple-element.20), channel_id=1, source_target_pairs={{0,4},{1,21},{2,6},{3,23},{4,0},{5,17},{6,2},{7,19},{8,12},{9,29},... | collective-permute-start | bytes 110600 | tf_op jit(solution)/shard_map/ppermute | solution.py:391
  10.8 5.1 %collective-permute-start.6 = (bf16[48,384]{1,0:T(8,128)(2,1)S(1)}, bf16[48,384]{1,0:T(8,128)(2,1)S(1)}, u32[]{:S(2)}, u32[]{:S(2)}) collective-permute-start(bf16[48,384]{1,0:T(8,128)(2,1)S(1)} %get-tuple-element.21), channel_id=1, source_target_pairs={{0,24},{1,25},{2,26},{3,27},{4,28},{5,29},{6,30},{7,31},{8,0},{9,1... | collective-permute-start | bytes 110600 | tf_op jit(solution)/shard_map/ppermute | solution.py:391

commit v10 on v9

--- a/solution.py
+++ b/solution.py
@@ -312,7 +312,7 @@
     def multiply(group, part, held):
         channel = group * 8 + wide * part
         weights = jnp.concatenate([band(channel + side) for side in range(wide)], axis=1)
-        product = dot(partner_ref[...], weights) * normalizer
+        product = dot(partner_ref[...], weights)
         for half, ref in enumerate(held):
             for side in range(wide):
                 ref[pl.ds(wide * part + side, rows, stride=STRIDE), :] = product[
@@ -324,7 +324,7 @@
             for line in range(TILE):
                 at = pl.ds((tile * TILE + line) * STRIDE, 8)
                 both = jnp.concatenate([ref[at, :] for ref in held], axis=1)
-                packed_ref[group, tile, line] = both.astype(jnp.bfloat16)
+                packed_ref[group, tile, line] = (both * normalizer).astype(jnp.bfloat16)
 
     def together(group, held, before):
         for part in range(parts):

time: 21.7 us -> 22.1 us (1.018)
  Pallas kernels: 7.14 us -> 7.48 us
    pallas_call x1, Pallas kernels: 5.71 us -> 6.04 us  [correlate(): pl.pallas_call(functools.partial(correlate_kernel, period), out_shape=jax...]
where the time goes in v10:
time: 22.1 us; the launch traced here: 21.9 us
  starting transfers between devices  12.1 us (55%)
  Pallas kernels  7.48 us (34%)
  waiting for transfers between devices  2.35 us (11%)
    ppermute x7, starting transfers between devices, on_device(): message = lax.ppermute(message, ('grp', 'rep'), way)  12.1 us
    pallas_call x1, Pallas kernels, correlate(): pl.pallas_call(functools.partial(correlate_kernel, period), out_shape=jax...  6.04 us
    ppermute x7, waiting for transfers between devices, on_device(): message = lax.ppermute(message, ('grp', 'rep'), way)  2.35 us
    pallas_call x1, Pallas kernels, pack(): pl.pallas_call(functools.partial(pack_kernel, rep_count), out_shape=[jax....  1.43 us
  transfers between devices with their start and end apart: 7, of which 3 were waited for; matrix products, arithmetic and copies ran while one was open for 0% of the time, Pallas kernels for 0%

profile of v10, /device:TPU:0, one launch (start us, length us, event | category | flops | bytes accessed | tf_op | source)
XLA Modules:
  0.0 21.9 jit_solution(10553511176664538722)
XLA Ops:
  0.0 1.4 %pack.1 = (bf16[48,384]{1,0:T(8,128)(2,1)S(1)}, bf16[48,384]{1,0:T(8,128)(2,1)S(1)}, bf16[48,384]{1,0:T(8,128)(2,1)S(1)}, bf16[48,384]{1,0:T(8,128)(2,1)S(1)}, b...) custom-call(s32[8,32]{1,0:T(8,128)} %bitcast.5, ...), custom_call_target="tpu_custom_call" | custom-call | tf_op jit(solution)/shard_map/pack/pallas_call | solution.py:161
  1.4 3.1 %collective-permute-start = (bf16[48,384]{1,0:T(8,128)(2,1)S(1)}, bf16[48,384]{1,0:T(8,128)(2,1)S(1)}, u32[]{:S(2)}, u32[]{:S(2)}) collective-permute-start(bf16[48,384]{1,0:T(8,128)(2,1)S(1)} %get-tuple-element.15), channel_id=1, source_target_pairs={{0,8},{1,13},{2,10},{3,15},{4,12},{5,9},{6,14},{7,11},{8,16},{9,21... | collective-permute-start | bytes 110600 | tf_op jit(solution)/shard_map/ppermute | solution.py:391
  4.5 1.7 %collective-permute-start.1 = (bf16[48,384]{1,0:T(8,128)(2,1)S(1)}, bf16[48,384]{1,0:T(8,128)(2,1)S(1)}, u32[]{:S(2)}, u32[]{:S(2)}) collective-permute-start(bf16[48,384]{1,0:T(8,128)(2,1)S(1)} %get-tuple-element.16), channel_id=1, source_target_pairs={{0,9},{1,20},{2,11},{3,22},{4,13},{5,16},{6,15},{7,18},{8,17},{9,2... | collective-permute-start | bytes 110600 | tf_op jit(solution)/shard_map/ppermute | solution.py:391
  6.2 2.1 %collective-permute-start.2 = (bf16[48,384]{1,0:T(8,128)(2,1)S(1)}, bf16[48,384]{1,0:T(8,128)(2,1)S(1)}, u32[]{:S(2)}, u32[]{:S(2)}) collective-permute-start(bf16[48,384]{1,0:T(8,128)(2,1)S(1)} %get-tuple-element.17), channel_id=1, source_target_pairs={{0,5},{1,28},{2,7},{3,30},{4,1},{5,24},{6,3},{7,26},{8,13},{9,4},{... | collective-permute-start | bytes 110600 | tf_op jit(solution)/shard_map/ppermute | solution.py:391
  8.3 0.3 %collective-permute-start.3 = (bf16[48,384]{1,0:T(8,128)(2,1)S(1)}, bf16[48,384]{1,0:T(8,128)(2,1)S(1)}, u32[]{:S(2)}, u32[]{:S(2)}) collective-permute-start(bf16[48,384]{1,0:T(8,128)(2,1)S(1)} %get-tuple-element.18), channel_id=1, source_target_pairs={{0,16},{1,29},{2,18},{3,31},{4,20},{5,25},{6,22},{7,27},{8,24},{9,... | collective-permute-start | bytes 110600 | tf_op jit(solution)/shard_map/ppermute | solution.py:391
  8.6 1.4 %collective-permute-start.4 = (bf16[48,384]{1,0:T(8,128)(2,1)S(1)}, bf16[48,384]{1,0:T(8,128)(2,1)S(1)}, u32[]{:S(2)}, u32[]{:S(2)}) collective-permute-start(bf16[48,384]{1,0:T(8,128)(2,1)S(1)} %get-tuple-element.19), channel_id=1, source_target_pairs={{0,17},{1,12},{2,19},{3,14},{4,21},{5,8},{6,23},{7,10},{8,25},{9,2... | collective-permute-start | bytes 110600 | tf_op jit(solution)/shard_map/ppermute | solution.py:391
  10.0 0.0 collective-permute-done.refs_0_
  10.0 0.6 %collective-permute-start.5 = (bf16[48,384]{1,0:T(8,128)(2,1)S(1)}, bf16[48,384]{1,0:T(8,128)(2,1)S(1)}, u32[]{:S(2)}, u32[]{:S(2)}) collective-permute-start(bf16[48,384]{1,0:T(8,128)(2,1)S(1)} %get-tuple-element.20), channel_id=1, source_target_pairs={{0,4},{1,21},{2,6},{3,23},{4,0},{5,17},{6,2},{7,19},{8,12},{9,29},... | collective-permute-start | bytes 110600 | tf_op jit(solution)/shard_map/ppermute | solution.py:391
  10.6 0.2 collective-permute-done.1.refs_1_
  10.8 2.9 %collective-permute-start.6 = (bf16[48,384]{1,0:T(8,128)(2,1)S(1)}, bf16[48,384]{1,0:T(8,128)(2,1)S(1)}, u32[]{:S(2)}, u32[]{:S(2)}) collective-permute-start(bf16[48,384]{1,0:T(8,128)(2,1)S(1)} %get-tuple-element.21), channel_id=1, source_target_pairs={{0,24},{1,25},{2,26},{3,27},{4,28},{5,29},{6,30},{7,31},{8,0},{9,1... | collective-permute-start | bytes 110600 | tf_op jit(solution)/shard_map/ppermute | solution.py:391
  13.7 0.0 collective-permute-done.2.refs_2_
  13.7 0.0 collective-permute-done.3.refs_3_
  13.7 1.2 %collective-permute-done.4.refs_4_ = bf16[48,384]{1,0:T(8,128)(2,1)S(1)} collective-permute-done((bf16[48,384]{1,0:T(8,128)(2,1)S(1)}, bf16[48,384]{1,0:T(8,128)(2,1)S(1)}, u32[]{:S(2)}, u32[]{:S(2)}) %collective-permute-start.4) | collective-permute-done | bytes 36896 | tf_op jit(solution)/shard_map/ppermute | solution.py:391
  14.9 0.0 collective-permute-done.5.refs_5_
  14.9 0.9 %collective-permute-done.6.refs_6_ = bf16[48,384]{1,0:T(8,128)(2,1)S(1)} collective-permute-done((bf16[48,384]{1,0:T(8,128)(2,1)S(1)}, bf16[48,384]{1,0:T(8,128)(2,1)S(1)}, u32[]{:S(2)}, u32[]{:S(2)}) %collective-permute-start.6) | collective-permute-done | bytes 36896 | tf_op jit(solution)/shard_map/ppermute | solution.py:391
  15.9 6.0 %correlate.1 = bf16[1,8,40,40,256]{4,3,2,1,0:T(8,128)(2,1)} custom-call(f32[1,64]{1,0:T(1,128)S(1)} %get-tuple-element.14.taps_ref, bf16[48,384]{1,0:T(8,128)(2,1)S(1)} %collective-permute-done.refs_0_, bf16[48,384]{1,0:T(8,128)(2,1)S(1)} %collective-permute-done.1.refs_1_, bf16[48,384]{1,0:T(8,128)(2,1)S(1)} %collective-permute-done.2.refs_2_, ...), custom_call_target="tpu_custom_call" | custom-call | tf_op jit(solution)/shard_map/correlate/pallas_call | solution.py:358
Async XLA Ops:
  1.4 8.6 %collective-permute-start = (bf16[48,384]{1,0:T(8,128)(2,1)S(1)}, bf16[48,384]{1,0:T(8,128)(2,1)S(1)}, u32[]{:S(2)}, u32[]{:S(2)}) collective-permute-start(bf16[48,384]{1,0:T(8,128)(2,1)S(1)} %get-tuple-element.15), channel_id=1, source_target_pairs={{0,8},{1,13},{2,10},{3,15},{4,12},{5,9},{6,14},{7,11},{8,16},{9,21... | collective-permute-start | bytes 110600 | tf_op jit(solution)/shard_map/ppermute | solution.py:391
  4.5 6.3 %collective-permute-start.1 = (bf16[48,384]{1,0:T(8,128)(2,1)S(1)}, bf16[48,384]{1,0:T(8,128)(2,1)S(1)}, u32[]{:S(2)}, u32[]{:S(2)}) collective-permute-start(bf16[48,384]{1,0:T(8,128)(2,1)S(1)} %get-tuple-element.16), channel_id=1, source_target_pairs={{0,9},{1,20},{2,11},{3,22},{4,13},{5,16},{6,15},{7,18},{8,17},{9,2... | collective-permute-start | bytes 110600 | tf_op jit(solution)/shard_map/ppermute | solution.py:391
  6.2 7.5 %collective-permute-start.2 = (bf16[48,384]{1,0:T(8,128)(2,1)S(1)}, bf16[48,384]{1,0:T(8,128)(2,1)S(1)}, u32[]{:S(2)}, u32[]{:S(2)}) collective-permute-start(bf16[48,384]{1,0:T(8,128)(2,1)S(1)} %get-tuple-element.17), channel_id=1, source_target_pairs={{0,5},{1,28},{2,7},{3,30},{4,1},{5,24},{6,3},{7,26},{8,13},{9,4},{... | collective-permute-start | bytes 110600 | tf_op jit(solution)/shard_map/ppermute | solution.py:391
  8.3 5.4 %collective-permute-start.3 = (bf16[48,384]{1,0:T(8,128)(2,1)S(1)}, bf16[48,384]{1,0:T(8,128)(2,1)S(1)}, u32[]{:S(2)}, u32[]{:S(2)}) collective-permute-start(bf16[48,384]{1,0:T(8,128)(2,1)S(1)} %get-tuple-element.18), channel_id=1, source_target_pairs={{0,16},{1,29},{2,18},{3,31},{4,20},{5,25},{6,22},{7,27},{8,24},{9,... | collective-permute-start | bytes 110600 | tf_op jit(solution)/shard_map/ppermute | solution.py:391
  8.6 6.3 %collective-permute-start.4 = (bf16[48,384]{1,0:T(8,128)(2,1)S(1)}, bf16[48,384]{1,0:T(8,128)(2,1)S(1)}, u32[]{:S(2)}, u32[]{:S(2)}) collective-permute-start(bf16[48,384]{1,0:T(8,128)(2,1)S(1)} %get-tuple-element.19), channel_id=1, source_target_pairs={{0,17},{1,12},{2,19},{3,14},{4,21},{5,8},{6,23},{7,10},{8,25},{9,2... | collective-permute-start | bytes 110600 | tf_op jit(solution)/shard_map/ppermute | solution.py:391
  10.0 4.9 %collective-permute-start.5 = (bf16[48,384]{1,0:T(8,128)(2,1)S(1)}, bf16[48,384]{1,0:T(8,128)(2,1)S(1)}, u32[]{:S(2)}, u32[]{:S(2)}) collective-permute-start(bf16[48,384]{1,0:T(8,128)(2,1)S(1)} %get-tuple-element.20), channel_id=1, source_target_pairs={{0,4},{1,21},{2,6},{3,23},{4,0},{5,17},{6,2},{7,19},{8,12},{9,29},... | collective-permute-start | bytes 110600 | tf_op jit(solution)/shard_map/ppermute | solution.py:391
  10.8 5.1 %collective-permute-start.6 = (bf16[48,384]{1,0:T(8,128)(2,1)S(1)}, bf16[48,384]{1,0:T(8,128)(2,1)S(1)}, u32[]{:S(2)}, u32[]{:S(2)}) collective-permute-start(bf16[48,384]{1,0:T(8,128)(2,1)S(1)} %get-tuple-element.21), channel_id=1, source_target_pairs={{0,24},{1,25},{2,26},{3,27},{4,28},{5,29},{6,30},{7,31},{8,0},{9,1... | collective-permute-start | bytes 110600 | tf_op jit(solution)/shard_map/ppermute | solution.py:391

commit v11 on v9

--- a/solution.py
+++ b/solution.py
@@ -11,7 +11,7 @@
 TILE = 40
 LAGS = 256
 LANES = 128
-STRIDE = 9
+STRIDE = 8
 PER_BLOCK = LANES // TILE
 
 

time: 21.7 us -> 22.4 us (1.032)
  Pallas kernels: 7.14 us -> 7.81 us
    pallas_call x1, Pallas kernels: 5.71 us -> 6.38 us  [correlate(): pl.pallas_call(functools.partial(correlate_kernel, period), out_shape=jax...]
where the time goes in v11:
time: 22.4 us; the launch traced here: 22.2 us
  starting transfers between devices  12.1 us (54%)
  Pallas kernels  7.81 us (35%)
  waiting for transfers between devices  2.35 us (10%)
    ppermute x7, starting transfers between devices, on_device(): message = lax.ppermute(message, ('grp', 'rep'), way)  12.1 us
    pallas_call x1, Pallas kernels, correlate(): pl.pallas_call(functools.partial(correlate_kernel, period), out_shape=jax...  6.38 us
    ppermute x7, waiting for transfers between devices, on_device(): message = lax.ppermute(message, ('grp', 'rep'), way)  2.35 us
    pallas_call x1, Pallas kernels, pack(): pl.pallas_call(functools.partial(pack_kernel, rep_count), out_shape=[jax....  1.43 us
  transfers between devices with their start and end apart: 7, of which 3 were waited for; matrix products, arithmetic and copies ran while one was open for 0% of the time, Pallas kernels for 0%

profile of v11, /device:TPU:0, one launch (start us, length us, event | category | flops | bytes accessed | tf_op | source)
XLA Modules:
  0.0 22.2 jit_solution(5143839079872371947)
XLA Ops:
  0.0 1.4 %pack.1 = (bf16[48,384]{1,0:T(8,128)(2,1)S(1)}, bf16[48,384]{1,0:T(8,128)(2,1)S(1)}, bf16[48,384]{1,0:T(8,128)(2,1)S(1)}, bf16[48,384]{1,0:T(8,128)(2,1)S(1)}, b...) custom-call(s32[8,32]{1,0:T(8,128)} %bitcast.5, ...), custom_call_target="tpu_custom_call" | custom-call | tf_op jit(solution)/shard_map/pack/pallas_call | solution.py:161
  1.4 3.1 %collective-permute-start = (bf16[48,384]{1,0:T(8,128)(2,1)S(1)}, bf16[48,384]{1,0:T(8,128)(2,1)S(1)}, u32[]{:S(2)}, u32[]{:S(2)}) collective-permute-start(bf16[48,384]{1,0:T(8,128)(2,1)S(1)} %get-tuple-element.15), channel_id=1, source_target_pairs={{0,8},{1,13},{2,10},{3,15},{4,12},{5,9},{6,14},{7,11},{8,16},{9,21... | collective-permute-start | bytes 110600 | tf_op jit(solution)/shard_map/ppermute | solution.py:391
  4.5 1.7 %collective-permute-start.1 = (bf16[48,384]{1,0:T(8,128)(2,1)S(1)}, bf16[48,384]{1,0:T(8,128)(2,1)S(1)}, u32[]{:S(2)}, u32[]{:S(2)}) collective-permute-start(bf16[48,384]{1,0:T(8,128)(2,1)S(1)} %get-tuple-element.16), channel_id=1, source_target_pairs={{0,9},{1,20},{2,11},{3,22},{4,13},{5,16},{6,15},{7,18},{8,17},{9,2... | collective-permute-start | bytes 110600 | tf_op jit(solution)/shard_map/ppermute | solution.py:391
  6.2 2.1 %collective-permute-start.2 = (bf16[48,384]{1,0:T(8,128)(2,1)S(1)}, bf16[48,384]{1,0:T(8,128)(2,1)S(1)}, u32[]{:S(2)}, u32[]{:S(2)}) collective-permute-start(bf16[48,384]{1,0:T(8,128)(2,1)S(1)} %get-tuple-element.17), channel_id=1, source_target_pairs={{0,5},{1,28},{2,7},{3,30},{4,1},{5,24},{6,3},{7,26},{8,13},{9,4},{... | collective-permute-start | bytes 110600 | tf_op jit(solution)/shard_map/ppermute | solution.py:391
  8.3 0.3 %collective-permute-start.3 = (bf16[48,384]{1,0:T(8,128)(2,1)S(1)}, bf16[48,384]{1,0:T(8,128)(2,1)S(1)}, u32[]{:S(2)}, u32[]{:S(2)}) collective-permute-start(bf16[48,384]{1,0:T(8,128)(2,1)S(1)} %get-tuple-element.18), channel_id=1, source_target_pairs={{0,16},{1,29},{2,18},{3,31},{4,20},{5,25},{6,22},{7,27},{8,24},{9,... | collective-permute-start | bytes 110600 | tf_op jit(solution)/shard_map/ppermute | solution.py:391
  8.6 1.4 %collective-permute-start.4 = (bf16[48,384]{1,0:T(8,128)(2,1)S(1)}, bf16[48,384]{1,0:T(8,128)(2,1)S(1)}, u32[]{:S(2)}, u32[]{:S(2)}) collective-permute-start(bf16[48,384]{1,0:T(8,128)(2,1)S(1)} %get-tuple-element.19), channel_id=1, source_target_pairs={{0,17},{1,12},{2,19},{3,14},{4,21},{5,8},{6,23},{7,10},{8,25},{9,2... | collective-permute-start | bytes 110600 | tf_op jit(solution)/shard_map/ppermute | solution.py:391
  10.0 0.0 collective-permute-done.refs_0_
  10.0 0.6 %collective-permute-start.5 = (bf16[48,384]{1,0:T(8,128)(2,1)S(1)}, bf16[48,384]{1,0:T(8,128)(2,1)S(1)}, u32[]{:S(2)}, u32[]{:S(2)}) collective-permute-start(bf16[48,384]{1,0:T(8,128)(2,1)S(1)} %get-tuple-element.20), channel_id=1, source_target_pairs={{0,4},{1,21},{2,6},{3,23},{4,0},{5,17},{6,2},{7,19},{8,12},{9,29},... | collective-permute-start | bytes 110600 | tf_op jit(solution)/shard_map/ppermute | solution.py:391
  10.6 0.2 collective-permute-done.1.refs_1_
  10.8 2.9 %collective-permute-start.6 = (bf16[48,384]{1,0:T(8,128)(2,1)S(1)}, bf16[48,384]{1,0:T(8,128)(2,1)S(1)}, u32[]{:S(2)}, u32[]{:S(2)}) collective-permute-start(bf16[48,384]{1,0:T(8,128)(2,1)S(1)} %get-tuple-element.21), channel_id=1, source_target_pairs={{0,24},{1,25},{2,26},{3,27},{4,28},{5,29},{6,30},{7,31},{8,0},{9,1... | collective-permute-start | bytes 110600 | tf_op jit(solution)/shard_map/ppermute | solution.py:391
  13.7 0.0 collective-permute-done.2.refs_2_
  13.7 0.0 collective-permute-done.3.refs_3_
  13.7 1.2 %collective-permute-done.4.refs_4_ = bf16[48,384]{1,0:T(8,128)(2,1)S(1)} collective-permute-done((bf16[48,384]{1,0:T(8,128)(2,1)S(1)}, bf16[48,384]{1,0:T(8,128)(2,1)S(1)}, u32[]{:S(2)}, u32[]{:S(2)}) %collective-permute-start.4) | collective-permute-done | bytes 36896 | tf_op jit(solution)/shard_map/ppermute | solution.py:391
  14.9 0.0 collective-permute-done.5.refs_5_
  14.9 0.9 %collective-permute-done.6.refs_6_ = bf16[48,384]{1,0:T(8,128)(2,1)S(1)} collective-permute-done((bf16[48,384]{1,0:T(8,128)(2,1)S(1)}, bf16[48,384]{1,0:T(8,128)(2,1)S(1)}, u32[]{:S(2)}, u32[]{:S(2)}) %collective-permute-start.6) | collective-permute-done | bytes 36896 | tf_op jit(solution)/shard_map/ppermute | solution.py:391
  15.9 6.4 %correlate.1 = bf16[1,8,40,40,256]{4,3,2,1,0:T(8,128)(2,1)} custom-call(f32[1,64]{1,0:T(1,128)S(1)} %get-tuple-element.14.taps_ref, bf16[48,384]{1,0:T(8,128)(2,1)S(1)} %collective-permute-done.refs_0_, bf16[48,384]{1,0:T(8,128)(2,1)S(1)} %collective-permute-done.1.refs_1_, bf16[48,384]{1,0:T(8,128)(2,1)S(1)} %collective-permute-done.2.refs_2_, ...), custom_call_target="tpu_custom_call" | custom-call | tf_op jit(solution)/shard_map/correlate/pallas_call | solution.py:358
Async XLA Ops:
  1.4 8.6 %collective-permute-start = (bf16[48,384]{1,0:T(8,128)(2,1)S(1)}, bf16[48,384]{1,0:T(8,128)(2,1)S(1)}, u32[]{:S(2)}, u32[]{:S(2)}) collective-permute-start(bf16[48,384]{1,0:T(8,128)(2,1)S(1)} %get-tuple-element.15), channel_id=1, source_target_pairs={{0,8},{1,13},{2,10},{3,15},{4,12},{5,9},{6,14},{7,11},{8,16},{9,21... | collective-permute-start | bytes 110600 | tf_op jit(solution)/shard_map/ppermute | solution.py:391
  4.5 6.3 %collective-permute-start.1 = (bf16[48,384]{1,0:T(8,128)(2,1)S(1)}, bf16[48,384]{1,0:T(8,128)(2,1)S(1)}, u32[]{:S(2)}, u32[]{:S(2)}) collective-permute-start(bf16[48,384]{1,0:T(8,128)(2,1)S(1)} %get-tuple-element.16), channel_id=1, source_target_pairs={{0,9},{1,20},{2,11},{3,22},{4,13},{5,16},{6,15},{7,18},{8,17},{9,2... | collective-permute-start | bytes 110600 | tf_op jit(solution)/shard_map/ppermute | solution.py:391
  6.2 7.5 %collective-permute-start.2 = (bf16[48,384]{1,0:T(8,128)(2,1)S(1)}, bf16[48,384]{1,0:T(8,128)(2,1)S(1)}, u32[]{:S(2)}, u32[]{:S(2)}) collective-permute-start(bf16[48,384]{1,0:T(8,128)(2,1)S(1)} %get-tuple-element.17), channel_id=1, source_target_pairs={{0,5},{1,28},{2,7},{3,30},{4,1},{5,24},{6,3},{7,26},{8,13},{9,4},{... | collective-permute-start | bytes 110600 | tf_op jit(solution)/shard_map/ppermute | solution.py:391
  8.3 5.4 %collective-permute-start.3 = (bf16[48,384]{1,0:T(8,128)(2,1)S(1)}, bf16[48,384]{1,0:T(8,128)(2,1)S(1)}, u32[]{:S(2)}, u32[]{:S(2)}) collective-permute-start(bf16[48,384]{1,0:T(8,128)(2,1)S(1)} %get-tuple-element.18), channel_id=1, source_target_pairs={{0,16},{1,29},{2,18},{3,31},{4,20},{5,25},{6,22},{7,27},{8,24},{9,... | collective-permute-start | bytes 110600 | tf_op jit(solution)/shard_map/ppermute | solution.py:391
  8.6 6.3 %collective-permute-start.4 = (bf16[48,384]{1,0:T(8,128)(2,1)S(1)}, bf16[48,384]{1,0:T(8,128)(2,1)S(1)}, u32[]{:S(2)}, u32[]{:S(2)}) collective-permute-start(bf16[48,384]{1,0:T(8,128)(2,1)S(1)} %get-tuple-element.19), channel_id=1, source_target_pairs={{0,17},{1,12},{2,19},{3,14},{4,21},{5,8},{6,23},{7,10},{8,25},{9,2... | collective-permute-start | bytes 110600 | tf_op jit(solution)/shard_map/ppermute | solution.py:391
  10.0 4.9 %collective-permute-start.5 = (bf16[48,384]{1,0:T(8,128)(2,1)S(1)}, bf16[48,384]{1,0:T(8,128)(2,1)S(1)}, u32[]{:S(2)}, u32[]{:S(2)}) collective-permute-start(bf16[48,384]{1,0:T(8,128)(2,1)S(1)} %get-tuple-element.20), channel_id=1, source_target_pairs={{0,4},{1,21},{2,6},{3,23},{4,0},{5,17},{6,2},{7,19},{8,12},{9,29},... | collective-permute-start | bytes 110600 | tf_op jit(solution)/shard_map/ppermute | solution.py:391
  10.8 5.1 %collective-permute-start.6 = (bf16[48,384]{1,0:T(8,128)(2,1)S(1)}, bf16[48,384]{1,0:T(8,128)(2,1)S(1)}, u32[]{:S(2)}, u32[]{:S(2)}) collective-permute-start(bf16[48,384]{1,0:T(8,128)(2,1)S(1)} %get-tuple-element.21), channel_id=1, source_target_pairs={{0,24},{1,25},{2,26},{3,27},{4,28},{5,29},{6,30},{7,31},{8,0},{9,1... | collective-permute-start | bytes 110600 | tf_op jit(solution)/shard_map/ppermute | solution.py:391
